TPU v7x, 32 devices: a whole 2x2x4 slice. The times are simulated.
32 devices in a mesh: bead: 8 (over z, x), space: 4 (over y, core).
Axes of the slice: x: 2, y: 2, z: 4, core: 2. Of those that a mesh axis runs over, the one named last changes fastest.
Arguments:
- positions: float32 [64, 3, 1024], P('bead', None, 'space'), may hold values from -1 to 5
- species: int32 [1024], P('space'), may hold values from 0 to 1
- neighbors: int32 [32, 1024], P(None, 'space'), may hold values from 0 to 383, as said below
- counts: int32 [1024], P('space'), may hold values from 1 to 32, as said below
- send_rows: int32 [512], P('space'), may hold values from 0 to 255, as said below
- embed: float32 [2, 128], replicated, may hold values from -6 to 6
- w_radial: float32 [2, 8, 128], replicated, may hold values from -2 to 2
- w_msg: float32 [2, 128, 128], replicated, may hold values from -0.5 to 0.5
- w_upd: float32 [2, 128, 128], replicated, may hold values from -0.5 to 0.5
- w_out: float32 [128], replicated, may hold values from -0.5 to 0.5
Outputs:
- forces: float32 [64, 3, 1024], P('bead', None, 'space')
Inputs may be any that keep to these rules, and one draw needn't show every extreme that they name: `neighbors`: entry n < 256 is the domain's own row n; 256 + s is the s-th left ghost and 320 + s the s-th right ghost. `counts`: slots of an atom below its count are live, the others padding. `send_rows`: each domain's first 64 entries are a permutation of its rows 0 to 63, the next 64 a permutation of its rows 192 to 255.
All inputs are finite; a program needn't handle non-finite values.
Results may differ from a plain program's by a relative error of at most 0.0003.
Values sent between devices are 32-bit elements; how exact they have to be, the bound alone decides.
No kernel may reach another device: no remote copies, remote signals or barrier semaphores. Data moves between devices by JAX's collectives and lax.ppermute only.
A program may use at most 64 MiB of HBM per device.

v0:
```python
from functools import partial

import jax
import jax.numpy as jnp
from jax import lax
from jax.sharding import PartitionSpec as P

PC = 16


exact_mode = lax.Precision.HIGHEST
spacing_floor = 0.01
radial_width = 0.2
radial_reach = 1.5
block_rows = 128


def with_halo(block, sides, width):
    for axis, dim in sides:
        count = lax.axis_size(axis)
        forward = [(i, i + 1) for i in range(count - 1)]
        forward.append((count - 1, 0))
        backward = [(target, source) for source, target in forward]
        low = lax.ppermute(
            lax.slice_in_dim(block, block.shape[dim] - width, None, axis=dim), axis, forward
        )
        high = lax.ppermute(lax.slice_in_dim(block, 0, width, axis=dim), axis, backward)
        block = jnp.concatenate([low, block, high], axis=dim)
    return block


def contraction(full_beads, reduced_beads):
    rowpos = jnp.arange(reduced_beads, dtype=jnp.float32)[:, None]
    colpos = jnp.arange(full_beads, dtype=jnp.float32)[None, :]
    phase_gap = rowpos / reduced_beads - colpos / full_beads
    running = jnp.ones_like(phase_gap)
    for harmonic in range(1, reduced_beads // 2):
        running = running + 2.0 * jnp.cos(2.0 * jnp.pi * harmonic * phase_gap)
    running = running + jnp.cos(jnp.pi * reduced_beads * phase_gap)
    return running / full_beads


def silu_slope(argument):
    sigmoid_part = jax.nn.sigmoid(argument)
    return sigmoid_part * (1.0 + argument * (1.0 - sigmoid_part))


def blocked(values, which_axis):
    dims_now = values.shape
    blocks = dims_now[which_axis] // block_rows
    reshaped = values.reshape(
        dims_now[:which_axis] + (blocks, block_rows) + dims_now[which_axis + 1 :]
    )
    return jnp.moveaxis(reshaped, which_axis, 0)


def unblocked(values, which_axis):
    moved_axes = jnp.moveaxis(values, 0, which_axis)
    dims_now = moved_axes.shape
    merged = (dims_now[which_axis] * dims_now[which_axis + 1],)
    return moved_axes.reshape(dims_now[:which_axis] + merged + dims_now[which_axis + 2 :])


def chooser_table(rows, extent):
    columns = lax.broadcasted_iota(jnp.int32, rows.shape + (extent,), rows.ndim)
    return (rows[..., None] == columns).astype(jnp.float32)


def block_message(lent_ext, radial_basis, live_slots, neighbor_rows, radial_map, edge_scale):
    radial_w = jnp.einsum("nbkr,nc->bkrc", radial_basis, radial_map, precision=exact_mode)
    chooser = chooser_table(neighbor_rows, lent_ext.shape[1])
    near_rows = jnp.einsum("kre,bec->bkrc", chooser, lent_ext, precision=exact_mode)
    return edge_scale * jnp.einsum(
        "bkrc,kr->brc", radial_w * near_rows, live_slots, precision=exact_mode
    )


def block_backward(state_pair, inputs, lent_ext, radial_map, edge_scale, want_features):
    grad_lent, grad_points = state_pair
    radial_basis, offsets, displace, distance, live_slots, neighbor_rows, grad_message = inputs
    radial_w = jnp.einsum("nbkr,nc->bkrc", radial_basis, radial_map, precision=exact_mode)
    chooser = chooser_table(neighbor_rows, lent_ext.shape[1])
    near_rows = jnp.einsum("kre,bec->bkrc", chooser, lent_ext, precision=exact_mode)
    weighted = edge_scale * live_slots[None, :, :, None] * grad_message[:, None]
    grad_radial = weighted * near_rows
    grad_basis = jnp.einsum("bkrc,nc->nbkr", grad_radial, radial_map, precision=exact_mode)
    grad_distance = jnp.sum(grad_basis * radial_basis * offsets, axis=0) * (-2.0 / radial_width)
    grad_displace = grad_distance[:, None] * displace / distance[:, None]
    grad_points = grad_points + jnp.einsum(
        "kre,bckr->bce", chooser, grad_displace, precision=exact_mode
    )
    if want_features:
        grad_near = weighted * radial_w
        grad_lent = grad_lent + jnp.einsum(
            "kre,bkrc->bec", chooser, grad_near, precision=exact_mode
        )
    return ((grad_lent, grad_points), -jnp.sum(grad_displace, axis=2))


def on_device(
    positions, species, neighbors, counts, send_rows, embed, w_radial, w_msg, w_upd, w_out
):
    full_dev = positions.shape[0]
    atom_count = positions.shape[2]
    beads_all = full_dev * lax.axis_size("bead")
    reduced_dev = PC // lax.axis_size("bead")
    bead_index = lax.axis_index("bead")
    contract_table = contraction(beads_all, PC)
    own_columns = lax.dynamic_slice_in_dim(contract_table, bead_index * full_dev, full_dev, 1)
    own_table = lax.dynamic_slice_in_dim(contract_table, bead_index * reduced_dev, reduced_dev, 0)
    weights = own_table
    reduced = jnp.einsum(
        "kj,jcn->kcn",
        weights,
        lax.all_gather(positions, "bead", axis=0, tiled=True),
        precision=exact_mode,
    )
    ghost_count = send_rows.shape[0] // 2
    domains = lax.axis_size("space")
    domain = lax.axis_index("space")
    selector = chooser_table(send_rows, atom_count)
    lent_points = jnp.einsum("ga,bca->bcg", selector, reduced, precision=exact_mode)
    lent_species = jnp.dot(selector, species.astype(jnp.float32), precision=exact_mode)
    lent_species = jnp.broadcast_to(lent_species[None, None], (reduced_dev, 1, 2 * ghost_count))
    outgoing = jnp.concatenate([lent_points, lent_species], axis=1)
    arrived = with_halo(outgoing, (("space", 2),), ghost_count)
    borrowed = jnp.concatenate(
        [arrived[:, :, :ghost_count], arrived[:, :, 3 * ghost_count :]], axis=2
    )
    left_shift = jnp.where(domain == 0, -float(domains), 0.0)
    right_shift = jnp.where(domain == domains - 1, float(domains), 0.0)
    ghost_slot = jnp.arange(2 * ghost_count, dtype=jnp.int32)
    box_shift = jnp.where(ghost_slot < ghost_count, left_shift, right_shift).astype(jnp.float32)
    ghost_points = borrowed[:, :3].at[:, 0].add(box_shift[None])
    ghost_species = borrowed[0, 3]
    ext_points = jnp.concatenate([reduced, ghost_points], axis=2)
    extent = ext_points.shape[2]
    blocks_rows = blocked(neighbors, 1)

    def pick_points(rows_block):
        chooser = chooser_table(rows_block, extent)
        return jnp.einsum("kre,bce->bckr", chooser, ext_points, precision=exact_mode)

    near_points = unblocked(lax.map(pick_points, blocks_rows), 3)
    displace = near_points - reduced[:, :, None, :]
    distance = jnp.sqrt(jnp.sum(displace * displace, axis=1) + spacing_floor)
    basis_count = w_radial.shape[1]
    centers = radial_reach * jnp.arange(basis_count, dtype=jnp.float32) / (basis_count - 1)
    offsets = (distance[None] - centers[:, None, None, None]) / radial_width
    radial_basis = jnp.exp(-offsets * offsets)
    slot_index = lax.broadcasted_iota(jnp.int32, neighbors.shape, 0)
    live_slots = (slot_index < counts[None, :]).astype(jnp.float32)
    edge_scale = neighbors.shape[0] ** (-0.5)
    kinds = jnp.arange(embed.shape[0], dtype=jnp.int32)
    own_onehot = (species[:, None] == kinds[None, :]).astype(jnp.float32)
    ghost_onehot = (ghost_species[:, None] == kinds.astype(jnp.float32)[None, :]).astype(
        jnp.float32
    )
    ext_onehot = jnp.concatenate([own_onehot, ghost_onehot], axis=0)
    channels = embed.shape[1]
    hidden = jnp.broadcast_to(
        jnp.dot(own_onehot, embed, precision=exact_mode)[None], (reduced_dev, atom_count, channels)
    )
    first_table = jnp.dot(embed, w_msg[0], precision=exact_mode)
    blocks_basis = blocked(radial_basis, 3)
    blocks_offsets = blocked(offsets, 3)
    blocks_displace = blocked(displace, 3)
    blocks_distance = blocked(distance, 2)
    blocks_live = blocked(live_slots, 1)
    layer_total = w_msg.shape[0]
    saved = []
    for layer_index in range(layer_total):
        if layer_index == 0:
            first_rows = jnp.dot(ext_onehot, first_table, precision=exact_mode)
            lent_ext = jnp.broadcast_to(first_rows[None], (reduced_dev,) + first_rows.shape)
        else:
            lent_own = jnp.einsum("bac,cd->bad", hidden, w_msg[layer_index], precision=exact_mode)
            outgoing_rows = jnp.einsum("ga,bac->bgc", selector, lent_own, precision=exact_mode)
            arrived_rows = with_halo(outgoing_rows, (("space", 1),), ghost_count)
            lent_ext = jnp.concatenate(
                [lent_own, arrived_rows[:, :ghost_count], arrived_rows[:, 3 * ghost_count :]],
                axis=1,
            )
        radial_map = w_radial[layer_index]
        per_block = lax.map(
            lambda parts: block_message(
                lent_ext, parts[0], parts[1], parts[2], radial_map, edge_scale
            ),
            (blocks_basis, blocks_live, blocks_rows),
        )
        message = unblocked(per_block, 1)
        update = jnp.einsum("bac,cd->bad", message, w_upd[layer_index], precision=exact_mode)
        saved.append((lent_ext, update))
        hidden = hidden + jax.nn.silu(update)
    grad_hidden = jnp.broadcast_to(w_out[None, None], hidden.shape)
    grad_points = jnp.zeros(ext_points.shape, jnp.float32)
    center_pull = jnp.zeros(reduced.shape, jnp.float32)
    for layer_index in reversed(range(layer_total)):
        lent_ext, update = saved[layer_index]
        grad_update = grad_hidden * silu_slope(update)
        grad_message = jnp.einsum(
            "bac,dc->bad", grad_update, w_upd[layer_index], precision=exact_mode
        )
        want_features = layer_index > 0
        if want_features:
            start_lent = jnp.zeros(lent_ext.shape, jnp.float32)
        else:
            start_lent = jnp.zeros((1,), jnp.float32)
        step_function = partial(
            block_backward,
            lent_ext=lent_ext,
            radial_map=w_radial[layer_index],
            edge_scale=edge_scale,
            want_features=want_features,
        )
        scanned = (
            blocks_basis,
            blocks_offsets,
            blocks_displace,
            blocks_distance,
            blocks_live,
            blocks_rows,
            blocked(grad_message, 1),
        )
        (grad_lent, grad_points), pulls = lax.scan(
            step_function, (start_lent, grad_points), scanned
        )
        center_pull = center_pull + unblocked(pulls, 2)
        if want_features:
            sent_back = with_halo(grad_lent[:, atom_count:], (("space", 1),), ghost_count)
            returned = jnp.concatenate(
                [sent_back[:, :ghost_count], sent_back[:, 3 * ghost_count :]], axis=1
            )
            grad_own = grad_lent[:, :atom_count] + jnp.einsum(
                "ga,bgc->bac", selector, returned, precision=exact_mode
            )
            grad_hidden = grad_hidden + jnp.einsum(
                "bac,dc->bad", grad_own, w_msg[layer_index], precision=exact_mode
            )
    sent_force = with_halo(grad_points[:, :, atom_count:], (("space", 2),), ghost_count)
    returned_force = jnp.concatenate(
        [sent_force[:, :, :ghost_count], sent_force[:, :, 3 * ghost_count :]], axis=2
    )
    energy_grad = (
        grad_points[:, :, :atom_count]
        + center_pull
        + jnp.einsum("ga,bcg->bca", selector, returned_force, precision=exact_mode)
    )
    pull_reduced = -energy_grad
    ratio = float(beads_all) / PC
    weights = own_columns
    return ratio * jnp.einsum(
        "kj,kcn->jcn",
        weights,
        lax.all_gather(pull_reduced, "bead", axis=0, tiled=True),
        precision=exact_mode,
    )


def solution(mesh):
    return jax.shard_map(
        on_device,
        mesh=mesh,
        in_specs=(
            P("bead", None, "space"),
            P("space"),
            P(None, "space"),
            P("space"),
            P("space"),
            P(),
            P(),
            P(),
            P(),
            P(),
        ),
        out_specs=P("bead", None, "space"),
        check_vma=False,
    )
```

profile of v0, /device:TPU:0, one launch (start us, length us, event | category | flops | bytes accessed | tf_op | source)
XLA Modules:
  0.0 246.2 jit_solution(14093666217045796062)
XLA Ops:
  0.0 32.6 %all_gather.6 = f32[64,3,256]{2,0,1:T(8,128)S(1)} all-gather(f32[8,3,256]{2,0,1:T(8,128)} %param.22), channel_id=1, replica_groups=mesh['bead'=8,'space'=4] {'bead'}, dimensions={0}, use_global_device_ids=true | all-gather | bytes 221184 | tf_op jit(solution)/shard_map/all_gather | solution.py:115
  32.7 0.7 convert_element_type.24
  33.9 0.9 fusion.120
  34.7 0.9 convolution_bitcast_fusion.4
  35.8 1.8 collective-permute-start.1
  37.5 0.7 iota_compare_fusion.8
  38.2 1.0 fusion.191
  39.2 1.0 fusion.130
  40.2 0.7 fusion.145
  40.9 0.7 slice_bitcast_fusion
  41.6 0.8 reshape.166
  42.6 7.0 %while.60 = (s32[]{:T(128)}, f32[2,2,3,32,128]{4,2,1,3,0:T(4,128)S(1)}, s32[2,32,128]{2,1,0:T(8,128)S(1)}, f32[2,3,384]{2,1,0:T(4,128)S(1)}, s32[]{:T(128)}) while((s32[]{:T(128)}, f32[2,2,3,32,128]{4,2,1,3,0:T(4,128)S(1)}, s32[2,32,128]{2,1,0:T(8,128)S(1)}, f32[2,3,384]{2,1,0:T(4,128)S(1)}, s32[]{:T(128)}) %tuple.111), condition=%wide.region_1.2_spmd, body=%wide.region_0.1_spmd.sunk | while | flops 114819072 | bytes 192581 | solution.py:144
  42.7 3.5 %fusion.259 = f32[2,2,3,32,128]{4,2,1,3,0:T(4,128)S(1)} fusion(f32[2,2,3,32,128]{4,2,1,3,0:T(4,128)S(1)} %get-tuple-element.847, s32[]{:T(128)} %get-tuple-element.846, s32[32,128]{1,0:T(8,128)S(1)} %dynamic-slice_bitcast_fusion.22, f32[2,3,384]{2,1,0:T(4,128)S(1)} %get-tuple-element.854), kind=kOutput, calls=%fused_computation.7.clone.1 | convolution fusion | flops 114819072 | bytes 159748 | tf_op jit(solution)/shard_map/while/body/eval_jaxpr/kre,bce->bckr/dot_general | solution.py:142
  46.2 3.5 %fusion.259 = f32[2,2,3,32,128]{4,2,1,3,0:T(4,128)S(1)} fusion(f32[2,2,3,32,128]{4,2,1,3,0:T(4,128)S(1)} %get-tuple-element.847, s32[]{:T(128)} %get-tuple-element.846, s32[32,128]{1,0:T(8,128)S(1)} %dynamic-slice_bitcast_fusion.22, f32[2,3,384]{2,1,0:T(4,128)S(1)} %get-tuple-element.854), kind=kOutput, calls=%fused_computation.7.clone.1 | convolution fusion | flops 114819072 | bytes 159748 | tf_op jit(solution)/shard_map/while/body/eval_jaxpr/kre,bce->bckr/dot_general | solution.py:142
  50.3 0.4 fusion.172
  50.7 37.5 %while.62 = (s32[]{:T(128)}, f32[2,2,128,128]{3,2,0,1:T(8,128)S(1)}, f32[2,32,128]{2,1,0:T(8,128)S(1)}, f32[2,8,2,32,128]{4,1,3,2,0:T(8,128)S(1)}, f32[8,128]{1,...) while((s32[]{:T(128)}, f32[2,2,128,128]{3,2,0,1:T(8,128)S(1)}, ...), condition=%wide.region_4.5_spmd.clone, body=%wide.region_3.4_spmd.clone.sunk | while | flops 4947738624 | bytes 17764452 | solution.py:185
  50.9 3.5 %fusion.274 = f32[32,128,2,128]{3,1,0,2:T(8,128)S(1)} fusion(s32[32,128]{1,0:T(8,128)S(1)} %dynamic-slice_bitcast_fusion.26, f32[384,128]{1,0:T(8,128)S(1)} %get-tuple-element.878), kind=kOutput, calls=%fused_computation.28.clone.1 | convolution fusion | flops 4833411072 | bytes 4407296 | tf_op jit(solution)/shard_map/while/body/eval_jaxpr/kre,bec->bkrc/dot_general | solution.py:72
  54.4 8.2 %bitcast_multiply_fusion.20 = f32[2,32,128,128]{3,2,1,0:T(8,128)} fusion(f32[32,128,2,128]{3,1,0,2:T(8,128)S(1)} %fusion.274, f32[2,8,2,32,128]{4,1,3,2,0:T(8,128)S(1)} %get-tuple-element.875, s32[]{:T(128)} %get-tuple-element.864, f32[8,128]{1,0:T(8,128)S(1)} %get-tuple-element.876), kind=kOutput, calls=%fused_computation.29.clone.1 | convolution fusion | flops 101711872 | bytes 8654852 | tf_op jit(solution)/shard_map/while/body/eval_jaxpr/nbkr,nc->bkrc/dot_general | solution.py:70
  62.8 6.5 %fusion.275 = f32[128,1,2,128]{3,1,2,0:T(1,128)S(1)} fusion(f32[32,128,1,1]{0,2,3,1:T(1,128)S(1)} %copy.130, f32[2,32,128,128]{3,2,1,0:T(8,128)} %bitcast_multiply_fusion.20), kind=kOutput, calls=%fused_computation.30.clone.1 | convolution fusion | flops 12582912 | bytes 4341760 | tf_op jit(solution)/shard_map/while/body/eval_jaxpr/bkrc,kr->brc/dot_general | solution.py:73
  69.4 3.5 %fusion.274 = f32[32,128,2,128]{3,1,0,2:T(8,128)S(1)} fusion(s32[32,128]{1,0:T(8,128)S(1)} %dynamic-slice_bitcast_fusion.26, f32[384,128]{1,0:T(8,128)S(1)} %get-tuple-element.878), kind=kOutput, calls=%fused_computation.28.clone.1 | convolution fusion | flops 4833411072 | bytes 4407296 | tf_op jit(solution)/shard_map/while/body/eval_jaxpr/kre,bec->bkrc/dot_general | solution.py:72
  72.9 8.2 %bitcast_multiply_fusion.20 = f32[2,32,128,128]{3,2,1,0:T(8,128)} fusion(f32[32,128,2,128]{3,1,0,2:T(8,128)S(1)} %fusion.274, f32[2,8,2,32,128]{4,1,3,2,0:T(8,128)S(1)} %get-tuple-element.875, s32[]{:T(128)} %get-tuple-element.864, f32[8,128]{1,0:T(8,128)S(1)} %get-tuple-element.876), kind=kOutput, calls=%fused_computation.29.clone.1 | convolution fusion | flops 101711872 | bytes 8654852 | tf_op jit(solution)/shard_map/while/body/eval_jaxpr/nbkr,nc->bkrc/dot_general | solution.py:70
  81.2 6.5 %fusion.275 = f32[128,1,2,128]{3,1,2,0:T(1,128)S(1)} fusion(f32[32,128,1,1]{0,2,3,1:T(1,128)S(1)} %copy.130, f32[2,32,128,128]{3,2,1,0:T(8,128)} %bitcast_multiply_fusion.20), kind=kOutput, calls=%fused_computation.30.clone.1 | convolution fusion | flops 12582912 | bytes 4341760 | tf_op jit(solution)/shard_map/while/body/eval_jaxpr/bkrc,kr->brc/dot_general | solution.py:73
  88.2 0.4 fusion.128
  88.6 0.4 fusion.109
  89.4 1.7 collective-permute-start.3
  91.2 1.9 collective-permute-done.2
  93.1 37.5 %while.61 = (s32[]{:T(128)}, f32[2,2,128,128]{3,2,0,1:T(8,128)S(1)}, f32[2,32,128]{2,1,0:T(8,128)S(1)}, f32[2,8,2,32,128]{4,1,3,2,0:T(8,128)S(1)}, f32[8,128]{1,...) while((s32[]{:T(128)}, f32[2,2,128,128]{3,2,0,1:T(8,128)S(1)}, ...), condition=%wide.region_6.7_spmd, body=%wide.region_5.6_spmd.sunk | while | flops 4947738624 | bytes 17961060 | solution.py:185
  93.2 3.8 %fusion.266 = f32[32,128,2,128]{3,1,0,2:T(8,128)S(1)} fusion(s32[32,128]{1,0:T(8,128)S(1)} %dynamic-slice_bitcast_fusion.24, f32[2,384,128]{2,1,0:T(8,128)S(1)} %get-tuple-element.902), kind=kOutput, calls=%fused_computation.12.clone.1 | convolution fusion | flops 4833411072 | bytes 4603904 | tf_op jit(solution)/shard_map/while/body/eval_jaxpr/kre,bec->bkrc/dot_general | solution.py:72
  96.9 8.2 %bitcast_multiply_fusion.19 = f32[2,32,128,128]{3,2,1,0:T(8,128)} fusion(f32[32,128,2,128]{3,1,0,2:T(8,128)S(1)} %fusion.266, f32[2,8,2,32,128]{4,1,3,2,0:T(8,128)S(1)} %get-tuple-element.899, s32[]{:T(128)} %get-tuple-element.888, f32[8,128]{1,0:T(8,128)S(1)} %get-tuple-element.900), kind=kOutput, calls=%fused_computation.13.clone.1 | convolution fusion | flops 101711872 | bytes 8654852 | tf_op jit(solution)/shard_map/while/body/eval_jaxpr/nbkr,nc->bkrc/dot_general | solution.py:70
  105.3 6.5 %fusion.267 = f32[128,1,2,128]{3,1,2,0:T(1,128)S(1)} fusion(f32[32,128,1,1]{0,2,3,1:T(1,128)S(1)} %copy.127, f32[2,32,128,128]{3,2,1,0:T(8,128)} %bitcast_multiply_fusion.19), kind=kOutput, calls=%fused_computation.14.clone.1 | convolution fusion | flops 12582912 | bytes 4341760 | tf_op jit(solution)/shard_map/while/body/eval_jaxpr/bkrc,kr->brc/dot_general | solution.py:73
  111.9 3.8 %fusion.266 = f32[32,128,2,128]{3,1,0,2:T(8,128)S(1)} fusion(s32[32,128]{1,0:T(8,128)S(1)} %dynamic-slice_bitcast_fusion.24, f32[2,384,128]{2,1,0:T(8,128)S(1)} %get-tuple-element.902), kind=kOutput, calls=%fused_computation.12.clone.1 | convolution fusion | flops 4833411072 | bytes 4603904 | tf_op jit(solution)/shard_map/while/body/eval_jaxpr/kre,bec->bkrc/dot_general | solution.py:72
  115.7 8.2 %bitcast_multiply_fusion.19 = f32[2,32,128,128]{3,2,1,0:T(8,128)} fusion(f32[32,128,2,128]{3,1,0,2:T(8,128)S(1)} %fusion.266, f32[2,8,2,32,128]{4,1,3,2,0:T(8,128)S(1)} %get-tuple-element.899, s32[]{:T(128)} %get-tuple-element.888, f32[8,128]{1,0:T(8,128)S(1)} %get-tuple-element.900), kind=kOutput, calls=%fused_computation.13.clone.1 | convolution fusion | flops 101711872 | bytes 8654852 | tf_op jit(solution)/shard_map/while/body/eval_jaxpr/nbkr,nc->bkrc/dot_general | solution.py:70
  124.0 6.5 %fusion.267 = f32[128,1,2,128]{3,1,2,0:T(1,128)S(1)} fusion(f32[32,128,1,1]{0,2,3,1:T(1,128)S(1)} %copy.127, f32[2,32,128,128]{3,2,1,0:T(8,128)} %bitcast_multiply_fusion.19), kind=kOutput, calls=%fused_computation.14.clone.1 | convolution fusion | flops 12582912 | bytes 4341760 | tf_op jit(solution)/shard_map/while/body/eval_jaxpr/bkrc,kr->brc/dot_general | solution.py:73
  130.6 0.4 multiply_multiply_fusion.16
  131.0 0.4 convolution_bitcast_fusion.2
  131.4 52.9 %while.64 = (s32[]{:T(128)}, f32[2,384,128]{1,2,0:T(8,128)S(1)}, f32[2,3,384]{2,1,0:T(4,128)S(1)}, f32[2,2,3,128]{3,2,1,0:T(4,128)S(1)}, f32[2,32,128]{2,1,0:T(8...) while((s32[]{:T(128)}, f32[2,384,128]{1,2,0:T(8,128)S(1)}, ...), condition=%wide.region_10.11_spmd.clone, body=%wide.region_7.10_spmd.clone.sunk | while | flops 9987638272 | bytes 19977400 | solution.py:225
  131.6 8.2 %fusion.293 = f32[2,32,128,128]{3,2,1,0:T(8,128)} fusion(f32[2,8,2,32,128]{4,1,3,2,0:T(8,128)S(1)} %get-tuple-element.940, s32[]{:T(128)} %get-tuple-element.919, f32[8,128]{1,0:T(8,128)S(1)} %get-tuple-element.941), kind=kOutput, calls=%fused_computation.96.clone.1 | convolution fusion | flops 100663296 | bytes 4460548 | tf_op jit(solution)/shard_map/while/body/eval_jaxpr/nbkr,nc->bkrc/dot_general | solution.py:81
  139.9 7.7 %fusion.294 = f32[2,384,128]{1,2,0:T(8,128)S(1)} fusion(s32[32,128]{1,0:T(8,128)S(1)} %dynamic-slice_bitcast_fusion.30, f32[2,32,128,128]{3,2,1,0:T(8,128)} %fusion.293, f32[2,128,128]{2,1,0:T(8,128)S(1)} %dynamic-slice_bitcast_fusion.31, f32[32,128]{1,0:T(8,128)S(1)} %multiply_bitcast_fusion.5, f32[2,384,128]{1,2,0:T(8,128)S(1)} %get-tuple-element.920, ...), kind=kOutput, calls=%fused_computation.88.clone.1 | convolution fusion | flops 4835704832 | bytes 5144577 | tf_op jit(solution)/shard_map/while/body/eval_jaxpr/kre,bkrc->bec/dot_general | solution.py:94
  147.6 3.9 %fusion.295 = f32[32,128,2,128]{3,1,0,2:T(8,128)S(1)} fusion(s32[32,128]{1,0:T(8,128)S(1)} %dynamic-slice_bitcast_fusion.30, f32[2,384,128]{2,1,0:T(8,128)S(1)} %get-tuple-element.943), kind=kOutput, calls=%fused_computation.74.clone.1 | convolution fusion | flops 4833411072 | bytes 4603904 | tf_op jit(solution)/shard_map/while/body/eval_jaxpr/kre,bec->bkrc/dot_general | solution.py:83
  151.5 4.1 %fusion.296 = f32[2,32,128]{2,1,0:T(8,128)S(1)} fusion(f32[32,128,2,128]{3,1,0,2:T(8,128)S(1)} %fusion.295, f32[2,128,128]{2,1,0:T(8,128)S(1)} %dynamic-slice_bitcast_fusion.31, f32[32,128]{1,0:T(8,128)S(1)} %multiply_bitcast_fusion.5, f32[2,8,2,32,128]{4,1,3,2,0:T(8,128)S(1)} %get-tuple-element.944, s32[]{:T(128)} %get-tuple-element.919, ...), kind=kOutput, calls=%fused_computation.92.clone.1 | convolution fusion | flops 102948864 | bytes 4902916 | tf_op jit(solution)/shard_map/while/body/eval_jaxpr/bkrc,nc->nbkr/dot_general | solution.py:86
  155.7 2.2 fusion.298
  157.9 8.2 %fusion.293 = f32[2,32,128,128]{3,2,1,0:T(8,128)} fusion(f32[2,8,2,32,128]{4,1,3,2,0:T(8,128)S(1)} %get-tuple-element.940, s32[]{:T(128)} %get-tuple-element.919, f32[8,128]{1,0:T(8,128)S(1)} %get-tuple-element.941), kind=kOutput, calls=%fused_computation.96.clone.1 | convolution fusion | flops 100663296 | bytes 4460548 | tf_op jit(solution)/shard_map/while/body/eval_jaxpr/nbkr,nc->bkrc/dot_general | solution.py:81
  166.2 7.7 %fusion.294 = f32[2,384,128]{1,2,0:T(8,128)S(1)} fusion(s32[32,128]{1,0:T(8,128)S(1)} %dynamic-slice_bitcast_fusion.30, f32[2,32,128,128]{3,2,1,0:T(8,128)} %fusion.293, f32[2,128,128]{2,1,0:T(8,128)S(1)} %dynamic-slice_bitcast_fusion.31, f32[32,128]{1,0:T(8,128)S(1)} %multiply_bitcast_fusion.5, f32[2,384,128]{1,2,0:T(8,128)S(1)} %get-tuple-element.920, ...), kind=kOutput, calls=%fused_computation.88.clone.1 | convolution fusion | flops 4835704832 | bytes 5144577 | tf_op jit(solution)/shard_map/while/body/eval_jaxpr/kre,bkrc->bec/dot_general | solution.py:94
  173.9 3.9 %fusion.295 = f32[32,128,2,128]{3,1,0,2:T(8,128)S(1)} fusion(s32[32,128]{1,0:T(8,128)S(1)} %dynamic-slice_bitcast_fusion.30, f32[2,384,128]{2,1,0:T(8,128)S(1)} %get-tuple-element.943), kind=kOutput, calls=%fused_computation.74.clone.1 | convolution fusion | flops 4833411072 | bytes 4603904 | tf_op jit(solution)/shard_map/while/body/eval_jaxpr/kre,bec->bkrc/dot_general | solution.py:83
  177.8 4.1 %fusion.296 = f32[2,32,128]{2,1,0:T(8,128)S(1)} fusion(f32[32,128,2,128]{3,1,0,2:T(8,128)S(1)} %fusion.295, f32[2,128,128]{2,1,0:T(8,128)S(1)} %dynamic-slice_bitcast_fusion.31, f32[32,128]{1,0:T(8,128)S(1)} %multiply_bitcast_fusion.5, f32[2,8,2,32,128]{4,1,3,2,0:T(8,128)S(1)} %get-tuple-element.944, s32[]{:T(128)} %get-tuple-element.919, ...), kind=kOutput, calls=%fused_computation.92.clone.1 | convolution fusion | flops 102948864 | bytes 4902916 | tf_op jit(solution)/shard_map/while/body/eval_jaxpr/bkrc,nc->nbkr/dot_general | solution.py:86
  181.9 2.2 fusion.298
  184.5 1.7 collective-permute-start.4
  186.3 2.6 %collective-permute-done.4 = f32[2,64,128]{1,2,0:T(8,128)S(1)} collective-permute-done((f32[2,64,128]{1,2,0:T(8,128)S(1)}, f32[2,64,128]{1,2,0:T(8,128)S(1)}, u32[]{:S(2)}, u32[]{:S(2)}) %collective-permute-start.4) | collective-permute-done | bytes 65568 | tf_op jit(solution)/shard_map/ppermute | solution.py:24
  188.9 0.4 collective-permute-done.5
  189.3 0.3 fusion.104
  189.7 0.6 fusion.103
  190.3 0.4 convolution_bitcast_fusion
  190.7 20.3 %while.63 = (s32[]{:T(128)}, f32[2,3,384]{2,1,0:T(4,128)S(1)}, f32[2,2,3,128]{3,2,1,0:T(4,128)S(1)}, f32[2,32,128]{2,1,0:T(8,128)S(1)}, f32[2,2,128,128]{3,2,0,1...) while((s32[]{:T(128)}, f32[2,3,384]{2,1,0:T(4,128)S(1)}, ...), condition=%wide.region_14.15_spmd.clone, body=%wide.region_11.14_spmd.clone.sunk | while | flops 5051267072 | bytes 10175641 | solution.py:225
  190.7 3.7 %fusion.281 = f32[32,128,2,128]{3,1,0,2:T(8,128)S(1)} fusion(s32[32,128]{1,0:T(8,128)S(1)} %dynamic-slice_bitcast_fusion.28, f32[384,128]{1,0:T(8,128)S(1)} %get-tuple-element.986), kind=kOutput, calls=%fused_computation.46.clone.1 | convolution fusion | flops 4833411072 | bytes 4407296 | tf_op jit(solution)/shard_map/while/body/eval_jaxpr/kre,bec->bkrc/dot_general | solution.py:83
  194.4 4.1 %fusion.282 = f32[2,32,128]{2,1,0:T(8,128)S(1)} fusion(f32[32,128,2,128]{3,1,0,2:T(8,128)S(1)} %fusion.281, f32[2,128,128]{2,1,0:T(8,128)S(1)} %dynamic-slice_bitcast_fusion.29, f32[32,128]{1,0:T(8,128)S(1)} %multiply_bitcast_fusion.4, f32[2,8,2,32,128]{4,1,3,2,0:T(8,128)S(1)} %get-tuple-element.983, s32[]{:T(128)} %get-tuple-element.962, ...), kind=kOutput, calls=%fused_computation.57.clone.1 | convolution fusion | flops 102948864 | bytes 4902916 | tf_op jit(solution)/shard_map/while/body/eval_jaxpr/bkrc,nc->nbkr/dot_general | solution.py:86
  198.6 2.2 fusion.284
  200.8 3.7 %fusion.281 = f32[32,128,2,128]{3,1,0,2:T(8,128)S(1)} fusion(s32[32,128]{1,0:T(8,128)S(1)} %dynamic-slice_bitcast_fusion.28, f32[384,128]{1,0:T(8,128)S(1)} %get-tuple-element.986), kind=kOutput, calls=%fused_computation.46.clone.1 | convolution fusion | flops 4833411072 | bytes 4407296 | tf_op jit(solution)/shard_map/while/body/eval_jaxpr/kre,bec->bkrc/dot_general | solution.py:83
  204.6 4.1 %fusion.282 = f32[2,32,128]{2,1,0:T(8,128)S(1)} fusion(f32[32,128,2,128]{3,1,0,2:T(8,128)S(1)} %fusion.281, f32[2,128,128]{2,1,0:T(8,128)S(1)} %dynamic-slice_bitcast_fusion.29, f32[32,128]{1,0:T(8,128)S(1)} %multiply_bitcast_fusion.4, f32[2,8,2,32,128]{4,1,3,2,0:T(8,128)S(1)} %get-tuple-element.983, s32[]{:T(128)} %get-tuple-element.962, ...), kind=kOutput, calls=%fused_computation.57.clone.1 | convolution fusion | flops 102948864 | bytes 4902916 | tf_op jit(solution)/shard_map/while/body/eval_jaxpr/bkrc,nc->nbkr/dot_general | solution.py:86
  208.7 2.2 fusion.284
  211.0 1.3 collective-permute-start.6
  212.3 0.7 collective-permute-start.7
  213.0 1.2 collective-permute-done.6
  214.6 30.5 %all_gather.7 = f32[16,3,256]{2,1,0:T(4,128)S(1)} all-gather(f32[2,3,256]{2,1,0:T(4,128)S(1)} %copy.72), channel_id=1, replica_groups=mesh['bead'=8,'space'=4] {'bead'}, dimensions={0}, use_global_device_ids=true | all-gather | bytes 55296 | tf_op jit(solution)/shard_map/all_gather | solution.py:255
  245.1 0.9 convolution_multiply_fusion
  (105 shorter events, 3.7 us)
Async XLA Ops:
  0.0 38.2 %copy-start = (f32[2,128]{1,0:T(2,128)S(1)}, f32[2,128]{1,0:T(2,128)}, u32[]{:S(2)}) copy-start(f32[2,128]{1,0:T(2,128)} %param.27) | copy-start | bytes 3076
  35.7 6.7 %collective-permute-start = (f32[2,4,64]{2,0,1:T(2,128)S(1)}, f32[2,4,64]{2,0,1:T(2,128)S(1)}, u32[]{:S(2)}, u32[]{:S(2)}) collective-permute-start(f32[2,4,64]{2,0,1:T(2,128)S(1)} %get-tuple-element.569), channel_id=1, source_target_pairs={{0,1},{1,2},{2,3},{3,0},{4,5},{5,6},{6,7},{7,4},{8,9},{9,10},{10,1... | collective-permute-start | bytes 6152 | tf_op jit(solution)/shard_map/ppermute | solution.py:24
  35.8 6.7 %collective-permute-start.1 = (f32[2,4,64]{2,0,1:T(2,128)S(1)}, f32[2,4,64]{2,0,1:T(2,128)S(1)}, u32[]{:S(2)}, u32[]{:S(2)}) collective-permute-start(f32[2,4,64]{2,0,1:T(2,128)S(1)} %get-tuple-element.568), channel_id=1, source_target_pairs={{1,0},{2,1},{3,2},{0,3},{5,4},{6,5},{7,6},{4,7},{9,8},{10,9},{11,1... | collective-permute-start | bytes 6152 | tf_op jit(solution)/shard_map/ppermute | solution.py:27
  50.7 37.5 %copy-start.1 = (f32[2,128,128]{2,1,0:T(8,128)S(1)}, f32[2,128,128]{2,1,0:T(8,128)}, u32[]{:S(2)}) copy-start(f32[2,128,128]{2,1,0:T(8,128)} %param.30) | copy-start | bytes 393220
  50.7 37.9 %copy-start.2 = (f32[2,128,128]{2,1,0:T(8,128)S(1)}, f32[2,128,128]{2,1,0:T(8,128)}, u32[]{:S(2)}) copy-start(f32[2,128,128]{2,1,0:T(8,128)} %param.29) | copy-start | bytes 393220
  50.7 38.3 %copy-start.3 = (s32[128]{0:T(128)S(1)}, s32[128]{0:T(128)}, u32[]{:S(2)}) copy-start(s32[128]{0:T(128)} %param.26) | copy-start | bytes 1540
  89.3 3.7 %collective-permute-start.2 = (f32[2,64,128]{2,1,0:T(8,128)S(1)}, f32[2,64,128]{2,1,0:T(8,128)S(1)}, u32[]{:S(2)}, u32[]{:S(2)}) collective-permute-start(f32[2,64,128]{2,1,0:T(8,128)S(1)} %get-tuple-element.560), channel_id=1, source_target_pairs={{0,1},{1,2},{2,3},{3,0},{4,5},{5,6},{6,7},{7,4},{8,9},{9,10},{10,1... | collective-permute-start | bytes 196616 | tf_op jit(solution)/shard_map/ppermute | solution.py:24
  89.4 3.7 %collective-permute-start.3 = (f32[2,64,128]{2,1,0:T(8,128)S(1)}, f32[2,64,128]{2,1,0:T(8,128)S(1)}, u32[]{:S(2)}, u32[]{:S(2)}) collective-permute-start(f32[2,64,128]{2,1,0:T(8,128)S(1)} %get-tuple-element.561), channel_id=1, source_target_pairs={{1,0},{2,1},{3,2},{0,3},{5,4},{6,5},{7,6},{4,7},{9,8},{10,9},{11,1... | collective-permute-start | bytes 196616 | tf_op jit(solution)/shard_map/ppermute | solution.py:27
  93.1 37.5 %copy-start.4 = (f32[128]{0:T(128)S(1)}, f32[128]{0:T(128)}, u32[]{:S(2)}) copy-start(f32[128]{0:T(128)} %param.31) | copy-start | bytes 1540
  184.5 4.4 %collective-permute-start.4 = (f32[2,64,128]{1,2,0:T(8,128)S(1)}, f32[2,64,128]{1,2,0:T(8,128)S(1)}, u32[]{:S(2)}, u32[]{:S(2)}) collective-permute-start(f32[2,64,128]{1,2,0:T(8,128)S(1)} %get-tuple-element.558), channel_id=1, source_target_pairs={{0,1},{1,2},{2,3},{3,0},{4,5},{5,6},{6,7},{7,4},{8,9},{9,10},{10,1... | collective-permute-start | bytes 196616 | tf_op jit(solution)/shard_map/ppermute | solution.py:24
  186.1 3.2 %collective-permute-start.5 = (f32[2,64,128]{1,2,0:T(8,128)S(1)}, f32[2,64,128]{1,2,0:T(8,128)S(1)}, u32[]{:S(2)}, u32[]{:S(2)}) collective-permute-start(f32[2,64,128]{1,2,0:T(8,128)S(1)} %get-tuple-element.559), channel_id=1, source_target_pairs={{1,0},{2,1},{3,2},{0,3},{5,4},{6,5},{7,6},{4,7},{9,8},{10,9},{11,1... | collective-permute-start | bytes 196616 | tf_op jit(solution)/shard_map/ppermute | solution.py:27
  211.0 3.2 %collective-permute-start.6 = (f32[2,3,64]{2,0,1:T(2,128)S(1)}, f32[2,3,64]{2,0,1:T(2,128)S(1)}, u32[]{:S(2)}, u32[]{:S(2)}) collective-permute-start(f32[2,3,64]{2,0,1:T(2,128)S(1)} %get-tuple-element.564), channel_id=1, source_target_pairs={{0,1},{1,2},{2,3},{3,0},{4,5},{5,6},{6,7},{7,4},{8,9},{9,10},{10,1... | collective-permute-start | bytes 4616 | tf_op jit(solution)/shard_map/ppermute | solution.py:24
  212.3 2.0 collective-permute-start.7
where the time goes:
time: 249 us; the launch traced here: 246 us
  matrix products  161 us (65%)
  blocking collectives  63.1 us (25%)
  starting transfers between devices  7.36 us (3%)
  waiting for transfers between devices  6.22 us (2%)
  other arithmetic  3.87 us (2%)
    dot_general x4, matrix products, block_message(): jnp.einsum('nbkr,nc->bkrc', radial_basis, radial_map, precision=exact_mode)  33 us
    all_gather x1, blocking collectives, on_device(): lax.all_gather(positions, 'bead', axis=0, tiled=True)  32.6 us
    all_gather x1, blocking collectives, on_device(): lax.all_gather(pull_reduced, 'bead', axis=0, tiled=True)  30.5 us
    dot_general x4, matrix products, block_message(): jnp.einsum('bkrc,kr->brc', radial_w * near_rows, live_slots, precision=ex...  26.1 us
    dot_general x2, matrix products, block_backward(): jnp.einsum('nbkr,nc->bkrc', radial_basis, radial_map, precision=exact_mode)  16.5 us
    dot_general x4, matrix products, block_backward(): jnp.einsum('bkrc,nc->nbkr', grad_radial, radial_map, precision=exact_mode)  16.2 us
    dot_general x2, matrix products, block_backward(): jnp.einsum('kre,bkrc->bec', chooser, grad_near, precision=exact_mode)  15.4 us
    dot_general x4, matrix products, block_backward(): jnp.einsum('kre,bec->bkrc', chooser, lent_ext, precision=exact_mode)  15 us
  transfers between devices with their start and end apart: 8, of which 5 were waited for; matrix products, arithmetic and copies ran while one was open for 2% of the time, Pallas kernels for 0%

commit v1 on v0

v1 whole, which is shorter than its diff:
```python
import functools
import math

import jax
import jax.numpy as jnp
import numpy as np
from jax import lax
from jax.experimental import pallas as pl
from jax.experimental.pallas import tpu as pltpu
from jax.sharding import PartitionSpec as P

PC = 16

exact_mode = lax.Precision.HIGHEST
spacing_floor = 0.01
radial_width = 0.2
radial_reach = 1.5
LANES = 128
PLANES = 4
ROWS = 16
BLOCK = 64
F32 = jnp.float32
BF16 = jnp.bfloat16
VMEM_BYTES = 48 * 1024 * 1024
kappa = math.sqrt(math.log2(math.e)) / radial_width


def contraction(full_beads, reduced_beads):
    gap = np.arange(reduced_beads)[:, None] / reduced_beads - np.arange(full_beads)[None, :] / full_beads
    total = np.ones_like(gap)
    for harmonic in range(1, reduced_beads // 2):
        total = total + 2.0 * np.cos(2.0 * np.pi * harmonic * gap)
    total = total + np.cos(np.pi * reduced_beads * gap)
    return (total / full_beads).astype(np.float32)


def exact_dot(left, right):
    return lax.dot(left, right, precision=exact_mode, preferred_element_type=F32)


def fast_dot(left, right):
    return lax.dot(left, right, preferred_element_type=F32)


def halves(values):
    high = values.astype(BF16)
    low = (values - high.astype(F32)).astype(BF16)
    return high, low


def spread_kernel(table_ref, pos_ref, out_ref):
    full_dev = pos_ref.shape[0]
    groups, domains, rows, _ = out_ref.shape
    first = lax.axis_index("bead") * full_dev
    beads = [pos_ref[j] for j in range(full_dev)]
    for group in range(groups):
        for local in range(rows // 3):
            k = group * (rows // 3) + local
            total = table_ref[k, first] * beads[0]
            for j in range(1, full_dev):
                total = total + table_ref[k, first + j] * beads[j]
            for domain in range(domains):
                out_ref[group, domain, local * 3 : local * 3 + 3, :] = total


def collect_kernel(ratio, table_ref, in_ref, out_ref):
    full_dev = out_ref.shape[0]
    groups, domains, rows, _ = in_ref.shape
    first = lax.axis_index("bead") * full_dev
    totals = [None] * full_dev
    for group in range(groups):
        arrived = in_ref[group, 0]
        for domain in range(1, domains):
            arrived = arrived + in_ref[group, domain]
        for local in range(rows // 3):
            k = group * (rows // 3) + local
            part = arrived[local * 3 : local * 3 + 3, :] * -ratio
            for j in range(full_dev):
                term = table_ref[k, first + j] * part
                totals[j] = term if totals[j] is None else totals[j] + term
    for j in range(full_dev):
        out_ref[j] = totals[j]


def prepare_kernel(
    own_ref, left_ref, right_ref, far_left_ref, far_right_ref, embed_ref, radial_ref, msg_ref, upd_ref,
    count_ref, hidden_ref, first_ref, first_t_ref, msg_t_ref, upd_t_ref,
    *, slots, ghosts,
):
    atoms = own_ref.shape[1]
    extent = atoms + 2 * ghosts
    species_count, channels = embed_ref.shape
    basis_count = radial_ref.shape[1]
    tail = atoms - ghosts
    count_row, species_row, send_row = slots, slots + 1, slots + 2

    def edge_pack(row, rows=1):
        return jnp.concatenate(
            [own_ref[row : row + rows], left_ref[row : row + rows, tail:], right_ref[row : row + rows, :ghosts]],
            axis=1,
        )

    neighbors = edge_pack(0, slots)
    counts = edge_pack(count_row)
    own_send = own_ref[send_row : send_row + 1]
    left_send = left_ref[send_row : send_row + 1]
    right_send = right_ref[send_row : send_row + 1]
    far_left_send = far_left_ref[1:2]
    far_right_send = far_right_ref[1:2]

    def ghost_map(from_left, from_right):
        return jnp.concatenate(
            [from_left[:, ghosts : 2 * ghosts] - tail, from_right[:, :ghosts] + ghosts], axis=1
        )

    maps = [
        ghost_map(left_send, right_send),
        ghost_map(far_left_send, own_send),
        ghost_map(own_send, far_right_send),
    ]
    maps = [jnp.broadcast_to(m, (slots, 2 * ghosts)) for m in maps]
    lane = lax.broadcasted_iota(jnp.int32, (slots, LANES), 1)
    slot = lax.broadcasted_iota(jnp.int32, (slots, LANES), 0)

    species_rows = []
    for near, lower, upper in (
        (own_ref[species_row : species_row + 1], left_ref[species_row : species_row + 1], right_ref[species_row : species_row + 1]),
        (left_ref[species_row : species_row + 1], far_left_ref[0:1], own_ref[species_row : species_row + 1]),
        (right_ref[species_row : species_row + 1], own_ref[species_row : species_row + 1], far_right_ref[0:1]),
    ):
        species_rows.append(jnp.concatenate([near, lower[:, tail:], upper[:, :ghosts]], axis=1))
    species_f = jnp.concatenate(species_rows + [species_rows[0]] * 5, axis=0).astype(F32)
    species_cols = species_f.T

    plane_rows = extent // PLANES
    chunks = extent // LANES
    plane_iota = lax.broadcasted_iota(jnp.int32, (plane_rows, LANES), 0)
    lane_block = lax.broadcasted_iota(jnp.int32, (plane_rows, LANES), 1)
    for chunk in range(chunks):
        lanes = slice(chunk * LANES, (chunk + 1) * LANES)
        rows_now = neighbors[:, lanes]
        index = jnp.clip(rows_now - atoms, 0, 2 * ghosts - 1)
        if (chunk + 1) * LANES <= atoms:
            mapped = jnp.take_along_axis(maps[0], index, axis=1, mode="promise_in_bounds")
        else:
            mapped = jnp.where(
                lane < ghosts,
                jnp.take_along_axis(maps[1], index, axis=1, mode="promise_in_bounds"),
                jnp.take_along_axis(maps[2], index, axis=1, mode="promise_in_bounds"),
            )
        rows_now = jnp.where(rows_now >= atoms, atoms + mapped, rows_now)
        plane = jnp.zeros_like(rows_now)
        for step in range(1, PLANES):
            plane = plane + (rows_now >= step * plane_rows).astype(jnp.int32)
        within = rows_now - plane * plane_rows
        within = jnp.where(slot < counts[:, lanes], within, -1)
        value = jnp.left_shift(jnp.ones_like(plane), 8 * plane)
        words = jnp.zeros((plane_rows, LANES), jnp.int32)
        for k in range(slots):
            words = words + jnp.where(within[k : k + 1] == plane_iota, value[k : k + 1], 0)
        for step in range(PLANES):
            rows = slice(step * plane_rows, (step + 1) * plane_rows)
            tally = (jnp.right_shift(words, 8 * step) & 255).astype(F32)
            if (chunk + 1) * LANES <= atoms:
                kind = jnp.broadcast_to(species_cols[rows, 0:1], (plane_rows, LANES))
            else:
                kind = jnp.where(lane_block < ghosts, species_cols[rows, 1:2], species_cols[rows, 2:3])
            for s in range(species_count):
                count_ref[s, rows, lanes] = jnp.where(kind == float(s), tally, 0.0)

    embed = embed_ref[...]
    embed_pad = jnp.concatenate([embed, jnp.zeros((8 - species_count, channels), F32)], axis=0)
    embed_cols = embed_pad.T
    hidden = jnp.zeros((channels, extent), F32)
    for s in range(species_count):
        hidden = hidden + embed_cols[:, s : s + 1] * (species_f[0:1] == float(s)).astype(F32)
    hidden_ref[...] = hidden

    scale = slots ** (-0.5)
    lent = exact_dot(embed_pad, msg_ref[0])
    stacked = []
    for b in range(basis_count):
        for s in range(species_count):
            row = radial_ref[0, b : b + 1] * lent[s : s + 1] * scale
            stacked.append(jnp.broadcast_to(row, (8, channels)))
    first = exact_dot(jnp.concatenate(stacked, axis=0), upd_ref[0])
    first_ref[...] = first
    first_t_ref[...] = first.T
    msg_t_ref[...] = msg_ref[1].T
    upd_t_ref[...] = upd_ref[1].T


def force_kernel(
    recv_ref, count_ref, hidden_ref, first_ref, first_t_ref, msg_t_ref, upd_t_ref, radial_ref, msg_ref, upd_ref, out_w_ref,
    out_ref,
    near_ref, reach_ref, inverse_ref, high_ref, low_ref, sums_ref, edge_ref, grads_ref, left_ref, slope_ref, row_h_ref,
    *, domains, slots, ghosts,
):
    groups = recv_ref.shape[0] // domains
    rows, atoms = recv_ref.shape[1:]
    reduced_dev = rows // 3
    extent = atoms + 2 * ghosts
    tail = atoms - ghosts
    species_count = count_ref.shape[0]
    basis_count, channels = radial_ref.shape[1:]
    own_chunks = atoms // LANES
    chunks = extent // LANES
    domain = lax.axis_index("space")
    scale = slots ** (-0.5)
    centers = [kappa * radial_reach * b / (basis_count - 1) for b in range(basis_count)]

    row_iota = lax.broadcasted_iota(jnp.int32, (8, atoms), 0)
    is_first = lax.rem(row_iota, 3) == 0
    segment = {}
    for step in range(-2, 3):
        shifted = domain + step + 2 * domains
        place = lax.rem(shifted, domains)
        wraps = (lax.div(shifted, domains) - 2).astype(F32) * float(domains)
        total = recv_ref[place]
        for group in range(1, groups):
            total = total + recv_ref[group * domains + place]
        if rows < 8:
            total = jnp.concatenate([total, jnp.zeros((8 - rows, atoms), F32)], axis=0)
        segment[step] = total + jnp.where(is_first, wraps, 0.0)

    def extended(step):
        return jnp.concatenate(
            [segment[step], segment[step - 1][:, tail:], segment[step + 1][:, :ghosts]], axis=1
        )

    ext_own, ext_left, ext_right = extended(0), extended(-1), extended(1)
    cols_own, cols_left, cols_right = ext_own.T, ext_left.T, ext_right.T
    lane_ext = lax.broadcasted_iota(jnp.int32, (extent, LANES), 1)
    for q in range(rows):
        near_ref[0, q] = jnp.broadcast_to(cols_own[:, q : q + 1], (extent, LANES))
        near_ref[1, q] = jnp.where(lane_ext < ghosts, cols_left[:, q : q + 1], cols_right[:, q : q + 1])

    edge_ref[...] = jnp.zeros_like(edge_ref)
    pulls = []
    for bead in range(reduced_dev):
        for chunk in range(chunks):
            lanes = slice(chunk * LANES, (chunk + 1) * LANES)
            own = chunk < own_chunks
            here = [
                jnp.broadcast_to(ext_own[bead * 3 + x : bead * 3 + x + 1, lanes], (ROWS, LANES)) for x in range(3)
            ]

            def gather_basis(step, sums, lanes=lanes, own=own, here=here):
                at = pl.ds(pl.multiple_of(step * ROWS, ROWS), ROWS)
                square = spacing_floor
                for x in range(3):
                    delta = near_ref[0 if own else 1, bead * 3 + x, at, :] - here[x]
                    square = square + delta * delta
                inverse = lax.rsqrt(square)
                reach = square * inverse * kappa
                inverse_ref[at, lanes] = inverse
                reach_ref[at, lanes] = reach
                tallies = [count_ref[s, at, lanes] for s in range(species_count)]
                if own:
                    tally = functools.reduce(jnp.add, tallies)
                sums = list(sums)
                for b in range(basis_count):
                    offset = reach - centers[b]
                    value = jnp.exp2(-(offset * offset))
                    for s in range(species_count):
                        term = tallies[s] * value
                        sums[b * species_count + s] = sums[b * species_count + s] + (term[:8] + term[8:])
                    if own:
                        high, low = halves(tally * value)
                        high_ref[b, at, lanes] = high
                        low_ref[b, at, lanes] = low
                return tuple(sums)

            zero = jnp.zeros((8, LANES), F32)
            sums = lax.fori_loop(0, extent // ROWS, gather_basis, (zero,) * (basis_count * species_count))
            for n, total in enumerate(sums):
                sums_ref[n * 8 : n * 8 + 8, lanes] = total

        update = exact_dot(first_t_ref[...], sums_ref[...])
        sigmoid = jax.nn.sigmoid(update)
        slope_ref[...] = sigmoid * (1.0 + update * (1.0 - sigmoid))
        hidden = hidden_ref[...] + update * sigmoid
        lent_t = exact_dot(msg_t_ref[...], hidden)
        lent = lent_t.T
        radial_cols = radial_ref[1].T * scale
        message = jnp.zeros((channels, atoms), F32)
        for b in range(basis_count):
            high, low = halves(lent_t * radial_cols[:, b : b + 1])
            both = fast_dot(jnp.concatenate([high, low], axis=0), high_ref[b])
            message = message + both[:channels] + both[channels:] + fast_dot(high, low_ref[b])
        update = exact_dot(upd_t_ref[...], message)
        sigmoid = jax.nn.sigmoid(update)
        out_cols = jnp.broadcast_to(out_w_ref[...], (8, channels)).T[:, 0:1]
        grad_update = out_cols * (sigmoid * (1.0 + update * (1.0 - sigmoid)))
        grad_message_t = exact_dot(upd_ref[1], grad_update)
        grad_message = grad_message_t.T

        grad_lent = jnp.zeros((extent, channels), F32)
        for b in range(basis_count):
            high, low = halves(grad_message * (radial_ref[1, b : b + 1] * scale))
            both = fast_dot(high_ref[b], jnp.concatenate([high, low], axis=1))
            grad_lent = grad_lent + both[:, :channels] + both[:, channels:] + fast_dot(low_ref[b], high)
        grad_hidden = exact_dot(msg_ref[1], grad_lent.T)
        grad_hidden = jnp.concatenate([grad_hidden[:, :atoms] + out_cols, grad_hidden[:, atoms:]], axis=1)
        row_h_ref[...] = exact_dot(first_ref[...], grad_hidden * slope_ref[...])
        high, low = halves(grad_message_t)
        grads_ref[...] = jnp.concatenate([high, high, low], axis=0)
        for b in range(basis_count):
            high, low = halves(lent * (radial_ref[1, b : b + 1] * scale))
            left_ref[b] = jnp.concatenate([high, low, high], axis=1)

        lane_row = lax.broadcasted_iota(jnp.int32, (BLOCK, LANES), 1)
        chain = -2.0 / (radial_width * math.sqrt(math.log2(math.e)))
        for own in (True, False):
            lanes = slice(0, atoms) if own else slice(atoms, extent)
            width = atoms if own else extent - atoms
            here = [ext_own[bead * 3 + x : bead * 3 + x + 1, lanes] for x in range(3)]

            def pair_grads(step, center, lanes=lanes, own=own, width=width, here=here):
                at = pl.ds(pl.multiple_of(step * BLOCK, BLOCK), BLOCK)
                reach = reach_ref[at, lanes]
                tallies = [count_ref[s, at, lanes] for s in range(species_count)]
                total = jnp.zeros((BLOCK, width), F32)
                for b in range(basis_count):
                    offset = reach - centers[b]
                    value = jnp.exp2(-(offset * offset)) * offset

                    def first_layer(s):
                        n = (b * species_count + s) * 8
                        return jnp.broadcast_to(row_h_ref[n : n + 1, lanes], (BLOCK, width))

                    slope = first_layer(0)
                    for s in range(1, species_count):
                        slope = jnp.where(tallies[s] > 0.0, first_layer(s), slope)
                    if own:
                        slope = slope + fast_dot(left_ref[b, at, :], grads_ref[...])
                    total = total + slope * value
                weight = total * functools.reduce(jnp.add, tallies) * inverse_ref[at, lanes] * chain
                center = list(center)
                columns = jnp.zeros((BLOCK, LANES), F32)
                for x in range(3):
                    near = near_ref[0 if own else 1, bead * 3 + x, at, :]
                    if width > LANES:
                        near = jnp.concatenate([near] * (width // LANES), axis=1)
                    pull = weight * (near - here[x])
                    for part in range(BLOCK // 8):
                        center[x] = center[x] + pull[part * 8 : part * 8 + 8]
                    if own:
                        columns = jnp.where(lane_row == bead * 3 + x, jnp.sum(pull, axis=1, keepdims=True), columns)
                    else:
                        left = jnp.sum(jnp.where(lane_row < ghosts, pull, 0.0), axis=1, keepdims=True)
                        right = jnp.sum(jnp.where(lane_row < ghosts, 0.0, pull), axis=1, keepdims=True)
                        columns = jnp.where(lane_row == 8 + bead * 3 + x, left, columns)
                        columns = jnp.where(lane_row == 16 + bead * 3 + x, right, columns)
                edge_ref[at, :] = edge_ref[at, :] + columns
                return tuple(center)

            zero = jnp.zeros((8, width), F32)
            center = lax.fori_loop(0, extent // BLOCK, pair_grads, (zero,) * 3)
            pulls.append([jnp.sum(c, axis=0, keepdims=True) for c in center])

    edges = edge_ref[...].T
    edge_own, edge_left, edge_right = edges[0:rows], edges[8 : 8 + rows], edges[16 : 16 + rows]
    center = jnp.concatenate(
        [
            jnp.concatenate([pulls[2 * bead][x], pulls[2 * bead + 1][x]], axis=1)
            for bead in range(reduced_dev)
            for x in range(3)
        ],
        axis=0,
    )
    edge_own = edge_own - center

    def at_head(values):
        return jnp.concatenate([values, jnp.zeros((rows, tail), F32)], axis=1)

    def at_tail(values):
        return jnp.concatenate([jnp.zeros((rows, tail), F32), values], axis=1)

    lower = slice(atoms, atoms + ghosts)
    upper = slice(atoms + ghosts, extent)
    back = {
        0: edge_own[:, :atoms] + at_head(edge_left[:, upper]) + at_tail(edge_right[:, lower]),
        -1: edge_left[:, :atoms] + at_tail(edge_own[:, lower]),
        1: edge_right[:, :atoms] + at_head(edge_own[:, upper]),
        -2: at_tail(edge_left[:, lower]),
        2: at_head(edge_right[:, upper]),
    }
    out_ref[0] = jnp.zeros_like(out_ref[0])
    for step, values in back.items():
        place = lax.rem(domain + step + 2 * domains, domains)
        out_ref[0, place] = out_ref[0, place] + values
    for group in range(1, groups):
        out_ref[group] = out_ref[0]


def on_device(
    positions, species, neighbors, counts, send_rows, embed, w_radial, w_msg, w_upd, w_out
):
    full_dev, _, atoms = positions.shape
    groups = lax.axis_size("bead")
    domains = lax.axis_size("space")
    beads_all = full_dev * groups
    reduced_dev = PC // groups
    rows = reduced_dev * 3
    slots = neighbors.shape[0]
    ghosts = send_rows.shape[0] // 2
    extent = atoms + 2 * ghosts
    species_count, channels = embed.shape
    layers, basis_count, _ = w_radial.shape
    table = jnp.asarray(contraction(beads_all, PC))
    vmem = pl.BlockSpec(memory_space=pltpu.VMEM)
    smem = pl.BlockSpec(memory_space=pltpu.SMEM)
    params = pltpu.CompilerParams(vmem_limit_bytes=VMEM_BYTES)

    def shaped(*shape):
        return jax.ShapeDtypeStruct(shape, F32)

    last = jnp.stack([species, jnp.pad(send_rows, (0, atoms - 2 * ghosts))])
    pack = jnp.concatenate([neighbors, counts[None], last], axis=0)

    def shift(values, by):
        return lax.ppermute(values, "space", [(i, (i + by) % domains) for i in range(domains)])

    from_left = shift(pack, 1)
    from_right = shift(pack, -1)
    from_far_left = shift(last, 2)
    from_far_right = from_far_left if domains == 4 else shift(last, -2)

    spread = pl.pallas_call(
        spread_kernel,
        out_shape=shaped(groups, domains, rows, atoms),
        in_specs=[smem, vmem],
        out_specs=vmem,
        compiler_params=params,
    )(table, positions)
    arrived = lax.all_to_all(
        spread.reshape(groups * domains, rows, atoms), ("bead", "space"), 0, 0, tiled=True
    )

    sums_rows = basis_count * species_count * 8
    prepared = pl.pallas_call(
        functools.partial(prepare_kernel, slots=slots, ghosts=ghosts),
        out_shape=[
            shaped(species_count, extent, extent),
            shaped(channels, extent),
            shaped(sums_rows, channels),
            shaped(channels, sums_rows),
            shaped(channels, channels),
            shaped(channels, channels),
        ],
        in_specs=[vmem] * 9,
        out_specs=[vmem] * 6,
        compiler_params=params,
    )(pack, from_left, from_right, from_far_left, from_far_right, embed, w_radial, w_msg, w_upd)

    grads = pl.pallas_call(
        functools.partial(force_kernel, domains=domains, slots=slots, ghosts=ghosts),
        out_shape=shaped(groups, domains, rows, atoms),
        in_specs=[vmem] * 11,
        out_specs=vmem,
        scratch_shapes=[
            pltpu.VMEM((2, rows, extent, LANES), F32),
            pltpu.VMEM((extent, extent), F32),
            pltpu.VMEM((extent, extent), F32),
            pltpu.VMEM((basis_count, extent, atoms), BF16),
            pltpu.VMEM((basis_count, extent, atoms), BF16),
            pltpu.VMEM((sums_rows, extent), F32),
            pltpu.VMEM((extent, LANES), F32),
            pltpu.VMEM((3 * channels, atoms), BF16),
            pltpu.VMEM((basis_count, extent, 3 * channels), BF16),
            pltpu.VMEM((channels, extent), F32),
            pltpu.VMEM((sums_rows, extent), F32),
        ],
        compiler_params=params,
    )(arrived, *prepared, w_radial, w_msg, w_upd, w_out[None])

    returned = lax.all_to_all(
        grads.reshape(groups * domains, rows, atoms), ("bead", "space"), 0, 0, tiled=True
    )
    return pl.pallas_call(
        functools.partial(collect_kernel, float(beads_all) / PC),
        out_shape=shaped(full_dev, 3, atoms),
        in_specs=[smem, vmem],
        out_specs=vmem,
        compiler_params=params,
    )(table, returned.reshape(groups, domains, rows, atoms))


def solution(mesh):
    return jax.shard_map(
        on_device,
        mesh=mesh,
        in_specs=(
            P("bead", None, "space"),
            P("space"),
            P(None, "space"),
            P("space"),
            P("space"),
            P(),
            P(),
            P(),
            P(),
            P(),
        ),
        out_specs=P("bead", None, "space"),
        check_vma=False,
    )
```

time: 249 us -> 67.6 us (0.27)
  matrix products: 161 us -> 0 us
  blocking collectives: 63.1 us -> 15.4 us
  Pallas kernels: 0 us -> 31.8 us
  local copies, waits for them, and re-layouts: 2.39 us -> 5.97 us
  waiting for transfers between devices: 6.22 us -> 2.84 us
    dot_general x46 -> x0, matrix products: 161 us -> none  [the longest x4 33 us: block_message(): jnp.einsum('nbkr,nc->bkrc', radial_basis, radial_map, precision=exact_mode)]
    all_gather x2 -> x0, blocking collectives: 63.1 us -> none  [the longest x1 32.6 us: on_device(): lax.all_gather(positions, 'bead', axis=0, tiled=True)]
    pallas_call x0 -> x4, Pallas kernels: none -> 31.8 us  [the longest x1 28.3 us: on_device(): pl.pallas_call(functools.partial(force_kernel, domains=domains, slots=slo...]
    all_to_all x0 -> x1, blocking collectives: none -> 15.4 us  [on_device(): lax.all_to_all(grads.reshape(groups * domains, rows, atoms), ('bead', 'sp...]
    all_to_all x0 -> x1, starting transfers between devices: none -> 7.3 us  [on_device(): lax.all_to_all(spread.reshape(groups * domains, rows, atoms), ('bead', 's...]
    ppermute x8 -> x3, starting transfers between devices: 7.36 us -> 2.3 us  [shift(): lax.ppermute(values, 'space', [(i, (i + by) % domains) for i in range(dom...]
    unnamed x10 -> x21, local copies, waits for them, and re-layouts: 0.03 us -> 4.69 us
    ppermute x8 -> x3, waiting for transfers between devices: 6.22 us -> 2.84 us  [shift(): lax.ppermute(values, 'space', [(i, (i + by) % domains) for i in range(dom...]
  transfers between devices with their start and end apart: 8 -> 4, of which waited for: 5 -> 1; matrix products, arithmetic and copies ran while one was open for 2% -> 3% of each run, Pallas kernels for 0% -> 2%
where the time goes in v1:
time: 67.6 us; the launch traced here: 67.2 us
  Pallas kernels  31.8 us (47%)
  blocking collectives  15.4 us (23%)
  starting transfers between devices  9.6 us (14%)
  local copies, waits for them, and re-layouts  5.97 us (9%)
  waiting for transfers between devices  2.84 us (4%)
  other arithmetic  1.49 us (2%)
    pallas_call x1, Pallas kernels, on_device(): pl.pallas_call(functools.partial(force_kernel, domains=domains, slots=slo...  28.3 us
    all_to_all x1, blocking collectives, on_device(): lax.all_to_all(grads.reshape(groups * domains, rows, atoms), ('bead', 'sp...  15.4 us
    all_to_all x1, starting transfers between devices, on_device(): lax.all_to_all(spread.reshape(groups * domains, rows, atoms), ('bead', 's...  7.3 us
    unnamed x21, local copies, waits for them, and re-layouts  4.69 us
    ppermute x3, waiting for transfers between devices, shift(): lax.ppermute(values, 'space', [(i, (i + by) % domains) for i in range(dom...  2.84 us
    ppermute x3, starting transfers between devices, shift(): lax.ppermute(values, 'space', [(i, (i + by) % domains) for i in range(dom...  2.3 us
    pallas_call x1, Pallas kernels, on_device(): pl.pallas_call(spread_kernel, out_shape=shaped(groups, domains, rows, ato...  1.49 us
  transfers between devices with their start and end apart: 4, of which 1 were waited for; matrix products, arithmetic and copies ran while one was open for 3% of the time, Pallas kernels for 2%

profile of v1, /device:TPU:0, one launch (start us, length us, event | category | flops | bytes accessed | tf_op | source)
XLA Modules:
  0.0 67.2 jit_solution(14955914341739953793)
XLA Ops:
  0.0 0.0 copy-start.3
  0.0 0.0 copy-start.1
  0.0 0.0 copy-start.5
  0.0 0.8 %copy.12.pos_ref = f32[8,3,256]{2,1,0:T(4,128)S(1)} copy(f32[8,3,256]{2,0,1:T(8,128)} %param.11) | data formatting | bytes 49152 | tf_op args[0]
  0.8 0.0 copy-start.6
  0.8 0.7 %copy-done.6 = f32[16,64]{1,0:T(8,128)S(1)} copy-done((f32[16,64]{1,0:T(8,128)S(1)}, f32[16,64]{1,0:T(8,128)}, u32[]{:S(2)}) %copy-start.6) | copy-done | bytes 4120
  1.5 0.0 copy-start.9
  1.5 1.5 %shard_map.109 = f32[8,4,6,256]{3,2,1,0:T(8,128)} custom-call(f32[16,64]{1,0:T(8,128)S(1)} %copy-done.6, f32[8,3,256]{2,1,0:T(4,128)S(1)} %copy.12.pos_ref), custom_call_target="tpu_custom_call" | custom-call | tf_op jit(solution)/shard_map/pallas_call | solution.py:430
  3.0 7.3 %all-to-all-start = ((f32[32,6,256]{2,1,0:T(8,128)}), f32[32,6,256]{2,1,0:T(8,128)S(1)}, u32[]{:S(2)}, u32[]{:S(2)}) async-start(f32[32,6,256]{2,1,0:T(8,128)} %bitcast), calls=%async_computation | async-start | bytes 524288 | tf_op jit(solution)/shard_map/all_to_all | solution.py:437
  10.3 0.7 pad.4
  11.0 0.8 %pad_add_fusion.own_ref = s32[35,256]{1,0:T(8,128)S(1)} fusion(s32[1,256]{1,0:T(1,128)S(1)} %bitcast.10, s32[1,256]{1,0:T(1,128)} %bitcast.12, s32[1,256]{1,0:T(1,128)} %bitcast.14, s32[32,256]{1,0:T(8,128)} %param.13), kind=kLoop, calls=%fused_computation | loop fusion | flops 26880 | bytes 71680 | tf_op jit(solution)/shard_map/concatenate | solution.py:420
  11.8 1.5 %collective-permute-start.1 = (s32[35,256]{1,0:T(8,128)S(1)}, s32[35,256]{1,0:T(8,128)S(1)}, u32[]{:S(2)}, u32[]{:S(2)}) collective-permute-start(s32[35,256]{1,0:T(8,128)S(1)} %pad_add_fusion.own_ref), channel_id=1, source_target_pairs={{0,3},{1,0},{2,1},{3,2},{4,7},{5,4},{6,5},{7,6},{8,11},{9,8},{10,9... | collective-permute-start | bytes 107528 | tf_op jit(solution)/shard_map/ppermute | solution.py:423
  13.3 0.0 collective-permute-start
  13.3 0.7 %pad_add_fusion.1 = s32[2,256]{1,0:T(2,128)S(1)} fusion(s32[1,256]{1,0:T(1,128)S(1)} %bitcast.11, s32[1,256]{1,0:T(1,128)} %bitcast.13), kind=kLoop, calls=%fused_computation.1 | loop fusion | flops 512 | bytes 4096 | tf_op jit(solution)/shard_map/stack | solution.py:419
  14.0 0.8 %collective-permute-start.2 = (s32[2,256]{1,0:T(2,128)S(1)}, s32[2,256]{1,0:T(2,128)S(1)}, u32[]{:S(2)}, u32[]{:S(2)}) collective-permute-start(s32[2,256]{1,0:T(2,128)S(1)} %pad_add_fusion.1), channel_id=1, source_target_pairs={{0,2},{1,3},{2,0},{3,1},{4,6},{5,7},{6,4},{7,5},{8,10},{9,11},{10,... | collective-permute-start | bytes 6152 | tf_op jit(solution)/shard_map/ppermute | solution.py:423
  14.8 2.8 %collective-permute-done.2.far_left_ref.far_right_ref = s32[2,256]{1,0:T(2,128)S(1)} collective-permute-done((s32[2,256]{1,0:T(2,128)S(1)}, s32[2,256]{1,0:T(2,128)S(1)}, u32[]{:S(2)}, u32[]{:S(2)}) %collective-permute-start.2) | collective-permute-done | bytes 2080 | tf_op jit(solution)/shard_map/ppermute | solution.py:423
  17.6 0.0 collective-permute-done.1.right_ref
  17.6 0.0 collective-permute-done.left_ref
  17.6 0.0 copy-start
  17.6 0.9 %copy-done = f32[2,128,128]{2,1,0:T(8,128)S(1)} copy-done((f32[2,128,128]{2,1,0:T(8,128)S(1)}, f32[2,128,128]{2,1,0:T(8,128)}, u32[]{:S(2)}) %copy-start) | copy-done | bytes 131096
  18.5 0.0 copy-start.2
  18.5 0.9 %copy-done.2 = f32[2,128,128]{2,1,0:T(8,128)S(1)} copy-done((f32[2,128,128]{2,1,0:T(8,128)S(1)}, f32[2,128,128]{2,1,0:T(8,128)}, u32[]{:S(2)}) %copy-start.2) | copy-done | bytes 131096
  19.4 0.0 copy-start.4
  19.4 0.7 %copy-done.4 = f32[2,8,128]{2,1,0:T(8,128)S(1)} copy-done((f32[2,8,128]{2,1,0:T(8,128)S(1)}, f32[2,8,128]{2,1,0:T(8,128)}, u32[]{:S(2)}) %copy-start.4) | copy-done | bytes 8216
  20.1 0.0 copy-start.8
  20.1 0.7 %copy-done.8 = f32[2,128]{1,0:T(2,128)S(1)} copy-done((f32[2,128]{1,0:T(2,128)S(1)}, f32[2,128]{1,0:T(2,128)}, u32[]{:S(2)}) %copy-start.8) | copy-done | bytes 1048
  20.8 1.2 %shard_map.110 = (f32[2,384,384]{2,1,0:T(8,128)S(1)}, f32[128,384]{1,0:T(8,128)S(1)}, f32[128,128]{1,0:T(8,128)S(1)}, f32[128,128]{1,0:T(8,128)S(1)}, f32[128,128]{1,0:T(8,128)S(1)}, /*index=5*/f32[128,128]{1,0:T(8,128)S(1)}) custom-call(s32[35,256]{1,0:T(8,128)S(1)} %pad_add_fusion.own_ref, s32[35,256]{1,0:T(8,128)S(1)} %collective-permute-done.left_ref, ...), custom_call_target="tpu_custom_call" | custom-call | tf_op jit(solution)/shard_map/pallas_call | solution.py:442
  22.0 0.0 all-to-all-done.recv_ref
  22.0 0.0 copy-done.3
  22.0 0.0 copy-done.1
  22.0 0.0 copy-done.5
  22.0 0.0 copy-done.9
  22.0 0.0 copy-start.7
  22.0 28.3 %shard_map.111 = f32[8,4,6,256]{3,2,1,0:T(8,128)S(1)} custom-call(f32[32,6,256]{2,1,0:T(8,128)S(1)} %all-to-all-done.recv_ref, f32[2,384,384]{2,1,0:T(8,128)S(1)} %get-tuple-element.11.count_ref, f32[128,384]{1,0:T(8,128)S(1)} %get-tuple-element.12.hidden_ref, f32[128,128]{1,0:T(8,128)S(1)} %get-tuple-element.13.first_ref, ...), custom_call_target="tpu_custom_call" | custom-call | tf_op jit(solution)/shard_map/pallas_call | solution.py:457
  50.3 15.4 %all_to_all.10 = f32[32,6,256]{2,1,0:T(8,128)S(1)} all-to-all(f32[32,6,256]{2,1,0:T(8,128)S(1)} %bitcast.8), channel_id=1, replica_groups=mesh['bead'=8,'space'=4] {'bead','space'}, dimensions={0} | all-to-all | bytes 393216 | tf_op jit(solution)/shard_map/all_to_all | solution.py:478
  65.8 0.0 copy-done.7
  65.8 0.8 %shard_map.112 = f32[8,3,256]{2,1,0:T(4,128)S(1)} custom-call(f32[16,64]{1,0:T(8,128)S(1)} %copy-done.7, f32[8,4,6,256]{3,2,1,0:T(8,128)S(1)} %bitcast.7), custom_call_target="tpu_custom_call" | custom-call | tf_op jit(solution)/shard_map/pallas_call | solution.py:481
  66.6 0.6 copy.13
Async XLA Ops:
  0.0 22.0 %copy-start.3 = (f32[2,128,128]{2,1,0:T(8,128)S(1)}, f32[2,128,128]{2,1,0:T(8,128)}, u32[]{:S(2)}) copy-start(f32[2,128,128]{2,1,0:T(8,128)} %upd_ref.3) | copy-start | bytes 393220
  0.0 22.0 %copy-start.1 = (f32[2,128,128]{2,1,0:T(8,128)S(1)}, f32[2,128,128]{2,1,0:T(8,128)}, u32[]{:S(2)}) copy-start(f32[2,128,128]{2,1,0:T(8,128)} %msg_ref.3) | copy-start | bytes 393220
  0.0 22.0 %copy-start.5 = (f32[2,8,128]{2,1,0:T(8,128)S(1)}, f32[2,8,128]{2,1,0:T(8,128)}, u32[]{:S(2)}) copy-start(f32[2,8,128]{2,1,0:T(8,128)} %radial_ref.3) | copy-start | bytes 24580
  0.8 0.7 %copy-start.6 = (f32[16,64]{1,0:T(8,128)S(1)}, f32[16,64]{1,0:T(8,128)}, u32[]{:S(2)}) copy-start(f32[16,64]{1,0:T(8,128)} %constant.4.clone.table_ref) | copy-start | bytes 12292
  1.5 20.5 %copy-start.9 = (f32[128]{0:T(128)S(1)}, f32[128]{0:T(128)}, u32[]{:S(2)}) copy-start(f32[128]{0:T(128)} %param.20) | copy-start | bytes 1540
  3.0 19.0 %all-to-all-start = ((f32[32,6,256]{2,1,0:T(8,128)}), f32[32,6,256]{2,1,0:T(8,128)S(1)}, u32[]{:S(2)}, u32[]{:S(2)}) async-start(f32[32,6,256]{2,1,0:T(8,128)} %bitcast), calls=%async_computation | async-start | bytes 524288 | tf_op jit(solution)/shard_map/all_to_all | solution.py:437
  11.8 5.8 %collective-permute-start.1 = (s32[35,256]{1,0:T(8,128)S(1)}, s32[35,256]{1,0:T(8,128)S(1)}, u32[]{:S(2)}, u32[]{:S(2)}) collective-permute-start(s32[35,256]{1,0:T(8,128)S(1)} %pad_add_fusion.own_ref), channel_id=1, source_target_pairs={{0,3},{1,0},{2,1},{3,2},{4,7},{5,4},{6,5},{7,6},{8,11},{9,8},{10,9... | collective-permute-start | bytes 107528 | tf_op jit(solution)/shard_map/ppermute | solution.py:423
  13.3 4.3 %collective-permute-start = (s32[35,256]{1,0:T(8,128)S(1)}, s32[35,256]{1,0:T(8,128)S(1)}, u32[]{:S(2)}, u32[]{:S(2)}) collective-permute-start(s32[35,256]{1,0:T(8,128)S(1)} %pad_add_fusion.own_ref), channel_id=1, source_target_pairs={{0,1},{1,2},{2,3},{3,0},{4,5},{5,6},{6,7},{7,4},{8,9},{9,10},{10,1... | collective-permute-start | bytes 107528 | tf_op jit(solution)/shard_map/ppermute | solution.py:423
  14.0 3.6 %collective-permute-start.2 = (s32[2,256]{1,0:T(2,128)S(1)}, s32[2,256]{1,0:T(2,128)S(1)}, u32[]{:S(2)}, u32[]{:S(2)}) collective-permute-start(s32[2,256]{1,0:T(2,128)S(1)} %pad_add_fusion.1), channel_id=1, source_target_pairs={{0,2},{1,3},{2,0},{3,1},{4,6},{5,7},{6,4},{7,5},{8,10},{9,11},{10,... | collective-permute-start | bytes 6152 | tf_op jit(solution)/shard_map/ppermute | solution.py:423
  17.6 0.9 %copy-start = (f32[2,128,128]{2,1,0:T(8,128)S(1)}, f32[2,128,128]{2,1,0:T(8,128)}, u32[]{:S(2)}) copy-start(f32[2,128,128]{2,1,0:T(8,128)} %msg_ref.3) | copy-start | bytes 393220
  18.5 0.9 %copy-start.2 = (f32[2,128,128]{2,1,0:T(8,128)S(1)}, f32[2,128,128]{2,1,0:T(8,128)}, u32[]{:S(2)}) copy-start(f32[2,128,128]{2,1,0:T(8,128)} %upd_ref.3) | copy-start | bytes 393220
  19.4 0.7 %copy-start.4 = (f32[2,8,128]{2,1,0:T(8,128)S(1)}, f32[2,8,128]{2,1,0:T(8,128)}, u32[]{:S(2)}) copy-start(f32[2,8,128]{2,1,0:T(8,128)} %radial_ref.3) | copy-start | bytes 24580
  20.1 0.7 %copy-start.8 = (f32[2,128]{1,0:T(2,128)S(1)}, f32[2,128]{1,0:T(2,128)}, u32[]{:S(2)}) copy-start(f32[2,128]{1,0:T(2,128)} %embed_ref.1) | copy-start | bytes 3076
  22.0 43.7 %copy-start.7 = (f32[16,64]{1,0:T(8,128)S(1)}, f32[16,64]{1,0:T(8,128)}, u32[]{:S(2)}) copy-start(f32[16,64]{1,0:T(8,128)} %constant.4.clone.table_ref) | copy-start | bytes 12292

commit v2 on v1

v2 whole, which is shorter than its diff:
```python
import functools
import math

import jax
import jax.numpy as jnp
import numpy as np
from jax import lax
from jax.experimental import pallas as pl
from jax.experimental.pallas import tpu as pltpu
from jax.sharding import PartitionSpec as P

PC = 16

exact_mode = lax.Precision.HIGHEST
spacing_floor = 0.01
radial_width = 0.2
radial_reach = 1.5
LANES = 128
PLANES = 4
ROWS = 16
BLOCK = 64
F32 = jnp.float32
BF16 = jnp.bfloat16
UNROLL = 4
VMEM_BYTES = 48 * 1024 * 1024
kappa = math.sqrt(math.log2(math.e)) / radial_width


def contraction(full_beads, reduced_beads):
    gap = np.arange(reduced_beads)[:, None] / reduced_beads - np.arange(full_beads)[None, :] / full_beads
    total = np.ones_like(gap)
    for harmonic in range(1, reduced_beads // 2):
        total = total + 2.0 * np.cos(2.0 * np.pi * harmonic * gap)
    total = total + np.cos(np.pi * reduced_beads * gap)
    return (total / full_beads).astype(np.float32)


def exact_dot(left, right):
    return lax.dot(left, right, precision=exact_mode, preferred_element_type=F32)


def near_dot(left, right):
    return lax.dot(left, right, precision=lax.Precision.HIGH, preferred_element_type=F32)


def fast_dot(left, right):
    return lax.dot(left, right, preferred_element_type=F32)


def halves(values):
    high = values.astype(BF16)
    low = (values - high.astype(F32)).astype(BF16)
    return high, low


def spread_kernel(table_ref, pos_ref, out_ref):
    components, full_dev, atoms = pos_ref.shape
    groups, domains, rows, _ = out_ref.shape
    values = pos_ref[...].reshape(components * full_dev, atoms)
    total = exact_dot(table_ref[lax.axis_index("bead")], values).reshape(groups, rows, atoms)
    for domain in range(domains):
        out_ref[:, domain] = total


def collect_kernel(table_ref, in_ref, out_ref):
    groups, domains, rows, atoms = in_ref.shape
    total = in_ref[:, 0]
    for domain in range(1, domains):
        total = total + in_ref[:, domain]
    out = exact_dot(table_ref[lax.axis_index("bead")], total.reshape(groups * rows, atoms))
    out_ref[...] = out.reshape(out_ref.shape)


def spread_tables(beads_all, groups, pad_rows):
    table = contraction(beads_all, PC)
    full_dev, reduced_dev = beads_all // groups, PC // groups
    out = np.zeros((groups, groups, pad_rows, 3, full_dev), np.float32)
    for own in range(groups):
        for group in range(groups):
            part = table[group * reduced_dev : (group + 1) * reduced_dev, own * full_dev : (own + 1) * full_dev]
            for x in range(3):
                out[own, group, x * reduced_dev : (x + 1) * reduced_dev, x] = part
    out = out.reshape(groups, groups * pad_rows, 3 * full_dev)
    back = -(beads_all / PC) * out.transpose(0, 2, 1)
    return jnp.asarray(out), jnp.asarray(np.ascontiguousarray(back.astype(np.float32)))


def prepare_kernel(
    own_ref, left_ref, right_ref, far_left_ref, far_right_ref, embed_ref, radial_ref, msg_ref, upd_ref,
    count_ref, hidden_ref, first_ref, first_t_ref, msg_t_ref, upd_t_ref, fan_ref, fold_ref,
    *, slots, ghosts,
):
    atoms = own_ref.shape[1]
    extent = atoms + 2 * ghosts
    species_count, channels = embed_ref.shape
    basis_count = radial_ref.shape[1]
    tail = atoms - ghosts
    count_row, species_row, send_row = slots, slots + 1, slots + 2

    def edge_pack(row, rows=1):
        return jnp.concatenate(
            [own_ref[row : row + rows], left_ref[row : row + rows, tail:], right_ref[row : row + rows, :ghosts]],
            axis=1,
        )

    neighbors = edge_pack(0, slots)
    counts = edge_pack(count_row)
    own_send = own_ref[send_row : send_row + 1]
    left_send = left_ref[send_row : send_row + 1]
    right_send = right_ref[send_row : send_row + 1]
    far_left_send = far_left_ref[1:2]
    far_right_send = far_right_ref[1:2]

    def ghost_map(from_left, from_right):
        return jnp.concatenate(
            [from_left[:, ghosts : 2 * ghosts] - tail, from_right[:, :ghosts] + ghosts], axis=1
        )

    maps = [
        ghost_map(left_send, right_send),
        ghost_map(far_left_send, own_send),
        ghost_map(own_send, far_right_send),
    ]
    maps = [jnp.broadcast_to(m, (slots, 2 * ghosts)) for m in maps]
    lane = lax.broadcasted_iota(jnp.int32, (slots, LANES), 1)
    slot = lax.broadcasted_iota(jnp.int32, (slots, LANES), 0)

    species_rows = []
    for near, lower, upper in (
        (own_ref[species_row : species_row + 1], left_ref[species_row : species_row + 1], right_ref[species_row : species_row + 1]),
        (left_ref[species_row : species_row + 1], far_left_ref[0:1], own_ref[species_row : species_row + 1]),
        (right_ref[species_row : species_row + 1], own_ref[species_row : species_row + 1], far_right_ref[0:1]),
    ):
        species_rows.append(jnp.concatenate([near, lower[:, tail:], upper[:, :ghosts]], axis=1))
    species_f = jnp.concatenate(species_rows + [species_rows[0]] * 5, axis=0).astype(F32)
    species_cols = species_f.T

    plane_rows = extent // PLANES
    chunks = extent // LANES
    plane_iota = lax.broadcasted_iota(jnp.int32, (plane_rows, LANES), 0)
    lane_block = lax.broadcasted_iota(jnp.int32, (plane_rows, LANES), 1)
    for chunk in range(chunks):
        lanes = slice(chunk * LANES, (chunk + 1) * LANES)
        rows_now = neighbors[:, lanes]
        index = jnp.clip(rows_now - atoms, 0, 2 * ghosts - 1)
        if (chunk + 1) * LANES <= atoms:
            mapped = jnp.take_along_axis(maps[0], index, axis=1, mode="promise_in_bounds")
        else:
            mapped = jnp.where(
                lane < ghosts,
                jnp.take_along_axis(maps[1], index, axis=1, mode="promise_in_bounds"),
                jnp.take_along_axis(maps[2], index, axis=1, mode="promise_in_bounds"),
            )
        rows_now = jnp.where(rows_now >= atoms, atoms + mapped, rows_now)
        plane = jnp.zeros_like(rows_now)
        for step in range(1, PLANES):
            plane = plane + (rows_now >= step * plane_rows).astype(jnp.int32)
        within = rows_now - plane * plane_rows
        within = jnp.where(slot < counts[:, lanes], within, -1)
        value = jnp.left_shift(jnp.ones_like(plane), 8 * plane)
        words = jnp.zeros((plane_rows, LANES), jnp.int32)
        for k in range(slots):
            words = words + jnp.where(within[k : k + 1] == plane_iota, value[k : k + 1], 0)
        for step in range(PLANES):
            rows = slice(step * plane_rows, (step + 1) * plane_rows)
            tally = (jnp.right_shift(words, 8 * step) & 255).astype(F32)
            if (chunk + 1) * LANES <= atoms:
                kind = jnp.broadcast_to(species_cols[rows, 0:1], (plane_rows, LANES))
            else:
                kind = jnp.where(lane_block < ghosts, species_cols[rows, 1:2], species_cols[rows, 2:3])
            for s in range(species_count):
                count_ref[s, rows, lanes] = jnp.where(kind == float(s), tally, 0.0)

    embed = embed_ref[...]
    embed_pad = jnp.concatenate([embed, jnp.zeros((8 - species_count, channels), F32)], axis=0)
    embed_cols = embed_pad.T
    hidden = jnp.zeros((channels, extent), F32)
    for s in range(species_count):
        hidden = hidden + embed_cols[:, s : s + 1] * (species_f[0:1] == float(s)).astype(F32)
    hidden_ref[...] = hidden

    scale = slots ** (-0.5)
    lent = exact_dot(embed_pad, msg_ref[0])
    stacked = []
    for b in range(basis_count):
        for s in range(species_count):
            row = radial_ref[0, b : b + 1] * lent[s : s + 1] * scale
            stacked.append(jnp.broadcast_to(row, (8, channels)))
    first = exact_dot(jnp.concatenate(stacked, axis=0), upd_ref[0])
    first_ref[...] = first
    first_t_ref[...] = first.T
    msg_t_ref[...] = msg_ref[1].T
    upd_t_ref[...] = upd_ref[1].T

    row = lax.broadcasted_iota(jnp.int32, fan_ref.shape, 0)
    column = lax.broadcasted_iota(jnp.int32, fan_ref.shape, 1)
    part = lax.rem(column, 2 * LANES)
    part = (part >= LANES).astype(jnp.int32) + (part >= LANES + ghosts).astype(jnp.int32)
    pad_rows = fan_ref.shape[0] // 9
    fan_ref[...] = jnp.where(
        lax.rem(row, 3 * pad_rows) == part * pad_rows + lax.div(column, 2 * LANES), 1.0, 0.0
    ).astype(BF16)
    row = lax.broadcasted_iota(jnp.int32, fold_ref.shape, 0)
    column = lax.broadcasted_iota(jnp.int32, fold_ref.shape, 1)
    part = jnp.where(
        lax.rem(row, 4 * LANES) < 2 * LANES, 0, jnp.where(lax.rem(row, LANES) < ghosts, 1, 2)
    )
    fold_ref[...] = jnp.where(column == part * pad_rows + lax.div(row, 4 * LANES), 1.0, 0.0).astype(BF16)


def force_kernel(
    recv_ref, count_ref, hidden_ref, first_ref, first_t_ref, msg_t_ref, upd_t_ref, fan_ref, fold_ref, radial_ref, msg_ref, upd_ref, out_w_ref,
    out_ref,
    near_ref, reach_ref, inverse_ref, high_ref, low_ref, sums_ref, edge_ref, slope_pair_ref, slope_ref, row_h_ref, wide_ref,
    *, domains, slots, ghosts, reduced_dev,
):
    groups = recv_ref.shape[0] // domains
    pad_rows, atoms = recv_ref.shape[1:]
    rows = reduced_dev * 3
    extent = atoms + 2 * ghosts
    tail = atoms - ghosts
    species_count = count_ref.shape[0]
    basis_count, channels = radial_ref.shape[1:]
    own_chunks = atoms // LANES
    chunks = extent // LANES
    beads = range(reduced_dev)
    domain = lax.axis_index("space")
    scale = slots ** (-0.5)
    centers = [kappa * radial_reach * b / (basis_count - 1) for b in range(basis_count)]

    is_first = lax.broadcasted_iota(jnp.int32, (pad_rows, atoms), 0) < reduced_dev
    segment = {}
    for step in range(-2, 3):
        shifted = domain + step + 2 * domains
        place = lax.rem(shifted, domains)
        wraps = (lax.div(shifted, domains) - 2).astype(F32) * float(domains)
        total = recv_ref[place]
        for group in range(1, groups):
            total = total + recv_ref[group * domains + place]
        segment[step] = total + jnp.where(is_first, wraps, 0.0)

    def extended(step):
        return jnp.concatenate(
            [segment[step], segment[step - 1][:, tail:], segment[step + 1][:, :ghosts]], axis=1
        )

    ext_own, ext_left, ext_right = extended(0), extended(-1), extended(1)
    stacked = jnp.concatenate([ext_own, ext_left, ext_right], axis=0)
    high = stacked.astype(BF16).astype(F32)
    middle = (stacked - high).astype(BF16).astype(F32)
    parts = jnp.concatenate([high, middle, stacked - high - middle], axis=0)
    near_ref[...] = fast_dot(parts.T.astype(BF16), fan_ref[...])

    def near(own, q, at):
        start = (2 * q + (0 if own else 1)) * LANES
        return near_ref[at, start : start + LANES]


    for bead in beads:
        for chunk in range(chunks):
            lanes = slice(chunk * LANES, (chunk + 1) * LANES)
            own = chunk < own_chunks
            here = [
                jnp.broadcast_to(ext_own[x * reduced_dev + bead : x * reduced_dev + bead + 1, lanes], (ROWS, LANES))
                for x in range(3)
            ]

            def gather_basis(step, sums, bead=bead, lanes=lanes, own=own, here=here):
                at = pl.ds(pl.multiple_of(step * ROWS, ROWS), ROWS)
                square = spacing_floor
                for x in range(3):
                    delta = near(own, x * reduced_dev + bead, at) - here[x]
                    square = square + delta * delta
                inverse = lax.rsqrt(square)
                reach = square * inverse * kappa
                inverse_ref[bead, at, lanes] = inverse
                reach_ref[bead, at, lanes] = reach
                tallies = [count_ref[s, at, lanes] for s in range(species_count)]
                tally = functools.reduce(jnp.add, tallies)
                sums = list(sums)
                for b in range(basis_count):
                    offset = reach - centers[b]
                    value = jnp.exp2(-(offset * offset))
                    for s in range(species_count):
                        term = tallies[s] * value
                        sums[b * species_count + s] = sums[b * species_count + s] + (term[:8] + term[8:])
                    if own:
                        high, low = halves(tally * value)
                        high_ref[bead, b, at, lanes] = high
                        low_ref[bead, b, at, lanes] = low
                return tuple(sums)

            zero = jnp.zeros((8, LANES), F32)
            sums = lax.fori_loop(0, extent // ROWS, gather_basis, (zero,) * (basis_count * species_count), unroll=UNROLL)
            for n, total in enumerate(sums):
                start = bead * extent + chunk * LANES
                sums_ref[n * 8 : n * 8 + 8, start : start + LANES] = total

    update = near_dot(first_t_ref[...], sums_ref[...])
    sigmoid = jax.nn.sigmoid(update)
    slope_ref[...] = sigmoid * (1.0 + update * (1.0 - sigmoid))
    hidden = jnp.concatenate([hidden_ref[...]] * reduced_dev, axis=1) + update * sigmoid
    lent_t = near_dot(msg_t_ref[...], hidden)
    lent = lent_t.T
    radial_cols = radial_ref[1].T * scale
    messages = []
    for bead in beads:
        for b in range(basis_count):
            high, low = halves(lent_t[:, bead * extent : (bead + 1) * extent] * radial_cols[:, b : b + 1])
            wide_ref[:channels, b * extent : (b + 1) * extent] = high
            wide_ref[channels:, b * extent : (b + 1) * extent] = low
        both = fast_dot(wide_ref[...], high_ref[bead].reshape(basis_count * extent, atoms))
        last = fast_dot(wide_ref[:channels], low_ref[bead].reshape(basis_count * extent, atoms))
        messages.append(both[:channels] + both[channels:] + last)
    message = jnp.concatenate(messages, axis=1)
    update = near_dot(upd_t_ref[...], message)
    sigmoid = jax.nn.sigmoid(update)
    out_cols = jnp.broadcast_to(out_w_ref[...], (8, channels)).T[:, 0:1]
    grad_update = out_cols * (sigmoid * (1.0 + update * (1.0 - sigmoid)))
    grad_message_t = near_dot(upd_ref[1], grad_update)
    grad_message = grad_message_t.T

    grads_lent = []
    for bead in beads:
        grad_lent = jnp.zeros((extent, channels), F32)
        for b in range(basis_count):
            high, low = halves(grad_message[bead * atoms : (bead + 1) * atoms] * (radial_ref[1, b : b + 1] * scale))
            both = fast_dot(high_ref[bead, b], jnp.concatenate([high, low], axis=1))
            grad_lent = grad_lent + both[:, :channels] + both[:, channels:] + fast_dot(low_ref[bead, b], high)
        grads_lent.append(grad_lent)
    grad_hidden = near_dot(msg_ref[1], jnp.concatenate(grads_lent, axis=0).T)
    parts = []
    for bead in beads:
        start = bead * extent
        parts += [grad_hidden[:, start : start + atoms] + out_cols, grad_hidden[:, start + atoms : start + extent]]
    row_h_ref[...] = near_dot(first_ref[...], jnp.concatenate(parts, axis=1) * slope_ref[...])
    for bead in beads:
        high, low = halves(grad_message_t[:, bead * atoms : (bead + 1) * atoms])
        grads = jnp.concatenate([high, high, low], axis=0)
        for b in range(basis_count):
            high, low = halves(lent[bead * extent : (bead + 1) * extent] * (radial_ref[1, b : b + 1] * scale))
            slope_pair_ref[bead, b] = fast_dot(jnp.concatenate([high, low, high], axis=1), grads)

    pulls = []
    chain = -2.0 / (radial_width * math.sqrt(math.log2(math.e)))
    for bead in beads:
        for own in (True, False):
            lanes = slice(0, atoms) if own else slice(atoms, extent)
            width = atoms if own else extent - atoms
            start = bead * extent + lanes.start
            here = [ext_own[x * reduced_dev + bead : x * reduced_dev + bead + 1, lanes] for x in range(3)]

            def pair_grads(step, center, bead=bead, lanes=lanes, own=own, width=width, here=here, start=start):
                at = pl.ds(pl.multiple_of(step * BLOCK, BLOCK), BLOCK)
                reach = reach_ref[bead, at, lanes]
                tallies = [count_ref[s, at, lanes] for s in range(species_count)]
                total = jnp.zeros((BLOCK, width), F32)
                for b in range(basis_count):
                    offset = reach - centers[b]
                    value = jnp.exp2(-(offset * offset)) * offset

                    def first_layer(s):
                        n = (b * species_count + s) * 8
                        tile = row_h_ref[n : n + 8, start : start + width]
                        return jnp.concatenate([tile] * (BLOCK // 8), axis=0)

                    slope = first_layer(0)
                    for s in range(1, species_count):
                        slope = jnp.where(tallies[s] > 0.0, first_layer(s), slope)
                    if own:
                        slope = slope + slope_pair_ref[bead, b, at, :]
                    total = total + slope * value
                weight = total * functools.reduce(jnp.add, tallies) * inverse_ref[bead, at, lanes] * chain
                center = list(center)
                for x in range(3):
                    q = x * reduced_dev + bead
                    place = near(own, q, at)
                    folded = None
                    for chunk in range(width // LANES):
                        cut = slice(chunk * LANES, (chunk + 1) * LANES)
                        pull = weight[:, cut] * (place - here[x][:, cut])
                        folded = pull if folded is None else folded + pull
                        n = x * (width // LANES) + chunk
                        for part in range(BLOCK // 8):
                            center[n] = center[n] + pull[part * 8 : part * 8 + 8]
                    high, low = halves(folded)
                    start_q = (2 * q + (0 if own else 1)) * 2 * LANES
                    edge_ref[at, start_q : start_q + LANES] = high
                    edge_ref[at, start_q + LANES : start_q + 2 * LANES] = low
                return tuple(center)

            zero = jnp.zeros((8, LANES), F32)
            many = width // LANES
            center = lax.fori_loop(0, extent // BLOCK, pair_grads, (zero,) * (3 * many))
            pulls.append(
                [
                    jnp.concatenate(
                        [jnp.sum(c, axis=0, keepdims=True) for c in center[x * many : (x + 1) * many]], axis=1
                    )
                    for x in range(3)
                ]
            )

    edges = fast_dot(edge_ref[...], fold_ref[...]).T
    edge_own, edge_left, edge_right = (edges[pad_rows * n : pad_rows * (n + 1)] for n in range(3))
    center = [
        jnp.concatenate([pulls[2 * bead][x], pulls[2 * bead + 1][x]], axis=1) for x in range(3) for bead in beads
    ]
    if rows < pad_rows:
        center.append(jnp.zeros((pad_rows - rows, extent), F32))
    edge_own = edge_own - jnp.concatenate(center, axis=0)

    def at_head(values):
        return jnp.concatenate([values, jnp.zeros((pad_rows, tail), F32)], axis=1)

    def at_tail(values):
        return jnp.concatenate([jnp.zeros((pad_rows, tail), F32), values], axis=1)

    lower = slice(atoms, atoms + ghosts)
    upper = slice(atoms + ghosts, extent)
    back = {
        0: edge_own[:, :atoms] + at_head(edge_left[:, upper]) + at_tail(edge_right[:, lower]),
        -1: edge_left[:, :atoms] + at_tail(edge_own[:, lower]),
        1: edge_right[:, :atoms] + at_head(edge_own[:, upper]),
        -2: at_tail(edge_left[:, lower]),
        2: at_head(edge_right[:, upper]),
    }
    out_ref[0] = jnp.zeros_like(out_ref[0])
    for step, values in back.items():
        place = lax.rem(domain + step + 2 * domains, domains)
        out_ref[0, place] = out_ref[0, place] + values
    for group in range(1, groups):
        out_ref[group] = out_ref[0]


def on_device(
    positions, species, neighbors, counts, send_rows, embed, w_radial, w_msg, w_upd, w_out
):
    full_dev, _, atoms = positions.shape
    groups = lax.axis_size("bead")
    domains = lax.axis_size("space")
    beads_all = full_dev * groups
    reduced_dev = PC // groups
    rows = -(-reduced_dev * 3 // 8) * 8
    slots = neighbors.shape[0]
    ghosts = send_rows.shape[0] // 2
    extent = atoms + 2 * ghosts
    species_count, channels = embed.shape
    layers, basis_count, _ = w_radial.shape
    table, back_table = spread_tables(beads_all, groups, rows)
    vmem = pl.BlockSpec(memory_space=pltpu.VMEM)
    params = pltpu.CompilerParams(vmem_limit_bytes=VMEM_BYTES)

    def shaped(*shape):
        return jax.ShapeDtypeStruct(shape, F32)

    last = jnp.stack([species, jnp.pad(send_rows, (0, atoms - 2 * ghosts))])
    pack = jnp.concatenate([neighbors, counts[None], last], axis=0)

    def shift(values, by):
        return lax.ppermute(values, "space", [(i, (i + by) % domains) for i in range(domains)])

    from_left = shift(pack, 1)
    from_right = shift(pack, -1)
    from_far_left = shift(last, 2)
    from_far_right = from_far_left if domains == 4 else shift(last, -2)

    spread = pl.pallas_call(
        spread_kernel,
        out_shape=shaped(groups, domains, rows, atoms),
        in_specs=[vmem, vmem],
        out_specs=vmem,
        compiler_params=params,
    )(table, positions.transpose(1, 0, 2))
    arrived = lax.all_to_all(
        spread.reshape(groups * domains, rows, atoms), ("bead", "space"), 0, 0, tiled=True
    )

    sums_rows = basis_count * species_count * 8
    lane_count = 2 * LANES * 3 * reduced_dev
    prepared = pl.pallas_call(
        functools.partial(prepare_kernel, slots=slots, ghosts=ghosts),
        out_shape=[
            shaped(species_count, extent, extent),
            shaped(channels, extent),
            shaped(sums_rows, channels),
            shaped(channels, sums_rows),
            shaped(channels, channels),
            shaped(channels, channels),
            jax.ShapeDtypeStruct((9 * rows, lane_count), BF16),
            jax.ShapeDtypeStruct((2 * lane_count, LANES), BF16),
        ],
        in_specs=[vmem] * 9,
        out_specs=[vmem] * 8,
        compiler_params=params,
    )(pack, from_left, from_right, from_far_left, from_far_right, embed, w_radial, w_msg, w_upd)

    grads = pl.pallas_call(
        functools.partial(force_kernel, domains=domains, slots=slots, ghosts=ghosts, reduced_dev=reduced_dev),
        out_shape=shaped(groups, domains, rows, atoms),
        in_specs=[vmem] * 13,
        out_specs=vmem,
        scratch_shapes=[
            pltpu.VMEM((extent, lane_count), F32),
            pltpu.VMEM((reduced_dev, extent, extent), F32),
            pltpu.VMEM((reduced_dev, extent, extent), F32),
            pltpu.VMEM((reduced_dev, basis_count, extent, atoms), BF16),
            pltpu.VMEM((reduced_dev, basis_count, extent, atoms), BF16),
            pltpu.VMEM((sums_rows, reduced_dev * extent), F32),
            pltpu.VMEM((extent, 2 * lane_count), BF16),
            pltpu.VMEM((reduced_dev, basis_count, extent, atoms), F32),
            pltpu.VMEM((channels, reduced_dev * extent), F32),
            pltpu.VMEM((sums_rows, reduced_dev * extent), F32),
            pltpu.VMEM((2 * channels, basis_count * extent), BF16),
        ],
        compiler_params=params,
    )(arrived, *prepared, w_radial, w_msg, w_upd, w_out[None])

    returned = lax.all_to_all(
        grads.reshape(groups * domains, rows, atoms), ("bead", "space"), 0, 0, tiled=True
    )
    forces = pl.pallas_call(
        collect_kernel,
        out_shape=shaped(3, full_dev, atoms),
        in_specs=[vmem, vmem],
        out_specs=vmem,
        compiler_params=params,
    )(back_table, returned.reshape(groups, domains, rows, atoms))
    return forces.transpose(1, 0, 2)


def solution(mesh):
    return jax.shard_map(
        on_device,
        mesh=mesh,
        in_specs=(
            P("bead", None, "space"),
            P("space"),
            P(None, "space"),
            P("space"),
            P("space"),
            P(),
            P(),
            P(),
            P(),
            P(),
        ),
        out_specs=P("bead", None, "space"),
        check_vma=False,
    )
```

time: 67.6 us -> 54.6 us (0.81)
  Pallas kernels: 31.8 us -> 21 us
  local copies, waits for them, and re-layouts: 5.97 us -> 3.78 us
    pallas_call x1, Pallas kernels: 28.3 us -> 17.7 us  [on_device(): pl.pallas_call(functools.partial(force_kernel, domains=domains, slots=slo...]
    unnamed x21 -> x18, local copies, waits for them, and re-layouts: 4.69 us -> 3.12 us
  transfers between devices with their start and end apart: 4 -> 4, of which waited for: 1 -> 2; matrix products, arithmetic and copies ran while one was open for 3% -> 4% of each run, Pallas kernels for 2% -> 3%
where the time goes in v2:
time: 54.6 us; the launch traced here: 54.2 us
  Pallas kernels  21 us (38%)
  blocking collectives  15.1 us (28%)
  starting transfers between devices  9.6 us (18%)
  local copies, waits for them, and re-layouts  3.78 us (7%)
  waiting for transfers between devices  3.14 us (6%)
  other arithmetic  1.49 us (3%)
    pallas_call x1, Pallas kernels, on_device(): pl.pallas_call(functools.partial(force_kernel, domains=domains, slots=slo...  17.7 us
    all_to_all x1, blocking collectives, on_device(): lax.all_to_all(grads.reshape(groups * domains, rows, atoms), ('bead', 'sp...  15.1 us
    all_to_all x1, starting transfers between devices, on_device(): lax.all_to_all(spread.reshape(groups * domains, rows, atoms), ('bead', 's...  7.3 us
    unnamed x18, local copies, waits for them, and re-layouts  3.12 us
    ppermute x3, waiting for transfers between devices, shift(): lax.ppermute(values, 'space', [(i, (i + by) % domains) for i in range(dom...  2.84 us
    ppermute x3, starting transfers between devices, shift(): lax.ppermute(values, 'space', [(i, (i + by) % domains) for i in range(dom...  2.3 us
    pallas_call x1, Pallas kernels, on_device(): pl.pallas_call(functools.partial(prepare_kernel, slots=slots, ghosts=ghos...  1.61 us
  transfers between devices with their start and end apart: 4, of which 2 were waited for; matrix products, arithmetic and copies ran while one was open for 4% of the time, Pallas kernels for 3%

profile of v2, /device:TPU:0, one launch (start us, length us, event | category | flops | bytes accessed | tf_op | source)
XLA Modules:
  0.0 54.2 jit_solution(2750167216305848394)
XLA Ops:
  0.0 0.0 copy-start.1
  0.0 0.0 copy-start
  0.0 0.0 copy-start.2
  0.0 1.0 %copy-done.2 = f32[8,64,24]{2,1,0:T(8,128)S(1)} copy-done((f32[8,64,24]{2,1,0:T(8,128)S(1)}, f32[8,64,24]{2,1,0:T(8,128)}, u32[]{:S(2)}) %copy-start.2) | copy-done | bytes 49176
  1.0 0.0 copy-start.6
  1.0 0.7 %copy-done.6 = f32[8,3,256]{2,0,1:T(8,128)S(1)} copy-done((f32[8,3,256]{2,0,1:T(8,128)S(1)}, f32[8,3,256]{2,0,1:T(8,128)}, u32[]{:S(2)}) %copy-start.6) | copy-done | bytes 24600
  1.7 0.0 copy-start.5
  1.7 0.0 copy-start.8
  1.7 0.9 %shard_map.118 = f32[8,4,8,256]{3,2,1,0:T(8,128)} custom-call(f32[8,64,24]{2,1,0:T(8,128)S(1)} %copy-done.2, f32[3,8,256]{2,1,0:T(8,128)S(1)} %bitcast.11), custom_call_target="tpu_custom_call" | custom-call | tf_op jit(solution)/shard_map/pallas_call | solution.py:468
  2.6 7.3 %all-to-all-start = ((f32[32,8,256]{2,1,0:T(8,128)}), f32[32,8,256]{2,1,0:T(8,128)S(1)}, u32[]{:S(2)}, u32[]{:S(2)}) async-start(f32[32,8,256]{2,1,0:T(8,128)} %bitcast.1), calls=%async_computation | async-start | bytes 524288 | tf_op jit(solution)/shard_map/all_to_all | solution.py:475
  9.9 0.7 %pad.4 = s32[256]{0:T(256)S(1)} pad(s32[128]{0:T(128)} %param.16, s32[]{:T(128)} %constant.2.clone.1), padding=0_128 | pad | bytes 1540 | tf_op jit(solution)/shard_map/jit(_pad)/pad | solution.py:457
  10.6 0.8 %pad_add_fusion.own_ref = s32[35,256]{1,0:T(8,128)S(1)} fusion(s32[1,256]{1,0:T(1,128)S(1)} %bitcast.13, s32[1,256]{1,0:T(1,128)} %bitcast.15, s32[1,256]{1,0:T(1,128)} %bitcast.17, s32[32,256]{1,0:T(8,128)} %param.14), kind=kLoop, calls=%fused_computation | loop fusion | flops 26880 | bytes 71680 | tf_op jit(solution)/shard_map/concatenate | solution.py:458
  11.4 1.5 %collective-permute-start.1 = (s32[35,256]{1,0:T(8,128)S(1)}, s32[35,256]{1,0:T(8,128)S(1)}, u32[]{:S(2)}, u32[]{:S(2)}) collective-permute-start(s32[35,256]{1,0:T(8,128)S(1)} %pad_add_fusion.own_ref), channel_id=1, source_target_pairs={{0,3},{1,0},{2,1},{3,2},{4,7},{5,4},{6,5},{7,6},{8,11},{9,8},{10,9... | collective-permute-start | bytes 107528 | tf_op jit(solution)/shard_map/ppermute | solution.py:461
  13.0 0.0 collective-permute-start
  13.0 0.7 %pad_add_fusion.1 = s32[2,256]{1,0:T(2,128)S(1)} fusion(s32[1,256]{1,0:T(1,128)S(1)} %bitcast.14, s32[1,256]{1,0:T(1,128)} %bitcast.16), kind=kLoop, calls=%fused_computation.1 | loop fusion | flops 512 | bytes 4096 | tf_op jit(solution)/shard_map/stack | solution.py:457
  13.6 0.8 %collective-permute-start.2 = (s32[2,256]{1,0:T(2,128)S(1)}, s32[2,256]{1,0:T(2,128)S(1)}, u32[]{:S(2)}, u32[]{:S(2)}) collective-permute-start(s32[2,256]{1,0:T(2,128)S(1)} %pad_add_fusion.1), channel_id=1, source_target_pairs={{0,2},{1,3},{2,0},{3,1},{4,6},{5,7},{6,4},{7,5},{8,10},{9,11},{10,... | collective-permute-start | bytes 6152 | tf_op jit(solution)/shard_map/ppermute | solution.py:461
  14.4 2.8 %collective-permute-done.2.far_left_ref.far_right_ref = s32[2,256]{1,0:T(2,128)S(1)} collective-permute-done((s32[2,256]{1,0:T(2,128)S(1)}, s32[2,256]{1,0:T(2,128)S(1)}, u32[]{:S(2)}, u32[]{:S(2)}) %collective-permute-start.2) | collective-permute-done | bytes 2080 | tf_op jit(solution)/shard_map/ppermute | solution.py:461
  17.2 0.0 collective-permute-done.1.right_ref
  17.2 0.0 collective-permute-done.left_ref
  17.2 0.0 copy-done.1
  17.2 0.0 copy-done
  17.2 0.0 copy-start.4
  17.3 0.7 %copy-done.4 = f32[2,8,128]{2,1,0:T(8,128)S(1)} copy-done((f32[2,8,128]{2,1,0:T(8,128)S(1)}, f32[2,8,128]{2,1,0:T(8,128)}, u32[]{:S(2)}) %copy-start.4) | copy-done | bytes 8216
  17.9 0.0 copy-start.7
  18.0 0.7 %copy-done.7 = f32[2,128]{1,0:T(2,128)S(1)} copy-done((f32[2,128]{1,0:T(2,128)S(1)}, f32[2,128]{1,0:T(2,128)}, u32[]{:S(2)}) %copy-start.7) | copy-done | bytes 1048
  18.6 1.6 %shard_map.119 = (f32[2,384,384]{2,1,0:T(8,128)S(1)}, f32[128,384]{1,0:T(8,128)S(1)}, f32[128,128]{1,0:T(8,128)S(1)}, f32[128,128]{1,0:T(8,128)S(1)}, f32[128,12...) custom-call(s32[35,256]{1,0:T(8,128)S(1)} %pad_add_fusion.own_ref, ...), custom_call_target="tpu_custom_call" | custom-call | tf_op jit(solution)/shard_map/pallas_call | solution.py:481
  20.2 0.3 all-to-all-done.recv_ref
  20.5 0.0 copy-done.5
  20.5 0.0 copy-done.8
  20.5 0.0 copy-start.3
  20.6 17.7 %shard_map.120 = f32[8,4,8,256]{3,2,1,0:T(8,128)S(1)} custom-call(f32[32,8,256]{2,1,0:T(8,128)S(1)} %all-to-all-done.recv_ref, f32[2,384,384]{2,1,0:T(8,128)S(1)} %get-tuple-element.13.count_ref, f32[128,384]{1,0:T(8,128)S(1)} %get-tuple-element.14.hidden_ref, f32[128,128]{1,0:T(8,128)S(1)} %get-tuple-element.15.first_ref, ...), custom_call_target="tpu_custom_call" | custom-call | tf_op jit(solution)/shard_map/pallas_call | solution.py:498
  38.3 15.1 %all_to_all.10 = f32[32,8,256]{2,1,0:T(8,128)S(1)} all-to-all(f32[32,8,256]{2,1,0:T(8,128)S(1)} %bitcast.9), channel_id=1, replica_groups=mesh['bead'=8,'space'=4] {'bead','space'}, dimensions={0} | all-to-all | bytes 524288 | tf_op jit(solution)/shard_map/all_to_all | solution.py:519
  53.4 0.0 copy-done.3
  53.4 0.8 %shard_map.121 = f32[3,8,256]{2,1,0:T(8,128)} custom-call(f32[8,24,64]{2,1,0:T(8,128)S(1)} %copy-done.3, f32[8,4,8,256]{3,2,1,0:T(8,128)S(1)} %bitcast.10), custom_call_target="tpu_custom_call" | custom-call | tf_op jit(solution)/shard_map/pallas_call | solution.py:522
Async XLA Ops:
  0.0 17.2 %copy-start.1 = (f32[2,128,128]{2,1,0:T(8,128)S(1)}, f32[2,128,128]{2,1,0:T(8,128)}, u32[]{:S(2)}) copy-start(f32[2,128,128]{2,1,0:T(8,128)} %upd_ref.3) | copy-start | bytes 393220
  0.0 17.2 %copy-start = (f32[2,128,128]{2,1,0:T(8,128)S(1)}, f32[2,128,128]{2,1,0:T(8,128)}, u32[]{:S(2)}) copy-start(f32[2,128,128]{2,1,0:T(8,128)} %msg_ref.3) | copy-start | bytes 393220
  0.0 1.0 %copy-start.2 = (f32[8,64,24]{2,1,0:T(8,128)S(1)}, f32[8,64,24]{2,1,0:T(8,128)}, u32[]{:S(2)}) copy-start(f32[8,64,24]{2,1,0:T(8,128)} %constant.6.clone.table_ref) | copy-start | bytes 147460
  1.0 0.7 %copy-start.6 = (f32[8,3,256]{2,0,1:T(8,128)S(1)}, f32[8,3,256]{2,0,1:T(8,128)}, u32[]{:S(2)}) copy-start(f32[8,3,256]{2,0,1:T(8,128)} %param.12) | copy-start | bytes 73732
  1.7 18.8 %copy-start.5 = (f32[2,8,128]{2,1,0:T(8,128)S(1)}, f32[2,8,128]{2,1,0:T(8,128)}, u32[]{:S(2)}) copy-start(f32[2,8,128]{2,1,0:T(8,128)} %radial_ref.3) | copy-start | bytes 24580
  1.7 18.8 %copy-start.8 = (f32[128]{0:T(128)S(1)}, f32[128]{0:T(128)}, u32[]{:S(2)}) copy-start(f32[128]{0:T(128)} %param.21) | copy-start | bytes 1540
  2.6 17.9 %all-to-all-start = ((f32[32,8,256]{2,1,0:T(8,128)}), f32[32,8,256]{2,1,0:T(8,128)S(1)}, u32[]{:S(2)}, u32[]{:S(2)}) async-start(f32[32,8,256]{2,1,0:T(8,128)} %bitcast.1), calls=%async_computation | async-start | bytes 524288 | tf_op jit(solution)/shard_map/all_to_all | solution.py:475
  11.4 5.8 %collective-permute-start.1 = (s32[35,256]{1,0:T(8,128)S(1)}, s32[35,256]{1,0:T(8,128)S(1)}, u32[]{:S(2)}, u32[]{:S(2)}) collective-permute-start(s32[35,256]{1,0:T(8,128)S(1)} %pad_add_fusion.own_ref), channel_id=1, source_target_pairs={{0,3},{1,0},{2,1},{3,2},{4,7},{5,4},{6,5},{7,6},{8,11},{9,8},{10,9... | collective-permute-start | bytes 107528 | tf_op jit(solution)/shard_map/ppermute | solution.py:461
  13.0 4.3 %collective-permute-start = (s32[35,256]{1,0:T(8,128)S(1)}, s32[35,256]{1,0:T(8,128)S(1)}, u32[]{:S(2)}, u32[]{:S(2)}) collective-permute-start(s32[35,256]{1,0:T(8,128)S(1)} %pad_add_fusion.own_ref), channel_id=1, source_target_pairs={{0,1},{1,2},{2,3},{3,0},{4,5},{5,6},{6,7},{7,4},{8,9},{9,10},{10,1... | collective-permute-start | bytes 107528 | tf_op jit(solution)/shard_map/ppermute | solution.py:461
  13.6 3.6 %collective-permute-start.2 = (s32[2,256]{1,0:T(2,128)S(1)}, s32[2,256]{1,0:T(2,128)S(1)}, u32[]{:S(2)}, u32[]{:S(2)}) collective-permute-start(s32[2,256]{1,0:T(2,128)S(1)} %pad_add_fusion.1), channel_id=1, source_target_pairs={{0,2},{1,3},{2,0},{3,1},{4,6},{5,7},{6,4},{7,5},{8,10},{9,11},{10,... | collective-permute-start | bytes 6152 | tf_op jit(solution)/shard_map/ppermute | solution.py:461
  17.2 0.7 %copy-start.4 = (f32[2,8,128]{2,1,0:T(8,128)S(1)}, f32[2,8,128]{2,1,0:T(8,128)}, u32[]{:S(2)}) copy-start(f32[2,8,128]{2,1,0:T(8,128)} %radial_ref.3) | copy-start | bytes 24580
  17.9 0.7 %copy-start.7 = (f32[2,128]{1,0:T(2,128)S(1)}, f32[2,128]{1,0:T(2,128)}, u32[]{:S(2)}) copy-start(f32[2,128]{1,0:T(2,128)} %embed_ref.1) | copy-start | bytes 3076
  20.5 32.9 %copy-start.3 = (f32[8,24,64]{2,1,0:T(8,128)S(1)}, f32[8,24,64]{2,1,0:T(8,128)}, u32[]{:S(2)}) copy-start(f32[8,24,64]{2,1,0:T(8,128)} %constant.7.clone.table_ref) | copy-start | bytes 147460

commit v3 on v2

--- a/solution.py
+++ b/solution.py
@@ -21,7 +21,7 @@
 BLOCK = 64
 F32 = jnp.float32
 BF16 = jnp.bfloat16
-UNROLL = 4
+UNROLL = 24
 VMEM_BYTES = 48 * 1024 * 1024
 kappa = math.sqrt(math.log2(math.e)) / radial_width
 
@@ -53,13 +53,29 @@
     return high, low
 
 
-def spread_kernel(table_ref, pos_ref, out_ref):
+def spread_kernel(pos_ref, out_ref):
     components, full_dev, atoms = pos_ref.shape
     groups, domains, rows, _ = out_ref.shape
-    values = pos_ref[...].reshape(components * full_dev, atoms)
-    total = exact_dot(table_ref[lax.axis_index("bead")], values).reshape(groups, rows, atoms)
-    for domain in range(domains):
-        out_ref[:, domain] = total
+    reduced_dev = PC // groups
+    beads_all = groups * full_dev
+    k = lax.broadcasted_iota(jnp.int32, (PC, full_dev), 0).astype(F32)
+    j = lax.broadcasted_iota(jnp.int32, (PC, full_dev), 1) + lax.axis_index("bead") * full_dev
+    gap = k / PC - j.astype(F32) / beads_all
+    table = jnp.ones_like(gap)
+    for harmonic in range(1, PC // 2 + 1):
+        turn = gap * harmonic
+        wave = jnp.cos((turn - jnp.floor(turn)) * (2.0 * math.pi))
+        table = table + (wave if harmonic == PC // 2 else 2.0 * wave)
+    table = table / beads_all
+    total = exact_dot(table, jnp.concatenate([pos_ref[x] for x in range(components)], axis=1))
+    for group in range(groups):
+        at = slice(group * reduced_dev, (group + 1) * reduced_dev)
+        parts = [total[at, x * atoms : (x + 1) * atoms] for x in range(components)]
+        if rows > 3 * reduced_dev:
+            parts.append(jnp.zeros((rows - 3 * reduced_dev, atoms), F32))
+        block = jnp.concatenate(parts, axis=0)
+        for domain in range(domains):
+            out_ref[group, domain] = block
 
 
 def collect_kernel(table_ref, in_ref, out_ref):
@@ -71,29 +87,58 @@
     out_ref[...] = out.reshape(out_ref.shape)
 
 
-def spread_tables(beads_all, groups, pad_rows):
+def collect_table(beads_all, groups, pad_rows):
     table = contraction(beads_all, PC)
     full_dev, reduced_dev = beads_all // groups, PC // groups
-    out = np.zeros((groups, groups, pad_rows, 3, full_dev), np.float32)
+    out = np.zeros((groups, 3, full_dev, groups, pad_rows), np.float32)
     for own in range(groups):
         for group in range(groups):
             part = table[group * reduced_dev : (group + 1) * reduced_dev, own * full_dev : (own + 1) * full_dev]
             for x in range(3):
-                out[own, group, x * reduced_dev : (x + 1) * reduced_dev, x] = part
-    out = out.reshape(groups, groups * pad_rows, 3 * full_dev)
-    back = -(beads_all / PC) * out.transpose(0, 2, 1)
-    return jnp.asarray(out), jnp.asarray(np.ascontiguousarray(back.astype(np.float32)))
-
-
-def prepare_kernel(
-    own_ref, left_ref, right_ref, far_left_ref, far_right_ref, embed_ref, radial_ref, msg_ref, upd_ref,
-    count_ref, hidden_ref, first_ref, first_t_ref, msg_t_ref, upd_t_ref, fan_ref, fold_ref,
+                out[own, x, :, group, x * reduced_dev : (x + 1) * reduced_dev] = part.T
+    return jnp.asarray(-(beads_all / PC) * out.reshape(groups, 3 * full_dev, groups * pad_rows))
+
+
+def weights_kernel(
+    embed_ref, radial_ref, msg_ref, upd_ref,
+    embed_cols_ref, first_ref, first_t_ref, msg_t_ref, upd_t_ref, fan_ref,
     *, slots, ghosts,
 ):
-    atoms = own_ref.shape[1]
-    extent = atoms + 2 * ghosts
     species_count, channels = embed_ref.shape
     basis_count = radial_ref.shape[1]
+    embed = embed_ref[...]
+    embed_pad = jnp.concatenate([embed, jnp.zeros((8 - species_count, channels), F32)], axis=0)
+    embed_cols_ref[...] = embed_pad.T
+    scale = slots ** (-0.5)
+    lent = exact_dot(embed_pad, msg_ref[0])
+    stacked = []
+    for b in range(basis_count):
+        for s in range(species_count):
+            row = radial_ref[0, b : b + 1] * lent[s : s + 1] * scale
+            stacked.append(jnp.broadcast_to(row, (8, channels)))
+    first = exact_dot(jnp.concatenate(stacked, axis=0), upd_ref[0])
+    first_ref[...] = first
+    first_t_ref[...] = first.T
+    msg_t_ref[...] = msg_ref[1].T
+    upd_t_ref[...] = upd_ref[1].T
+
+    row = lax.broadcasted_iota(jnp.int32, fan_ref.shape, 0)
+    column = lax.broadcasted_iota(jnp.int32, fan_ref.shape, 1)
+    part = lax.rem(column, 2 * LANES)
+    part = (part >= LANES).astype(jnp.int32) + (part >= LANES + ghosts).astype(jnp.int32)
+    pad_rows = fan_ref.shape[0] // 9
+    fan_ref[...] = jnp.where(
+        lax.rem(row, 3 * pad_rows) == part * pad_rows + lax.div(column, 2 * LANES), 1.0, 0.0
+    ).astype(BF16)
+
+
+def counts_kernel(
+    own_ref, left_ref, right_ref, far_left_ref, far_right_ref, embed_cols_ref, count_ref, hidden_ref, *, slots, ghosts
+):
+    atoms = own_ref.shape[1]
+    channels = embed_cols_ref.shape[0]
+    species_count = count_ref.shape[0]
+    extent = atoms + 2 * ghosts
     tail = atoms - ghosts
     count_row, species_row, send_row = slots, slots + 1, slots + 2
 
@@ -108,8 +153,8 @@
     own_send = own_ref[send_row : send_row + 1]
     left_send = left_ref[send_row : send_row + 1]
     right_send = right_ref[send_row : send_row + 1]
-    far_left_send = far_left_ref[1:2]
-    far_right_send = far_right_ref[1:2]
+    far_left_send = far_left_ref[send_row : send_row + 1]
+    far_right_send = far_right_ref[send_row : send_row + 1]
 
     def ghost_map(from_left, from_right):
         return jnp.concatenate(
@@ -128,8 +173,8 @@
     species_rows = []
     for near, lower, upper in (
         (own_ref[species_row : species_row + 1], left_ref[species_row : species_row + 1], right_ref[species_row : species_row + 1]),
-        (left_ref[species_row : species_row + 1], far_left_ref[0:1], own_ref[species_row : species_row + 1]),
-        (right_ref[species_row : species_row + 1], own_ref[species_row : species_row + 1], far_right_ref[0:1]),
+        (left_ref[species_row : species_row + 1], far_left_ref[species_row : species_row + 1], own_ref[species_row : species_row + 1]),
+        (right_ref[species_row : species_row + 1], own_ref[species_row : species_row + 1], far_right_ref[species_row : species_row + 1]),
     ):
         species_rows.append(jnp.concatenate([near, lower[:, tail:], upper[:, :ghosts]], axis=1))
     species_f = jnp.concatenate(species_rows + [species_rows[0]] * 5, axis=0).astype(F32)
@@ -171,47 +216,16 @@
             for s in range(species_count):
                 count_ref[s, rows, lanes] = jnp.where(kind == float(s), tally, 0.0)
 
-    embed = embed_ref[...]
-    embed_pad = jnp.concatenate([embed, jnp.zeros((8 - species_count, channels), F32)], axis=0)
-    embed_cols = embed_pad.T
     hidden = jnp.zeros((channels, extent), F32)
     for s in range(species_count):
-        hidden = hidden + embed_cols[:, s : s + 1] * (species_f[0:1] == float(s)).astype(F32)
+        hidden = hidden + embed_cols_ref[:, s : s + 1] * (species_f[0:1] == float(s)).astype(F32)
     hidden_ref[...] = hidden
 
-    scale = slots ** (-0.5)
-    lent = exact_dot(embed_pad, msg_ref[0])
-    stacked = []
-    for b in range(basis_count):
-        for s in range(species_count):
-            row = radial_ref[0, b : b + 1] * lent[s : s + 1] * scale
-            stacked.append(jnp.broadcast_to(row, (8, channels)))
-    first = exact_dot(jnp.concatenate(stacked, axis=0), upd_ref[0])
-    first_ref[...] = first
-    first_t_ref[...] = first.T
-    msg_t_ref[...] = msg_ref[1].T
-    upd_t_ref[...] = upd_ref[1].T
-
-    row = lax.broadcasted_iota(jnp.int32, fan_ref.shape, 0)
-    column = lax.broadcasted_iota(jnp.int32, fan_ref.shape, 1)
-    part = lax.rem(column, 2 * LANES)
-    part = (part >= LANES).astype(jnp.int32) + (part >= LANES + ghosts).astype(jnp.int32)
-    pad_rows = fan_ref.shape[0] // 9
-    fan_ref[...] = jnp.where(
-        lax.rem(row, 3 * pad_rows) == part * pad_rows + lax.div(column, 2 * LANES), 1.0, 0.0
-    ).astype(BF16)
-    row = lax.broadcasted_iota(jnp.int32, fold_ref.shape, 0)
-    column = lax.broadcasted_iota(jnp.int32, fold_ref.shape, 1)
-    part = jnp.where(
-        lax.rem(row, 4 * LANES) < 2 * LANES, 0, jnp.where(lax.rem(row, LANES) < ghosts, 1, 2)
-    )
-    fold_ref[...] = jnp.where(column == part * pad_rows + lax.div(row, 4 * LANES), 1.0, 0.0).astype(BF16)
-
 
 def force_kernel(
-    recv_ref, count_ref, hidden_ref, first_ref, first_t_ref, msg_t_ref, upd_t_ref, fan_ref, fold_ref, radial_ref, msg_ref, upd_ref, out_w_ref,
+    recv_ref, count_ref, hidden_ref, first_ref, first_t_ref, msg_t_ref, upd_t_ref, fan_ref, radial_ref, msg_ref, upd_ref, out_w_ref,
     out_ref,
-    near_ref, reach_ref, inverse_ref, high_ref, low_ref, sums_ref, edge_ref, slope_pair_ref, slope_ref, row_h_ref, wide_ref,
+    near_ref, inverse_ref, high_ref, low_ref, sums_ref, edge_ref, slope_pair_ref, slope_ref, row_h_ref, wide_ref, wave_ref,
     *, domains, slots, ghosts, reduced_dev,
 ):
     groups = recv_ref.shape[0] // domains
@@ -274,13 +288,13 @@
                 inverse = lax.rsqrt(square)
                 reach = square * inverse * kappa
                 inverse_ref[bead, at, lanes] = inverse
-                reach_ref[bead, at, lanes] = reach
                 tallies = [count_ref[s, at, lanes] for s in range(species_count)]
                 tally = functools.reduce(jnp.add, tallies)
                 sums = list(sums)
                 for b in range(basis_count):
                     offset = reach - centers[b]
                     value = jnp.exp2(-(offset * offset))
+                    wave_ref[bead, b, at, lanes] = value * offset
                     for s in range(species_count):
                         term = tallies[s] * value
                         sums[b * species_count + s] = sums[b * species_count + s] + (term[:8] + term[8:])
@@ -342,6 +356,8 @@
             slope_pair_ref[bead, b] = fast_dot(jnp.concatenate([high, low, high], axis=1), grads)
 
     pulls = []
+    edge_ref[...] = jnp.zeros_like(edge_ref)
+    lane_row = lax.broadcasted_iota(jnp.int32, (BLOCK, LANES), 1)
     chain = -2.0 / (radial_width * math.sqrt(math.log2(math.e)))
     for bead in beads:
         for own in (True, False):
@@ -352,12 +368,10 @@
 
             def pair_grads(step, center, bead=bead, lanes=lanes, own=own, width=width, here=here, start=start):
                 at = pl.ds(pl.multiple_of(step * BLOCK, BLOCK), BLOCK)
-                reach = reach_ref[bead, at, lanes]
                 tallies = [count_ref[s, at, lanes] for s in range(species_count)]
                 total = jnp.zeros((BLOCK, width), F32)
                 for b in range(basis_count):
-                    offset = reach - centers[b]
-                    value = jnp.exp2(-(offset * offset)) * offset
+                    value = wave_ref[bead, b, at, lanes]
 
                     def first_layer(s):
                         n = (b * species_count + s) * 8
@@ -372,6 +386,7 @@
                     total = total + slope * value
                 weight = total * functools.reduce(jnp.add, tallies) * inverse_ref[bead, at, lanes] * chain
                 center = list(center)
+                columns = jnp.zeros((BLOCK, LANES), F32)
                 for x in range(3):
                     q = x * reduced_dev + bead
                     place = near(own, q, at)
@@ -383,15 +398,19 @@
                         n = x * (width // LANES) + chunk
                         for part in range(BLOCK // 8):
                             center[n] = center[n] + pull[part * 8 : part * 8 + 8]
-                    high, low = halves(folded)
-                    start_q = (2 * q + (0 if own else 1)) * 2 * LANES
-                    edge_ref[at, start_q : start_q + LANES] = high
-                    edge_ref[at, start_q + LANES : start_q + 2 * LANES] = low
+                    if own:
+                        columns = jnp.where(lane_row == q, jnp.sum(folded, axis=1, keepdims=True), columns)
+                    else:
+                        left = jnp.sum(jnp.where(lane_row < ghosts, folded, 0.0), axis=1, keepdims=True)
+                        right = jnp.sum(jnp.where(lane_row < ghosts, 0.0, folded), axis=1, keepdims=True)
+                        columns = jnp.where(lane_row == pad_rows + q, left, columns)
+                        columns = jnp.where(lane_row == 2 * pad_rows + q, right, columns)
+                edge_ref[at, :] = edge_ref[at, :] + columns
                 return tuple(center)
 
             zero = jnp.zeros((8, LANES), F32)
             many = width // LANES
-            center = lax.fori_loop(0, extent // BLOCK, pair_grads, (zero,) * (3 * many))
+            center = lax.fori_loop(0, extent // BLOCK, pair_grads, (zero,) * (3 * many), unroll=extent // BLOCK)
             pulls.append(
                 [
                     jnp.concatenate(
@@ -401,7 +420,7 @@
                 ]
             )
 
-    edges = fast_dot(edge_ref[...], fold_ref[...]).T
+    edges = edge_ref[...].T
     edge_own, edge_left, edge_right = (edges[pad_rows * n : pad_rows * (n + 1)] for n in range(3))
     center = [
         jnp.concatenate([pulls[2 * bead][x], pulls[2 * bead + 1][x]], axis=1) for x in range(3) for bead in beads
@@ -447,74 +466,79 @@
     extent = atoms + 2 * ghosts
     species_count, channels = embed.shape
     layers, basis_count, _ = w_radial.shape
-    table, back_table = spread_tables(beads_all, groups, rows)
+    back_table = collect_table(beads_all, groups, rows)
     vmem = pl.BlockSpec(memory_space=pltpu.VMEM)
     params = pltpu.CompilerParams(vmem_limit_bytes=VMEM_BYTES)
 
     def shaped(*shape):
         return jax.ShapeDtypeStruct(shape, F32)
 
-    last = jnp.stack([species, jnp.pad(send_rows, (0, atoms - 2 * ghosts))])
-    pack = jnp.concatenate([neighbors, counts[None], last], axis=0)
+    sends = jnp.pad(send_rows, (0, atoms - 2 * ghosts))
+    pack = jnp.concatenate([neighbors, counts[None], species[None], sends[None]], axis=0)
 
     def shift(values, by):
         return lax.ppermute(values, "space", [(i, (i + by) % domains) for i in range(domains)])
 
     from_left = shift(pack, 1)
     from_right = shift(pack, -1)
-    from_far_left = shift(last, 2)
-    from_far_right = from_far_left if domains == 4 else shift(last, -2)
+    from_far_left = shift(pack, 2)
+    from_far_right = from_far_left if domains == 4 else shift(pack, -2)
 
     spread = pl.pallas_call(
         spread_kernel,
         out_shape=shaped(groups, domains, rows, atoms),
-        in_specs=[vmem, vmem],
+        in_specs=[vmem],
         out_specs=vmem,
         compiler_params=params,
-    )(table, positions.transpose(1, 0, 2))
+    )(positions.transpose(1, 0, 2))
     arrived = lax.all_to_all(
         spread.reshape(groups * domains, rows, atoms), ("bead", "space"), 0, 0, tiled=True
     )
 
     sums_rows = basis_count * species_count * 8
     lane_count = 2 * LANES * 3 * reduced_dev
-    prepared = pl.pallas_call(
-        functools.partial(prepare_kernel, slots=slots, ghosts=ghosts),
+    embed_cols, *weights = pl.pallas_call(
+        functools.partial(weights_kernel, slots=slots, ghosts=ghosts),
         out_shape=[
-            shaped(species_count, extent, extent),
-            shaped(channels, extent),
+            shaped(channels, 8),
             shaped(sums_rows, channels),
             shaped(channels, sums_rows),
             shaped(channels, channels),
             shaped(channels, channels),
             jax.ShapeDtypeStruct((9 * rows, lane_count), BF16),
-            jax.ShapeDtypeStruct((2 * lane_count, LANES), BF16),
         ],
-        in_specs=[vmem] * 9,
-        out_specs=[vmem] * 8,
+        in_specs=[vmem] * 4,
+        out_specs=[vmem] * 6,
         compiler_params=params,
-    )(pack, from_left, from_right, from_far_left, from_far_right, embed, w_radial, w_msg, w_upd)
+    )(embed, w_radial, w_msg, w_upd)
+    prepared = pl.pallas_call(
+        functools.partial(counts_kernel, slots=slots, ghosts=ghosts),
+        out_shape=[shaped(species_count, extent, extent), shaped(channels, extent)],
+        in_specs=[vmem] * 6,
+        out_specs=[vmem] * 2,
+        compiler_params=params,
+    )(pack, from_left, from_right, from_far_left, from_far_right, embed_cols)
 
     grads = pl.pallas_call(
         functools.partial(force_kernel, domains=domains, slots=slots, ghosts=ghosts, reduced_dev=reduced_dev),
         out_shape=shaped(groups, domains, rows, atoms),
-        in_specs=[vmem] * 13,
+        in_specs=[vmem] * 12,
         out_specs=vmem,
         scratch_shapes=[
             pltpu.VMEM((extent, lane_count), F32),
             pltpu.VMEM((reduced_dev, extent, extent), F32),
-            pltpu.VMEM((reduced_dev, extent, extent), F32),
             pltpu.VMEM((reduced_dev, basis_count, extent, atoms), BF16),
             pltpu.VMEM((reduced_dev, basis_count, extent, atoms), BF16),
             pltpu.VMEM((sums_rows, reduced_dev * extent), F32),
-            pltpu.VMEM((extent, 2 * lane_count), BF16),
+            pltpu.VMEM((extent, LANES), F32),
             pltpu.VMEM((reduced_dev, basis_count, extent, atoms), F32),
             pltpu.VMEM((channels, reduced_dev * extent), F32),
             pltpu.VMEM((sums_rows, reduced_dev * extent), F32),
             pltpu.VMEM((2 * channels, basis_count * extent), BF16),
+            pltpu.VMEM((reduced_dev, basis_count, extent, extent), F32),
         ],
         compiler_params=params,
-    )(arrived, *prepared, w_radial, w_msg, w_upd, w_out[None])
+    )(arrived, *prepared, *weights, w_radial, w_msg, w_upd, w_out[None])
 
     returned = lax.all_to_all(
         grads.reshape(groups * domains, rows, atoms), ("bead", "space"), 0, 0, tiled=True

time: 54.6 us -> 47.9 us (0.88)
  Pallas kernels: 21 us -> 16.6 us
  blocking collectives: 15.1 us -> 13.8 us
  waiting for transfers between devices: 3.14 us -> 1.93 us
  local copies, waits for them, and re-layouts: 3.78 us -> 4.64 us
  other arithmetic: 1.49 us -> 0.8 us
    pallas_call x1, Pallas kernels: 17.7 us -> 13 us  [on_device(): pl.pallas_call(functools.partial(force_kernel, domains=domains, slots=slo...]
    ppermute x3, waiting for transfers between devices: 2.84 us -> 0.01 us  [shift(): lax.ppermute(values, 'space', [(i, (i + by) % domains) for i in range(dom...]
    all_to_all x1, waiting for transfers between devices: 0.3 us -> 1.92 us  [on_device(): lax.all_to_all(spread.reshape(groups * domains, rows, atoms), ('bead', 's...]
    all_to_all x1, blocking collectives: 15.1 us -> 13.8 us  [on_device(): lax.all_to_all(grads.reshape(groups * domains, rows, atoms), ('bead', 'sp...]
    unnamed x18 -> x20, local copies, waits for them, and re-layouts: 3.12 us -> 3.98 us
    another operation x1 -> x0, other arithmetic: 0.69 us -> none  [on_device(): last = jnp.stack([species, jnp.pad(send_rows, (0, atoms - 2 * ghosts))])]
    pallas_call x1 -> x2, Pallas kernels: 1.61 us -> 1.67 us  [the longest x1 1.11 us: on_device(): pl.pallas_call(functools.partial(counts_kernel, slots=slots, ghosts=ghost...]
  transfers between devices with their start and end apart: 4 -> 4, of which waited for: 2 -> 1; matrix products, arithmetic and copies ran while one was open for 4% -> 3% of each run, Pallas kernels for 3% -> 4%
where the time goes in v3:
time: 47.9 us; the launch traced here: 47.5 us
  Pallas kernels  16.6 us (35%)
  blocking collectives  13.8 us (29%)
  starting transfers between devices  9.61 us (20%)
  local copies, waits for them, and re-layouts  4.64 us (10%)
  waiting for transfers between devices  1.93 us (4%)
  other arithmetic  0.8 us (2%)
    all_to_all x1, blocking collectives, on_device(): lax.all_to_all(grads.reshape(groups * domains, rows, atoms), ('bead', 'sp...  13.8 us
    pallas_call x1, Pallas kernels, on_device(): pl.pallas_call(functools.partial(force_kernel, domains=domains, slots=slo...  13 us
    all_to_all x1, starting transfers between devices, on_device(): lax.all_to_all(spread.reshape(groups * domains, rows, atoms), ('bead', 's...  7.3 us
    unnamed x20, local copies, waits for them, and re-layouts  3.98 us
    ppermute x3, starting transfers between devices, shift(): lax.ppermute(values, 'space', [(i, (i + by) % domains) for i in range(dom...  2.31 us
    all_to_all x1, waiting for transfers between devices, on_device(): lax.all_to_all(spread.reshape(groups * domains, rows, atoms), ('bead', 's...  1.92 us
    pallas_call x1, Pallas kernels, on_device(): pl.pallas_call(spread_kernel, out_shape=shaped(groups, domains, rows, ato...  1.14 us
    pallas_call x1, Pallas kernels, on_device(): pl.pallas_call(functools.partial(counts_kernel, slots=slots, ghosts=ghost...  1.11 us
  transfers between devices with their start and end apart: 4, of which 1 were waited for; matrix products, arithmetic and copies ran while one was open for 3% of the time, Pallas kernels for 4%

profile of v3, /device:TPU:0, one launch (start us, length us, event | category | flops | bytes accessed | tf_op | source)
XLA Modules:
  0.0 47.5 jit_solution(14495569014014999360)
XLA Ops:
  0.0 0.0 copy-start.3
  0.0 0.0 copy-start.1
  0.0 0.0 copy-start.6
  0.0 0.0 copy-start.7
  0.0 0.8 %copy-done.7 = f32[8,3,256]{2,0,1:T(8,128)S(1)} copy-done((f32[8,3,256]{2,0,1:T(8,128)S(1)}, f32[8,3,256]{2,0,1:T(8,128)}, u32[]{:S(2)}) %copy-start.7) | copy-done | bytes 24600
  0.8 0.0 copy-start.9
  0.8 1.1 %shard_map.109 = f32[8,4,8,256]{3,2,1,0:T(8,128)} custom-call(f32[3,8,256]{2,1,0:T(8,128)S(1)} %bitcast.11), custom_call_target="tpu_custom_call" | custom-call | tf_op jit(solution)/shard_map/pallas_call | solution.py:487
  1.9 7.3 %all-to-all-start = ((f32[32,8,256]{2,1,0:T(8,128)}), f32[32,8,256]{2,1,0:T(8,128)S(1)}, u32[]{:S(2)}, u32[]{:S(2)}) async-start(f32[32,8,256]{2,1,0:T(8,128)} %bitcast.1), calls=%async_computation | async-start | bytes 524288 | tf_op jit(solution)/shard_map/all_to_all | solution.py:494
  9.2 0.7 %pad.4 = s32[256]{0:T(256)S(1)} pad(s32[128]{0:T(128)} %param.15, s32[]{:T(128)} %constant.1.clone.1), padding=0_128 | pad | bytes 1540 | tf_op jit(solution)/shard_map/jit(_pad)/pad | solution.py:476
  9.9 0.8 %pad_add_fusion.own_ref = s32[35,256]{1,0:T(8,128)S(1)} fusion(s32[1,256]{1,0:T(1,128)S(1)} %bitcast.13, s32[1,256]{1,0:T(1,128)} %bitcast.14, s32[1,256]{1,0:T(1,128)} %bitcast.15, s32[32,256]{1,0:T(8,128)} %param.13), kind=kLoop, calls=%fused_computation | loop fusion | flops 26880 | bytes 71680 | tf_op jit(solution)/shard_map/concatenate | solution.py:477
  10.7 1.8 %collective-permute-start.2 = (s32[35,256]{1,0:T(8,128)S(1)}, s32[35,256]{1,0:T(8,128)S(1)}, u32[]{:S(2)}, u32[]{:S(2)}) collective-permute-start(s32[35,256]{1,0:T(8,128)S(1)} %pad_add_fusion.own_ref), channel_id=1, source_target_pairs={{0,2},{1,3},{2,0},{3,1},{4,6},{5,7},{6,4},{7,5},{8,10},{9,11},{10,... | collective-permute-start | bytes 107528 | tf_op jit(solution)/shard_map/ppermute | solution.py:480
  12.5 0.0 collective-permute-start.1
  12.5 0.5 %collective-permute-start = (s32[35,256]{1,0:T(8,128)S(1)}, s32[35,256]{1,0:T(8,128)S(1)}, u32[]{:S(2)}, u32[]{:S(2)}) collective-permute-start(s32[35,256]{1,0:T(8,128)S(1)} %pad_add_fusion.own_ref), channel_id=1, source_target_pairs={{0,1},{1,2},{2,3},{3,0},{4,5},{5,6},{6,7},{7,4},{8,9},{9,10},{10,1... | collective-permute-start | bytes 107528 | tf_op jit(solution)/shard_map/ppermute | solution.py:480
  13.0 0.0 copy-start
  13.0 0.9 %copy-done = f32[2,128,128]{2,1,0:T(8,128)S(1)} copy-done((f32[2,128,128]{2,1,0:T(8,128)S(1)}, f32[2,128,128]{2,1,0:T(8,128)}, u32[]{:S(2)}) %copy-start) | copy-done | bytes 131096
  13.9 0.0 copy-start.2
  13.9 0.9 %copy-done.2 = f32[2,128,128]{2,1,0:T(8,128)S(1)} copy-done((f32[2,128,128]{2,1,0:T(8,128)S(1)}, f32[2,128,128]{2,1,0:T(8,128)}, u32[]{:S(2)}) %copy-start.2) | copy-done | bytes 131096
  14.8 0.0 copy-start.5
  14.8 0.7 %copy-done.5 = f32[2,8,128]{2,1,0:T(8,128)S(1)} copy-done((f32[2,8,128]{2,1,0:T(8,128)S(1)}, f32[2,8,128]{2,1,0:T(8,128)}, u32[]{:S(2)}) %copy-start.5) | copy-done | bytes 8216
  15.5 0.0 copy-start.8
  15.5 0.7 %copy-done.8 = f32[2,128]{1,0:T(2,128)S(1)} copy-done((f32[2,128]{1,0:T(2,128)S(1)}, f32[2,128]{1,0:T(2,128)}, u32[]{:S(2)}) %copy-start.8) | copy-done | bytes 1048
  16.2 0.6 %shard_map.110 = (f32[128,8]{1,0:T(8,128)S(1)}, f32[128,128]{1,0:T(8,128)S(1)}, f32[128,128]{1,0:T(8,128)S(1)}, f32[128,128]{1,0:T(8,128)S(1)}, f32[128,128]{1,0:T(8,128)S(1)}, /*index=5*/bf16[72,1536]{1,0:T(8,128)(2,1)S(1)}) custom-call(f32[2,128]{1,0:T(2,128)S(1)} %copy-done.8, f32[2,8,128]{2,1,0:T(8,128)S(1)} %copy-done.5, f32[2,128,128]{2,1,0:T(8,128)S(1)} %copy-done, ...), custom_call_target="tpu_custom_call" | custom-call | tf_op jit(solution)/shard_map/pallas_call | solution.py:500
  16.8 0.0 collective-permute-done.2.far_left_ref.far_right_ref
  16.8 0.0 collective-permute-done.1.right_ref
  16.8 0.0 collective-permute-done.left_ref
  16.8 1.1 %shard_map.111 = (f32[2,384,384]{2,1,0:T(8,128)S(1)}, f32[128,384]{1,0:T(8,128)S(1)}) custom-call(s32[35,256]{1,0:T(8,128)S(1)} %pad_add_fusion.own_ref, s32[35,256]{1,0:T(8,128)S(1)} %collective-permute-done.left_ref, s32[35,256]{1,0:T(8,128)S(1)} %collective-permute-done.1.right_ref, s32[35,256]{1,0:T(8,128)S(1)} %collective-permute-done.2.far_left_ref.far_right_ref, ...), custom_call_target="tpu_custom_call" | custom-call | tf_op jit(solution)/shard_map/pallas_call | solution.py:514
  17.9 1.9 %all-to-all-done.recv_ref = f32[32,8,256]{2,1,0:T(8,128)S(1)} async-done(((f32[32,8,256]{2,1,0:T(8,128)}), f32[32,8,256]{2,1,0:T(8,128)S(1)}, u32[]{:S(2)}, u32[]{:S(2)}) %all-to-all-start) | async-done | bytes 262176 | tf_op jit(solution)/shard_map/all_to_all | solution.py:494
  19.8 0.0 copy-done.3
  19.8 0.0 copy-done.1
  19.8 0.0 copy-done.6
  19.8 0.0 copy-done.9
  19.9 0.0 copy-start.4
  19.9 13.0 %shard_map.112 = f32[8,4,8,256]{3,2,1,0:T(8,128)S(1)} custom-call(f32[32,8,256]{2,1,0:T(8,128)S(1)} %all-to-all-done.recv_ref, f32[2,384,384]{2,1,0:T(8,128)S(1)} %get-tuple-element.14.count_ref, f32[128,384]{1,0:T(8,128)S(1)} %get-tuple-element.15.hidden_ref, f32[128,128]{1,0:T(8,128)S(1)} %get-tuple-element.16.first_ref, ...), custom_call_target="tpu_custom_call" | custom-call | tf_op jit(solution)/shard_map/pallas_call | solution.py:522
  32.9 13.8 %all_to_all.10 = f32[32,8,256]{2,1,0:T(8,128)S(1)} all-to-all(f32[32,8,256]{2,1,0:T(8,128)S(1)} %bitcast.9), channel_id=1, replica_groups=mesh['bead'=8,'space'=4] {'bead','space'}, dimensions={0} | all-to-all | bytes 524288 | tf_op jit(solution)/shard_map/all_to_all | solution.py:543
  46.8 0.0 copy-done.4
  46.8 0.8 %shard_map.113 = f32[3,8,256]{2,1,0:T(8,128)} custom-call(f32[8,24,64]{2,1,0:T(8,128)S(1)} %copy-done.4, f32[8,4,8,256]{3,2,1,0:T(8,128)S(1)} %bitcast.10), custom_call_target="tpu_custom_call" | custom-call | tf_op jit(solution)/shard_map/pallas_call | solution.py:546
Async XLA Ops:
  0.0 19.8 %copy-start.3 = (f32[2,128,128]{2,1,0:T(8,128)S(1)}, f32[2,128,128]{2,1,0:T(8,128)}, u32[]{:S(2)}) copy-start(f32[2,128,128]{2,1,0:T(8,128)} %upd_ref.3) | copy-start | bytes 393220
  0.0 19.8 %copy-start.1 = (f32[2,128,128]{2,1,0:T(8,128)S(1)}, f32[2,128,128]{2,1,0:T(8,128)}, u32[]{:S(2)}) copy-start(f32[2,128,128]{2,1,0:T(8,128)} %msg_ref.3) | copy-start | bytes 393220
  0.0 19.8 %copy-start.6 = (f32[2,8,128]{2,1,0:T(8,128)S(1)}, f32[2,8,128]{2,1,0:T(8,128)}, u32[]{:S(2)}) copy-start(f32[2,8,128]{2,1,0:T(8,128)} %radial_ref.3) | copy-start | bytes 24580
  0.0 0.8 %copy-start.7 = (f32[8,3,256]{2,0,1:T(8,128)S(1)}, f32[8,3,256]{2,0,1:T(8,128)}, u32[]{:S(2)}) copy-start(f32[8,3,256]{2,0,1:T(8,128)} %param.11) | copy-start | bytes 73732
  0.8 19.1 %copy-start.9 = (f32[128]{0:T(128)S(1)}, f32[128]{0:T(128)}, u32[]{:S(2)}) copy-start(f32[128]{0:T(128)} %param.20) | copy-start | bytes 1540
  1.9 17.9 %all-to-all-start = ((f32[32,8,256]{2,1,0:T(8,128)}), f32[32,8,256]{2,1,0:T(8,128)S(1)}, u32[]{:S(2)}, u32[]{:S(2)}) async-start(f32[32,8,256]{2,1,0:T(8,128)} %bitcast.1), calls=%async_computation | async-start | bytes 524288 | tf_op jit(solution)/shard_map/all_to_all | solution.py:494
  10.7 6.1 %collective-permute-start.2 = (s32[35,256]{1,0:T(8,128)S(1)}, s32[35,256]{1,0:T(8,128)S(1)}, u32[]{:S(2)}, u32[]{:S(2)}) collective-permute-start(s32[35,256]{1,0:T(8,128)S(1)} %pad_add_fusion.own_ref), channel_id=1, source_target_pairs={{0,2},{1,3},{2,0},{3,1},{4,6},{5,7},{6,4},{7,5},{8,10},{9,11},{10,... | collective-permute-start | bytes 107528 | tf_op jit(solution)/shard_map/ppermute | solution.py:480
  12.5 4.3 %collective-permute-start.1 = (s32[35,256]{1,0:T(8,128)S(1)}, s32[35,256]{1,0:T(8,128)S(1)}, u32[]{:S(2)}, u32[]{:S(2)}) collective-permute-start(s32[35,256]{1,0:T(8,128)S(1)} %pad_add_fusion.own_ref), channel_id=1, source_target_pairs={{0,3},{1,0},{2,1},{3,2},{4,7},{5,4},{6,5},{7,6},{8,11},{9,8},{10,9... | collective-permute-start | bytes 107528 | tf_op jit(solution)/shard_map/ppermute | solution.py:480
  12.5 4.3 %collective-permute-start = (s32[35,256]{1,0:T(8,128)S(1)}, s32[35,256]{1,0:T(8,128)S(1)}, u32[]{:S(2)}, u32[]{:S(2)}) collective-permute-start(s32[35,256]{1,0:T(8,128)S(1)} %pad_add_fusion.own_ref), channel_id=1, source_target_pairs={{0,1},{1,2},{2,3},{3,0},{4,5},{5,6},{6,7},{7,4},{8,9},{9,10},{10,1... | collective-permute-start | bytes 107528 | tf_op jit(solution)/shard_map/ppermute | solution.py:480
  13.0 0.9 %copy-start = (f32[2,128,128]{2,1,0:T(8,128)S(1)}, f32[2,128,128]{2,1,0:T(8,128)}, u32[]{:S(2)}) copy-start(f32[2,128,128]{2,1,0:T(8,128)} %msg_ref.3) | copy-start | bytes 393220
  13.9 0.9 %copy-start.2 = (f32[2,128,128]{2,1,0:T(8,128)S(1)}, f32[2,128,128]{2,1,0:T(8,128)}, u32[]{:S(2)}) copy-start(f32[2,128,128]{2,1,0:T(8,128)} %upd_ref.3) | copy-start | bytes 393220
  14.8 0.7 %copy-start.5 = (f32[2,8,128]{2,1,0:T(8,128)S(1)}, f32[2,8,128]{2,1,0:T(8,128)}, u32[]{:S(2)}) copy-start(f32[2,8,128]{2,1,0:T(8,128)} %radial_ref.3) | copy-start | bytes 24580
  15.5 0.7 %copy-start.8 = (f32[2,128]{1,0:T(2,128)S(1)}, f32[2,128]{1,0:T(2,128)}, u32[]{:S(2)}) copy-start(f32[2,128]{1,0:T(2,128)} %embed_ref.1) | copy-start | bytes 3076
  19.9 26.9 %copy-start.4 = (f32[8,24,64]{2,1,0:T(8,128)S(1)}, f32[8,24,64]{2,1,0:T(8,128)}, u32[]{:S(2)}) copy-start(f32[8,24,64]{2,1,0:T(8,128)} %constant.4.clone.table_ref) | copy-start | bytes 147460

commit v4 on v3

--- a/solution.py
+++ b/solution.py
@@ -55,8 +55,7 @@
 
 def spread_kernel(pos_ref, out_ref):
     components, full_dev, atoms = pos_ref.shape
-    groups, domains, rows, _ = out_ref.shape
-    reduced_dev = PC // groups
+    groups, domains, reduced_dev, _ = out_ref.shape
     beads_all = groups * full_dev
     k = lax.broadcasted_iota(jnp.int32, (PC, full_dev), 0).astype(F32)
     j = lax.broadcasted_iota(jnp.int32, (PC, full_dev), 1) + lax.axis_index("bead") * full_dev
@@ -69,34 +68,28 @@
     table = table / beads_all
     total = exact_dot(table, jnp.concatenate([pos_ref[x] for x in range(components)], axis=1))
     for group in range(groups):
-        at = slice(group * reduced_dev, (group + 1) * reduced_dev)
-        parts = [total[at, x * atoms : (x + 1) * atoms] for x in range(components)]
-        if rows > 3 * reduced_dev:
-            parts.append(jnp.zeros((rows - 3 * reduced_dev, atoms), F32))
-        block = jnp.concatenate(parts, axis=0)
+        block = total[group * reduced_dev : (group + 1) * reduced_dev]
         for domain in range(domains):
             out_ref[group, domain] = block
 
 
 def collect_kernel(table_ref, in_ref, out_ref):
-    groups, domains, rows, atoms = in_ref.shape
-    total = in_ref[:, 0]
-    for domain in range(1, domains):
-        total = total + in_ref[:, domain]
-    out = exact_dot(table_ref[lax.axis_index("bead")], total.reshape(groups * rows, atoms))
-    out_ref[...] = out.reshape(out_ref.shape)
-
-
-def collect_table(beads_all, groups, pad_rows):
-    table = contraction(beads_all, PC)
-    full_dev, reduced_dev = beads_all // groups, PC // groups
-    out = np.zeros((groups, 3, full_dev, groups, pad_rows), np.float32)
-    for own in range(groups):
-        for group in range(groups):
-            part = table[group * reduced_dev : (group + 1) * reduced_dev, own * full_dev : (own + 1) * full_dev]
-            for x in range(3):
-                out[own, x, :, group, x * reduced_dev : (x + 1) * reduced_dev] = part.T
-    return jnp.asarray(-(beads_all / PC) * out.reshape(groups, 3 * full_dev, groups * pad_rows))
+    groups, domains = in_ref.shape[:2]
+    atoms = out_ref.shape[2]
+    pulls = []
+    for group in range(groups):
+        total = in_ref[group, 0]
+        for domain in range(1, domains):
+            total = total + in_ref[group, domain]
+        pulls.append(total)
+    out = exact_dot(table_ref[lax.axis_index("bead")], jnp.concatenate(pulls, axis=0))
+    for x in range(out_ref.shape[0]):
+        out_ref[x] = out[:, x * atoms : (x + 1) * atoms]
+
+
+def collect_table(beads_all, groups):
+    table = contraction(beads_all, PC).T.reshape(groups, beads_all // groups, PC)
+    return jnp.asarray(-(beads_all / PC) * table)
 
 
 def weights_kernel(
@@ -229,8 +222,9 @@
     *, domains, slots, ghosts, reduced_dev,
 ):
     groups = recv_ref.shape[0] // domains
-    pad_rows, atoms = recv_ref.shape[1:]
     rows = reduced_dev * 3
+    pad_rows = -(-rows // 8) * 8
+    atoms = recv_ref.shape[2] // 3
     extent = atoms + 2 * ghosts
     tail = atoms - ghosts
     species_count = count_ref.shape[0]
@@ -251,6 +245,10 @@
         total = recv_ref[place]
         for group in range(1, groups):
             total = total + recv_ref[group * domains + place]
+        total = [total[:, x * atoms : (x + 1) * atoms] for x in range(3)]
+        if rows < pad_rows:
+            total.append(jnp.zeros((pad_rows - rows, atoms), F32))
+        total = jnp.concatenate(total, axis=0)
         segment[step] = total + jnp.where(is_first, wraps, 0.0)
 
     def extended(step):
@@ -447,7 +445,8 @@
     out_ref[0] = jnp.zeros_like(out_ref[0])
     for step, values in back.items():
         place = lax.rem(domain + step + 2 * domains, domains)
-        out_ref[0, place] = out_ref[0, place] + values
+        flat = [values[x * reduced_dev : (x + 1) * reduced_dev] for x in range(3)]
+        out_ref[0, place] = out_ref[0, place] + jnp.concatenate(flat, axis=1)
     for group in range(1, groups):
         out_ref[group] = out_ref[0]
 
@@ -466,7 +465,7 @@
     extent = atoms + 2 * ghosts
     species_count, channels = embed.shape
     layers, basis_count, _ = w_radial.shape
-    back_table = collect_table(beads_all, groups, rows)
+    back_table = collect_table(beads_all, groups)
     vmem = pl.BlockSpec(memory_space=pltpu.VMEM)
     params = pltpu.CompilerParams(vmem_limit_bytes=VMEM_BYTES)
 
@@ -486,13 +485,13 @@
 
     spread = pl.pallas_call(
         spread_kernel,
-        out_shape=shaped(groups, domains, rows, atoms),
+        out_shape=shaped(groups, domains, reduced_dev, 3 * atoms),
         in_specs=[vmem],
         out_specs=vmem,
         compiler_params=params,
     )(positions.transpose(1, 0, 2))
     arrived = lax.all_to_all(
-        spread.reshape(groups * domains, rows, atoms), ("bead", "space"), 0, 0, tiled=True
+        spread.reshape(groups * domains, reduced_dev, 3 * atoms), ("bead", "space"), 0, 0, tiled=True
     )
 
     sums_rows = basis_count * species_count * 8
@@ -521,7 +520,7 @@
 
     grads = pl.pallas_call(
         functools.partial(force_kernel, domains=domains, slots=slots, ghosts=ghosts, reduced_dev=reduced_dev),
-        out_shape=shaped(groups, domains, rows, atoms),
+        out_shape=shaped(groups, domains, reduced_dev, 3 * atoms),
         in_specs=[vmem] * 12,
         out_specs=vmem,
         scratch_shapes=[
@@ -541,7 +540,7 @@
     )(arrived, *prepared, *weights, w_radial, w_msg, w_upd, w_out[None])
 
     returned = lax.all_to_all(
-        grads.reshape(groups * domains, rows, atoms), ("bead", "space"), 0, 0, tiled=True
+        grads.reshape(groups * domains, reduced_dev, 3 * atoms), ("bead", "space"), 0, 0, tiled=True
     )
     forces = pl.pallas_call(
         collect_kernel,
@@ -549,7 +548,7 @@
         in_specs=[vmem, vmem],
         out_specs=vmem,
         compiler_params=params,
-    )(back_table, returned.reshape(groups, domains, rows, atoms))
+    )(back_table, returned.reshape(groups, domains, reduced_dev, 3 * atoms))
     return forces.transpose(1, 0, 2)
 
 

time: 47.9 us -> 46.9 us (0.979)
  waiting for transfers between devices: 1.93 us -> 0.01 us
  starting transfers between devices: 9.61 us -> 10.9 us
  blocking collectives: 13.8 us -> 13.3 us
    all_to_all x1, waiting for transfers between devices: 1.92 us -> 0.01 us  [on_device(): lax.all_to_all(spread.reshape(groups * domains, reduced_dev, 3 * atoms),...]
    ppermute x3, starting transfers between devices: 2.31 us -> 3.55 us  [shift(): lax.ppermute(values, 'space', [(i, (i + by) % domains) for i in range(dom...]
    all_to_all x1, blocking collectives: 13.8 us -> 13.3 us  [on_device(): lax.all_to_all(grads.reshape(groups * domains, reduced_dev, 3 * atoms), (...]
  transfers between devices with their start and end apart: 4 -> 4, of which waited for: 1 -> 0; matrix products, arithmetic and copies ran while one was open for 3% -> 3% of each run, Pallas kernels for 4% -> 4%
where the time goes in v4:
time: 46.9 us; the launch traced here: 46.3 us
  Pallas kernels  16.6 us (35%)
  blocking collectives  13.3 us (28%)
  starting transfers between devices  10.9 us (23%)
  local copies, waits for them, and re-layouts  4.65 us (10%)
  other arithmetic  0.8 us (2%)
    all_to_all x1, blocking collectives, on_device(): lax.all_to_all(grads.reshape(groups * domains, reduced_dev, 3 * atoms), (...  13.3 us
    pallas_call x1, Pallas kernels, on_device(): pl.pallas_call(functools.partial(force_kernel, domains=domains, slots=slo...  13 us
    all_to_all x1, starting transfers between devices, on_device(): lax.all_to_all(spread.reshape(groups * domains, reduced_dev, 3 * atoms),...  7.3 us
    unnamed x20, local copies, waits for them, and re-layouts  3.98 us
    ppermute x3, starting transfers between devices, shift(): lax.ppermute(values, 'space', [(i, (i + by) % domains) for i in range(dom...  3.55 us
    pallas_call x1, Pallas kernels, on_device(): pl.pallas_call(spread_kernel, out_shape=shaped(groups, domains, reduced_d...  1.12 us
    pallas_call x1, Pallas kernels, on_device(): pl.pallas_call(functools.partial(counts_kernel, slots=slots, ghosts=ghost...  1.11 us
  transfers between devices with their start and end apart: 4, of which 0 were waited for; matrix products, arithmetic and copies ran while one was open for 3% of the time, Pallas kernels for 4%

profile of v4, /device:TPU:0, one launch (start us, length us, event | category | flops | bytes accessed | tf_op | source)
XLA Modules:
  0.0 46.3 jit_solution(13744638037156658733)
XLA Ops:
  0.0 0.0 copy-start.5
  0.0 0.0 copy-start.1
  0.0 0.0 copy-start.3
  0.0 0.0 copy-start.7
  0.0 0.8 %copy-done.7 = f32[8,3,256]{2,0,1:T(8,128)S(1)} copy-done((f32[8,3,256]{2,0,1:T(8,128)S(1)}, f32[8,3,256]{2,0,1:T(8,128)}, u32[]{:S(2)}) %copy-start.7) | copy-done | bytes 24600
  0.8 0.0 copy-start.9
  0.8 1.1 %shard_map.109 = f32[8,4,2,768]{3,2,1,0:T(2,128)} custom-call(f32[3,8,256]{2,1,0:T(8,128)S(1)} %bitcast.11), custom_call_target="tpu_custom_call" | custom-call | tf_op jit(solution)/shard_map/pallas_call | solution.py:486
  1.9 7.3 %all-to-all-start = ((f32[32,2,768]{2,1,0:T(2,128)}), f32[32,2,768]{2,1,0:T(2,128)S(1)}, u32[]{:S(2)}, u32[]{:S(2)}) async-start(f32[32,2,768]{2,1,0:T(2,128)} %bitcast.1), calls=%async_computation | async-start | bytes 393216 | tf_op jit(solution)/shard_map/all_to_all | solution.py:493
  9.2 0.7 %pad.4 = s32[256]{0:T(256)S(1)} pad(s32[128]{0:T(128)} %param.15, s32[]{:T(128)} %constant.1.clone.1), padding=0_128 | pad | bytes 1540 | tf_op jit(solution)/shard_map/jit(_pad)/pad | solution.py:475
  9.9 0.8 %pad_add_fusion.own_ref = s32[35,256]{1,0:T(8,128)S(1)} fusion(s32[1,256]{1,0:T(1,128)S(1)} %bitcast.13, s32[1,256]{1,0:T(1,128)} %bitcast.14, s32[1,256]{1,0:T(1,128)} %bitcast.15, s32[32,256]{1,0:T(8,128)} %param.13), kind=kLoop, calls=%fused_computation | loop fusion | flops 26880 | bytes 71680 | tf_op jit(solution)/shard_map/concatenate | solution.py:476
  10.7 0.3 collective-permute-start
  11.0 1.5 %collective-permute-start.1 = (s32[35,256]{1,0:T(8,128)S(1)}, s32[35,256]{1,0:T(8,128)S(1)}, u32[]{:S(2)}, u32[]{:S(2)}) collective-permute-start(s32[35,256]{1,0:T(8,128)S(1)} %pad_add_fusion.own_ref), channel_id=1, source_target_pairs={{0,3},{1,0},{2,1},{3,2},{4,7},{5,4},{6,5},{7,6},{8,11},{9,8},{10,9... | collective-permute-start | bytes 107528 | tf_op jit(solution)/shard_map/ppermute | solution.py:479
  12.4 1.8 %collective-permute-start.2 = (s32[35,256]{1,0:T(8,128)S(1)}, s32[35,256]{1,0:T(8,128)S(1)}, u32[]{:S(2)}, u32[]{:S(2)}) collective-permute-start(s32[35,256]{1,0:T(8,128)S(1)} %pad_add_fusion.own_ref), channel_id=1, source_target_pairs={{0,2},{1,3},{2,0},{3,1},{4,6},{5,7},{6,4},{7,5},{8,10},{9,11},{10,... | collective-permute-start | bytes 107528 | tf_op jit(solution)/shard_map/ppermute | solution.py:479
  14.2 0.0 copy-start
  14.2 0.9 %copy-done = f32[2,128,128]{2,1,0:T(8,128)S(1)} copy-done((f32[2,128,128]{2,1,0:T(8,128)S(1)}, f32[2,128,128]{2,1,0:T(8,128)}, u32[]{:S(2)}) %copy-start) | copy-done | bytes 131096
  15.1 0.0 copy-start.2
  15.1 0.9 %copy-done.2 = f32[2,128,128]{2,1,0:T(8,128)S(1)} copy-done((f32[2,128,128]{2,1,0:T(8,128)S(1)}, f32[2,128,128]{2,1,0:T(8,128)}, u32[]{:S(2)}) %copy-start.2) | copy-done | bytes 131096
  16.0 0.0 copy-start.4
  16.0 0.7 %copy-done.4 = f32[2,8,128]{2,1,0:T(8,128)S(1)} copy-done((f32[2,8,128]{2,1,0:T(8,128)S(1)}, f32[2,8,128]{2,1,0:T(8,128)}, u32[]{:S(2)}) %copy-start.4) | copy-done | bytes 8216
  16.7 0.0 copy-start.8
  16.7 0.7 %copy-done.8 = f32[2,128]{1,0:T(2,128)S(1)} copy-done((f32[2,128]{1,0:T(2,128)S(1)}, f32[2,128]{1,0:T(2,128)}, u32[]{:S(2)}) %copy-start.8) | copy-done | bytes 1048
  17.4 0.6 %shard_map.110 = (f32[128,8]{1,0:T(8,128)S(1)}, f32[128,128]{1,0:T(8,128)S(1)}, f32[128,128]{1,0:T(8,128)S(1)}, f32[128,128]{1,0:T(8,128)S(1)}, f32[128,128]{1,0:T(8,128)S(1)}, /*index=5*/bf16[72,1536]{1,0:T(8,128)(2,1)S(1)}) custom-call(f32[2,128]{1,0:T(2,128)S(1)} %copy-done.8, f32[2,8,128]{2,1,0:T(8,128)S(1)} %copy-done.4, f32[2,128,128]{2,1,0:T(8,128)S(1)} %copy-done, ...), custom_call_target="tpu_custom_call" | custom-call | tf_op jit(solution)/shard_map/pallas_call | solution.py:499
  18.0 0.0 collective-permute-done.left_ref
  18.0 0.0 collective-permute-done.1.right_ref
  18.0 0.0 collective-permute-done.2.far_left_ref.far_right_ref
  18.0 1.1 %shard_map.111 = (f32[2,384,384]{2,1,0:T(8,128)S(1)}, f32[128,384]{1,0:T(8,128)S(1)}) custom-call(s32[35,256]{1,0:T(8,128)S(1)} %pad_add_fusion.own_ref, s32[35,256]{1,0:T(8,128)S(1)} %collective-permute-done.left_ref, s32[35,256]{1,0:T(8,128)S(1)} %collective-permute-done.1.right_ref, s32[35,256]{1,0:T(8,128)S(1)} %collective-permute-done.2.far_left_ref.far_right_ref, ...), custom_call_target="tpu_custom_call" | custom-call | tf_op jit(solution)/shard_map/pallas_call | solution.py:513
  19.1 0.0 all-to-all-done.recv_ref
  19.1 0.0 copy-done.5
  19.2 0.0 copy-done.1
  19.2 0.0 copy-done.3
  19.2 0.0 copy-done.9
  19.2 0.0 copy-start.6
  19.2 13.0 %shard_map.112 = f32[8,4,2,768]{3,2,1,0:T(2,128)S(1)} custom-call(f32[32,2,768]{2,1,0:T(2,128)S(1)} %all-to-all-done.recv_ref, f32[2,384,384]{2,1,0:T(8,128)S(1)} %get-tuple-element.14.count_ref, f32[128,384]{1,0:T(8,128)S(1)} %get-tuple-element.15.hidden_ref, f32[128,128]{1,0:T(8,128)S(1)} %get-tuple-element.16.first_ref, ...), custom_call_target="tpu_custom_call" | custom-call | tf_op jit(solution)/shard_map/pallas_call | solution.py:521
  32.2 13.3 %all_to_all.10 = f32[32,2,768]{2,1,0:T(2,128)S(1)} all-to-all(f32[32,2,768]{2,1,0:T(2,128)S(1)} %bitcast.10), channel_id=1, replica_groups=mesh['bead'=8,'space'=4] {'bead','space'}, dimensions={0} | all-to-all | bytes 393216 | tf_op jit(solution)/shard_map/all_to_all | solution.py:542
  45.6 0.0 copy-done.6
  45.6 0.8 %shard_map.113 = f32[3,8,256]{2,1,0:T(8,128)} custom-call(f32[8,8,16]{2,1,0:T(8,128)S(1)} %copy-done.6, f32[8,4,2,768]{3,2,1,0:T(2,128)S(1)} %bitcast.9), custom_call_target="tpu_custom_call" | custom-call | tf_op jit(solution)/shard_map/pallas_call | solution.py:545
Async XLA Ops:
  0.0 19.1 %copy-start.5 = (f32[2,8,128]{2,1,0:T(8,128)S(1)}, f32[2,8,128]{2,1,0:T(8,128)}, u32[]{:S(2)}) copy-start(f32[2,8,128]{2,1,0:T(8,128)} %radial_ref.3) | copy-start | bytes 24580
  0.0 19.2 %copy-start.1 = (f32[2,128,128]{2,1,0:T(8,128)S(1)}, f32[2,128,128]{2,1,0:T(8,128)}, u32[]{:S(2)}) copy-start(f32[2,128,128]{2,1,0:T(8,128)} %msg_ref.3) | copy-start | bytes 393220
  0.0 19.2 %copy-start.3 = (f32[2,128,128]{2,1,0:T(8,128)S(1)}, f32[2,128,128]{2,1,0:T(8,128)}, u32[]{:S(2)}) copy-start(f32[2,128,128]{2,1,0:T(8,128)} %upd_ref.3) | copy-start | bytes 393220
  0.0 0.8 %copy-start.7 = (f32[8,3,256]{2,0,1:T(8,128)S(1)}, f32[8,3,256]{2,0,1:T(8,128)}, u32[]{:S(2)}) copy-start(f32[8,3,256]{2,0,1:T(8,128)} %param.11) | copy-start | bytes 73732
  0.8 18.4 %copy-start.9 = (f32[128]{0:T(128)S(1)}, f32[128]{0:T(128)}, u32[]{:S(2)}) copy-start(f32[128]{0:T(128)} %param.20) | copy-start | bytes 1540
  1.9 17.2 %all-to-all-start = ((f32[32,2,768]{2,1,0:T(2,128)}), f32[32,2,768]{2,1,0:T(2,128)S(1)}, u32[]{:S(2)}, u32[]{:S(2)}) async-start(f32[32,2,768]{2,1,0:T(2,128)} %bitcast.1), calls=%async_computation | async-start | bytes 393216 | tf_op jit(solution)/shard_map/all_to_all | solution.py:493
  10.7 7.3 %collective-permute-start = (s32[35,256]{1,0:T(8,128)S(1)}, s32[35,256]{1,0:T(8,128)S(1)}, u32[]{:S(2)}, u32[]{:S(2)}) collective-permute-start(s32[35,256]{1,0:T(8,128)S(1)} %pad_add_fusion.own_ref), channel_id=1, source_target_pairs={{0,1},{1,2},{2,3},{3,0},{4,5},{5,6},{6,7},{7,4},{8,9},{9,10},{10,1... | collective-permute-start | bytes 107528 | tf_op jit(solution)/shard_map/ppermute | solution.py:479
  11.0 7.0 %collective-permute-start.1 = (s32[35,256]{1,0:T(8,128)S(1)}, s32[35,256]{1,0:T(8,128)S(1)}, u32[]{:S(2)}, u32[]{:S(2)}) collective-permute-start(s32[35,256]{1,0:T(8,128)S(1)} %pad_add_fusion.own_ref), channel_id=1, source_target_pairs={{0,3},{1,0},{2,1},{3,2},{4,7},{5,4},{6,5},{7,6},{8,11},{9,8},{10,9... | collective-permute-start | bytes 107528 | tf_op jit(solution)/shard_map/ppermute | solution.py:479
  12.4 5.6 %collective-permute-start.2 = (s32[35,256]{1,0:T(8,128)S(1)}, s32[35,256]{1,0:T(8,128)S(1)}, u32[]{:S(2)}, u32[]{:S(2)}) collective-permute-start(s32[35,256]{1,0:T(8,128)S(1)} %pad_add_fusion.own_ref), channel_id=1, source_target_pairs={{0,2},{1,3},{2,0},{3,1},{4,6},{5,7},{6,4},{7,5},{8,10},{9,11},{10,... | collective-permute-start | bytes 107528 | tf_op jit(solution)/shard_map/ppermute | solution.py:479
  14.2 0.9 %copy-start = (f32[2,128,128]{2,1,0:T(8,128)S(1)}, f32[2,128,128]{2,1,0:T(8,128)}, u32[]{:S(2)}) copy-start(f32[2,128,128]{2,1,0:T(8,128)} %msg_ref.3) | copy-start | bytes 393220
  15.1 0.9 %copy-start.2 = (f32[2,128,128]{2,1,0:T(8,128)S(1)}, f32[2,128,128]{2,1,0:T(8,128)}, u32[]{:S(2)}) copy-start(f32[2,128,128]{2,1,0:T(8,128)} %upd_ref.3) | copy-start | bytes 393220
  16.0 0.7 %copy-start.4 = (f32[2,8,128]{2,1,0:T(8,128)S(1)}, f32[2,8,128]{2,1,0:T(8,128)}, u32[]{:S(2)}) copy-start(f32[2,8,128]{2,1,0:T(8,128)} %radial_ref.3) | copy-start | bytes 24580
  16.7 0.7 %copy-start.8 = (f32[2,128]{1,0:T(2,128)S(1)}, f32[2,128]{1,0:T(2,128)}, u32[]{:S(2)}) copy-start(f32[2,128]{1,0:T(2,128)} %embed_ref.1) | copy-start | bytes 3076
  19.2 26.4 %copy-start.6 = (f32[8,8,16]{2,1,0:T(8,128)S(1)}, f32[8,8,16]{2,1,0:T(8,128)}, u32[]{:S(2)}) copy-start(f32[8,8,16]{2,1,0:T(8,128)} %constant.4.clone.table_ref) | copy-start | bytes 12292

commit v5 on v4

--- a/solution.py
+++ b/solution.py
@@ -94,7 +94,7 @@
 
 def weights_kernel(
     embed_ref, radial_ref, msg_ref, upd_ref,
-    embed_cols_ref, first_ref, first_t_ref, msg_t_ref, upd_t_ref, fan_ref,
+    embed_cols_ref, first_ref, first_t_ref, msg_t_ref, upd_t_ref, fan_ref, last_radial_ref, last_msg_ref, last_upd_ref,
     *, slots, ghosts,
 ):
     species_count, channels = embed_ref.shape
@@ -114,6 +114,9 @@
     first_t_ref[...] = first.T
     msg_t_ref[...] = msg_ref[1].T
     upd_t_ref[...] = upd_ref[1].T
+    last_radial_ref[...] = radial_ref[1]
+    last_msg_ref[...] = msg_ref[1]
+    last_upd_ref[...] = upd_ref[1]
 
     row = lax.broadcasted_iota(jnp.int32, fan_ref.shape, 0)
     column = lax.broadcasted_iota(jnp.int32, fan_ref.shape, 1)
@@ -228,7 +231,7 @@
     extent = atoms + 2 * ghosts
     tail = atoms - ghosts
     species_count = count_ref.shape[0]
-    basis_count, channels = radial_ref.shape[1:]
+    basis_count, channels = radial_ref.shape
     own_chunks = atoms // LANES
     chunks = extent // LANES
     beads = range(reduced_dev)
@@ -314,7 +317,7 @@
     hidden = jnp.concatenate([hidden_ref[...]] * reduced_dev, axis=1) + update * sigmoid
     lent_t = near_dot(msg_t_ref[...], hidden)
     lent = lent_t.T
-    radial_cols = radial_ref[1].T * scale
+    radial_cols = radial_ref[...].T * scale
     messages = []
     for bead in beads:
         for b in range(basis_count):
@@ -329,18 +332,18 @@
     sigmoid = jax.nn.sigmoid(update)
     out_cols = jnp.broadcast_to(out_w_ref[...], (8, channels)).T[:, 0:1]
     grad_update = out_cols * (sigmoid * (1.0 + update * (1.0 - sigmoid)))
-    grad_message_t = near_dot(upd_ref[1], grad_update)
+    grad_message_t = near_dot(upd_ref[...], grad_update)
     grad_message = grad_message_t.T
 
     grads_lent = []
     for bead in beads:
         grad_lent = jnp.zeros((extent, channels), F32)
         for b in range(basis_count):
-            high, low = halves(grad_message[bead * atoms : (bead + 1) * atoms] * (radial_ref[1, b : b + 1] * scale))
+            high, low = halves(grad_message[bead * atoms : (bead + 1) * atoms] * (radial_ref[b : b + 1] * scale))
             both = fast_dot(high_ref[bead, b], jnp.concatenate([high, low], axis=1))
             grad_lent = grad_lent + both[:, :channels] + both[:, channels:] + fast_dot(low_ref[bead, b], high)
         grads_lent.append(grad_lent)
-    grad_hidden = near_dot(msg_ref[1], jnp.concatenate(grads_lent, axis=0).T)
+    grad_hidden = near_dot(msg_ref[...], jnp.concatenate(grads_lent, axis=0).T)
     parts = []
     for bead in beads:
         start = bead * extent
@@ -350,7 +353,7 @@
         high, low = halves(grad_message_t[:, bead * atoms : (bead + 1) * atoms])
         grads = jnp.concatenate([high, high, low], axis=0)
         for b in range(basis_count):
-            high, low = halves(lent[bead * extent : (bead + 1) * extent] * (radial_ref[1, b : b + 1] * scale))
+            high, low = halves(lent[bead * extent : (bead + 1) * extent] * (radial_ref[b : b + 1] * scale))
             slope_pair_ref[bead, b] = fast_dot(jnp.concatenate([high, low, high], axis=1), grads)
 
     pulls = []
@@ -505,9 +508,12 @@
             shaped(channels, channels),
             shaped(channels, channels),
             jax.ShapeDtypeStruct((9 * rows, lane_count), BF16),
+            shaped(basis_count, channels),
+            shaped(channels, channels),
+            shaped(channels, channels),
         ],
         in_specs=[vmem] * 4,
-        out_specs=[vmem] * 6,
+        out_specs=[vmem] * 9,
         compiler_params=params,
     )(embed, w_radial, w_msg, w_upd)
     prepared = pl.pallas_call(
@@ -537,7 +543,7 @@
             pltpu.VMEM((reduced_dev, basis_count, extent, extent), F32),
         ],
         compiler_params=params,
-    )(arrived, *prepared, *weights, w_radial, w_msg, w_upd, w_out[None])
+    )(arrived, *prepared, *weights, w_out[None])
 
     returned = lax.all_to_all(
         grads.reshape(groups * domains, reduced_dev, 3 * atoms), ("bead", "space"), 0, 0, tiled=True

time: 46.9 us -> 46.8 us (level)
    unnamed x20 -> x14, local copies, waits for them, and re-layouts: 3.98 us -> 3.94 us
where the time goes in v5:
time: 46.8 us; the launch traced here: 46.3 us
  Pallas kernels  16.6 us (35%)
  blocking collectives  13.3 us (28%)
  starting transfers between devices  10.8 us (23%)
  local copies, waits for them, and re-layouts  4.6 us (10%)
  other arithmetic  0.8 us (2%)
    all_to_all x1, blocking collectives, on_device(): lax.all_to_all(grads.reshape(groups * domains, reduced_dev, 3 * atoms), (...  13.3 us
    pallas_call x1, Pallas kernels, on_device(): pl.pallas_call(functools.partial(force_kernel, domains=domains, slots=slo...  13 us
    all_to_all x1, starting transfers between devices, on_device(): lax.all_to_all(spread.reshape(groups * domains, reduced_dev, 3 * atoms),...  7.3 us
    unnamed x14, local copies, waits for them, and re-layouts  3.94 us
    ppermute x3, starting transfers between devices, shift(): lax.ppermute(values, 'space', [(i, (i + by) % domains) for i in range(dom...  3.55 us
    pallas_call x1, Pallas kernels, on_device(): pl.pallas_call(spread_kernel, out_shape=shaped(groups, domains, reduced_d...  1.12 us
    pallas_call x1, Pallas kernels, on_device(): pl.pallas_call(functools.partial(counts_kernel, slots=slots, ghosts=ghost...  1.11 us
  transfers between devices with their start and end apart: 4, of which 0 were waited for; matrix products, arithmetic and copies ran while one was open for 3% of the time, Pallas kernels for 4%

profile of v5, /device:TPU:0, one launch (start us, length us, event | category | flops | bytes accessed | tf_op | source)
XLA Modules:
  0.0 46.3 jit_solution(8809721666787625092)
XLA Ops:
  0.0 0.0 copy-start.6
  0.0 0.0 copy-start.3
  0.0 0.7 %copy-done.3 = f32[8,3,256]{2,0,1:T(8,128)S(1)} copy-done((f32[8,3,256]{2,0,1:T(8,128)S(1)}, f32[8,3,256]{2,0,1:T(8,128)}, u32[]{:S(2)}) %copy-start.3) | copy-done | bytes 24600
  0.8 1.1 %shard_map.109 = f32[8,4,2,768]{3,2,1,0:T(2,128)} custom-call(f32[3,8,256]{2,1,0:T(8,128)S(1)} %bitcast.11), custom_call_target="tpu_custom_call" | custom-call | tf_op jit(solution)/shard_map/pallas_call | solution.py:489
  1.9 7.3 %all-to-all-start = ((f32[32,2,768]{2,1,0:T(2,128)}), f32[32,2,768]{2,1,0:T(2,128)S(1)}, u32[]{:S(2)}, u32[]{:S(2)}) async-start(f32[32,2,768]{2,1,0:T(2,128)} %bitcast.1), calls=%async_computation | async-start | bytes 393216 | tf_op jit(solution)/shard_map/all_to_all | solution.py:496
  9.2 0.7 %pad.4 = s32[256]{0:T(256)S(1)} pad(s32[128]{0:T(128)} %param.15, s32[]{:T(128)} %constant.1.clone.1), padding=0_128 | pad | bytes 1540 | tf_op jit(solution)/shard_map/jit(_pad)/pad | solution.py:478
  9.8 0.8 %pad_add_fusion.own_ref = s32[35,256]{1,0:T(8,128)S(1)} fusion(s32[1,256]{1,0:T(1,128)S(1)} %bitcast.13, s32[1,256]{1,0:T(1,128)} %bitcast.14, s32[1,256]{1,0:T(1,128)} %bitcast.15, s32[32,256]{1,0:T(8,128)} %param.13), kind=kLoop, calls=%fused_computation | loop fusion | flops 26880 | bytes 71680 | tf_op jit(solution)/shard_map/concatenate | solution.py:479
  10.6 0.3 collective-permute-start
  10.9 1.5 %collective-permute-start.1 = (s32[35,256]{1,0:T(8,128)S(1)}, s32[35,256]{1,0:T(8,128)S(1)}, u32[]{:S(2)}, u32[]{:S(2)}) collective-permute-start(s32[35,256]{1,0:T(8,128)S(1)} %pad_add_fusion.own_ref), channel_id=1, source_target_pairs={{0,3},{1,0},{2,1},{3,2},{4,7},{5,4},{6,5},{7,6},{8,11},{9,8},{10,9... | collective-permute-start | bytes 107528 | tf_op jit(solution)/shard_map/ppermute | solution.py:482
  12.4 1.8 %collective-permute-start.2 = (s32[35,256]{1,0:T(8,128)S(1)}, s32[35,256]{1,0:T(8,128)S(1)}, u32[]{:S(2)}, u32[]{:S(2)}) collective-permute-start(s32[35,256]{1,0:T(8,128)S(1)} %pad_add_fusion.own_ref), channel_id=1, source_target_pairs={{0,2},{1,3},{2,0},{3,1},{4,6},{5,7},{6,4},{7,5},{8,10},{9,11},{10,... | collective-permute-start | bytes 107528 | tf_op jit(solution)/shard_map/ppermute | solution.py:482
  14.2 0.0 copy-start
  14.2 0.9 %copy-done = f32[2,128,128]{2,1,0:T(8,128)S(1)} copy-done((f32[2,128,128]{2,1,0:T(8,128)S(1)}, f32[2,128,128]{2,1,0:T(8,128)}, u32[]{:S(2)}) %copy-start) | copy-done | bytes 131096
  15.1 0.0 copy-start.1
  15.1 0.9 %copy-done.1 = f32[2,128,128]{2,1,0:T(8,128)S(1)} copy-done((f32[2,128,128]{2,1,0:T(8,128)S(1)}, f32[2,128,128]{2,1,0:T(8,128)}, u32[]{:S(2)}) %copy-start.1) | copy-done | bytes 131096
  16.0 0.0 copy-start.4
  16.0 0.7 %copy-done.4 = f32[2,8,128]{2,1,0:T(8,128)S(1)} copy-done((f32[2,8,128]{2,1,0:T(8,128)S(1)}, f32[2,8,128]{2,1,0:T(8,128)}, u32[]{:S(2)}) %copy-start.4) | copy-done | bytes 8216
  16.7 0.0 copy-start.5
  16.7 0.7 %copy-done.5 = f32[2,128]{1,0:T(2,128)S(1)} copy-done((f32[2,128]{1,0:T(2,128)S(1)}, f32[2,128]{1,0:T(2,128)}, u32[]{:S(2)}) %copy-start.5) | copy-done | bytes 1048
  17.4 0.6 %shard_map.110 = (f32[128,8]{1,0:T(8,128)S(1)}, f32[128,128]{1,0:T(8,128)S(1)}, f32[128,128]{1,0:T(8,128)S(1)}, f32[128,128]{1,0:T(8,128)S(1)}, f32[128,128]{1,0...) custom-call(f32[2,128]{1,0:T(2,128)S(1)} %copy-done.5, ...), custom_call_target="tpu_custom_call" | custom-call | tf_op jit(solution)/shard_map/pallas_call | solution.py:502
  17.9 0.0 collective-permute-done.left_ref
  18.0 0.0 collective-permute-done.1.right_ref
  18.0 0.0 collective-permute-done.2.far_left_ref.far_right_ref
  18.0 1.1 %shard_map.111 = (f32[2,384,384]{2,1,0:T(8,128)S(1)}, f32[128,384]{1,0:T(8,128)S(1)}) custom-call(s32[35,256]{1,0:T(8,128)S(1)} %pad_add_fusion.own_ref, s32[35,256]{1,0:T(8,128)S(1)} %collective-permute-done.left_ref, s32[35,256]{1,0:T(8,128)S(1)} %collective-permute-done.1.right_ref, s32[35,256]{1,0:T(8,128)S(1)} %collective-permute-done.2.far_left_ref.far_right_ref, ...), custom_call_target="tpu_custom_call" | custom-call | tf_op jit(solution)/shard_map/pallas_call | solution.py:519
  19.1 0.0 all-to-all-done.recv_ref
  19.1 0.0 copy-done.6
  19.1 0.0 copy-start.2
  19.1 13.0 %shard_map.112 = f32[8,4,2,768]{3,2,1,0:T(2,128)S(1)} custom-call(f32[32,2,768]{2,1,0:T(2,128)S(1)} %all-to-all-done.recv_ref, f32[2,384,384]{2,1,0:T(8,128)S(1)} %get-tuple-element.17.count_ref, f32[128,384]{1,0:T(8,128)S(1)} %get-tuple-element.18.hidden_ref, f32[128,128]{1,0:T(8,128)S(1)} %get-tuple-element.19.first_ref, ...), custom_call_target="tpu_custom_call" | custom-call | tf_op jit(solution)/shard_map/pallas_call | solution.py:527
  32.2 13.3 %all_to_all.10 = f32[32,2,768]{2,1,0:T(2,128)S(1)} all-to-all(f32[32,2,768]{2,1,0:T(2,128)S(1)} %bitcast.10), channel_id=1, replica_groups=mesh['bead'=8,'space'=4] {'bead','space'}, dimensions={0} | all-to-all | bytes 393216 | tf_op jit(solution)/shard_map/all_to_all | solution.py:548
  45.5 0.0 copy-done.2
  45.5 0.8 %shard_map.113 = f32[3,8,256]{2,1,0:T(8,128)} custom-call(f32[8,8,16]{2,1,0:T(8,128)S(1)} %copy-done.2, f32[8,4,2,768]{3,2,1,0:T(2,128)S(1)} %bitcast.9), custom_call_target="tpu_custom_call" | custom-call | tf_op jit(solution)/shard_map/pallas_call | solution.py:551
Async XLA Ops:
  0.0 19.1 %copy-start.6 = (f32[128]{0:T(128)S(1)}, f32[128]{0:T(128)}, u32[]{:S(2)}) copy-start(f32[128]{0:T(128)} %param.20) | copy-start | bytes 1540
  0.0 0.8 %copy-start.3 = (f32[8,3,256]{2,0,1:T(8,128)S(1)}, f32[8,3,256]{2,0,1:T(8,128)}, u32[]{:S(2)}) copy-start(f32[8,3,256]{2,0,1:T(8,128)} %param.11) | copy-start | bytes 73732
  1.9 17.2 %all-to-all-start = ((f32[32,2,768]{2,1,0:T(2,128)}), f32[32,2,768]{2,1,0:T(2,128)S(1)}, u32[]{:S(2)}, u32[]{:S(2)}) async-start(f32[32,2,768]{2,1,0:T(2,128)} %bitcast.1), calls=%async_computation | async-start | bytes 393216 | tf_op jit(solution)/shard_map/all_to_all | solution.py:496
  10.6 7.3 %collective-permute-start = (s32[35,256]{1,0:T(8,128)S(1)}, s32[35,256]{1,0:T(8,128)S(1)}, u32[]{:S(2)}, u32[]{:S(2)}) collective-permute-start(s32[35,256]{1,0:T(8,128)S(1)} %pad_add_fusion.own_ref), channel_id=1, source_target_pairs={{0,1},{1,2},{2,3},{3,0},{4,5},{5,6},{6,7},{7,4},{8,9},{9,10},{10,1... | collective-permute-start | bytes 107528 | tf_op jit(solution)/shard_map/ppermute | solution.py:482
  10.9 7.0 %collective-permute-start.1 = (s32[35,256]{1,0:T(8,128)S(1)}, s32[35,256]{1,0:T(8,128)S(1)}, u32[]{:S(2)}, u32[]{:S(2)}) collective-permute-start(s32[35,256]{1,0:T(8,128)S(1)} %pad_add_fusion.own_ref), channel_id=1, source_target_pairs={{0,3},{1,0},{2,1},{3,2},{4,7},{5,4},{6,5},{7,6},{8,11},{9,8},{10,9... | collective-permute-start | bytes 107528 | tf_op jit(solution)/shard_map/ppermute | solution.py:482
  12.4 5.6 %collective-permute-start.2 = (s32[35,256]{1,0:T(8,128)S(1)}, s32[35,256]{1,0:T(8,128)S(1)}, u32[]{:S(2)}, u32[]{:S(2)}) collective-permute-start(s32[35,256]{1,0:T(8,128)S(1)} %pad_add_fusion.own_ref), channel_id=1, source_target_pairs={{0,2},{1,3},{2,0},{3,1},{4,6},{5,7},{6,4},{7,5},{8,10},{9,11},{10,... | collective-permute-start | bytes 107528 | tf_op jit(solution)/shard_map/ppermute | solution.py:482
  14.2 0.9 %copy-start = (f32[2,128,128]{2,1,0:T(8,128)S(1)}, f32[2,128,128]{2,1,0:T(8,128)}, u32[]{:S(2)}) copy-start(f32[2,128,128]{2,1,0:T(8,128)} %msg_ref.1) | copy-start | bytes 393220
  15.1 0.9 %copy-start.1 = (f32[2,128,128]{2,1,0:T(8,128)S(1)}, f32[2,128,128]{2,1,0:T(8,128)}, u32[]{:S(2)}) copy-start(f32[2,128,128]{2,1,0:T(8,128)} %upd_ref.1) | copy-start | bytes 393220
  16.0 0.7 %copy-start.4 = (f32[2,8,128]{2,1,0:T(8,128)S(1)}, f32[2,8,128]{2,1,0:T(8,128)}, u32[]{:S(2)}) copy-start(f32[2,8,128]{2,1,0:T(8,128)} %radial_ref.1) | copy-start | bytes 24580
  16.7 0.7 %copy-start.5 = (f32[2,128]{1,0:T(2,128)S(1)}, f32[2,128]{1,0:T(2,128)}, u32[]{:S(2)}) copy-start(f32[2,128]{1,0:T(2,128)} %embed_ref.1) | copy-start | bytes 3076
  19.1 26.4 %copy-start.2 = (f32[8,8,16]{2,1,0:T(8,128)S(1)}, f32[8,8,16]{2,1,0:T(8,128)}, u32[]{:S(2)}) copy-start(f32[8,8,16]{2,1,0:T(8,128)} %constant.4.clone.table_ref) | copy-start | bytes 12292
